TPU v7x, 32 devices: a whole 2x2x4 slice. The times are simulated.
32 devices in a mesh: dp: 4 (over y, core), seq: 8 (over z, x).
Axes of the slice: x: 2, y: 2, z: 4, core: 2. Of those that a mesh axis runs over, the one named last changes fastest.
Arguments:
- video_in: bfloat16 [4, 16, 32, 64, 128], P('dp', 'seq'), may hold values from -110 to 180
- w_spatial: bfloat16 [3, 3, 128, 128], replicated, may hold values from -0.1875 to 0.1875
- w_temporal: bfloat16 [3, 128, 128], replicated, may hold values from -0.3125 to 0.3125
- norm_gain: float32 [128], replicated, may hold values from 0.5 to 1.5
- norm_shift: float32 [128], replicated, may hold values from -3 to 3
- cotangent: bfloat16 [4, 16, 16, 32, 128], P('dp', 'seq'), may hold values from -6 to 6
Outputs:
- encoded: bfloat16 [4, 16, 16, 32, 128], P('dp', 'seq')
- grad_spatial: float32 [3, 3, 128, 128], replicated
- grad_temporal: float32 [3, 128, 128], replicated
- grad_gain: float32 [128], replicated
- grad_shift: float32 [128], replicated
All inputs are finite; a program needn't handle non-finite values.
Results may differ from a plain program's by a relative error of at most 0.0056.
Values may be sent and summed in bfloat16 or wider, within the bound.
No kernel may reach another device: no remote copies, remote signals or barrier semaphores. Data moves between devices by JAX's collectives and lax.ppermute only.
A program may use at most 128 MiB of HBM per device.

v0:
```python
import jax
import jax.numpy as jnp
from jax import lax
from jax.sharding import PartitionSpec as P

GROUPS = 32
FRAMES = 8


CONTRACT_ROWS = (((0,), (0,)), ((), ()))


def row_sources(frames):
    frame_count, height, width, channels = frames.shape
    paired = frames.reshape(frame_count, height // 2, 2, width // 2, 2 * channels)
    even_rows = paired[:, :, 0]
    odd_rows = paired[:, :, 1]
    odd_above = jnp.concatenate([jnp.zeros_like(odd_rows[:, :1]), odd_rows[:, :-1]], axis=1)
    return [odd_above, even_rows, odd_rows]


def column_right(values):
    return jnp.concatenate([jnp.zeros_like(values[:, :, :1]), values[:, :, :-1]], axis=2)


def column_left(values):
    return jnp.concatenate([values[:, :, 1:], jnp.zeros_like(values[:, :, :1])], axis=2)


def spatial_forward(sources, w_spatial, channels):
    total = None
    for tap_row in range(3):
        source = sources[tap_row]
        out_shape = source.shape[:3] + (channels,)
        pair_kernel = jnp.concatenate([w_spatial[tap_row, 1], w_spatial[tap_row, 2]], axis=0)
        main_part = jnp.dot(
            source.reshape(-1, 2 * channels), pair_kernel, preferred_element_type=jnp.float32
        ).reshape(out_shape)
        side_part = jnp.dot(
            source[..., channels:].reshape(-1, channels),
            w_spatial[tap_row, 0],
            preferred_element_type=jnp.float32,
        ).reshape(out_shape)
        term = main_part + column_right(side_part)
        total = term if total is None else total + term
    return total


def spatial_backward(sources, back_spatial, channels):
    back_flat = back_spatial.reshape(-1, channels)
    back_next = column_left(back_spatial).reshape(-1, channels)
    row_list = []
    for tap_row in range(3):
        source = sources[tap_row]
        pair_grad = lax.dot_general(
            source.reshape(-1, 2 * channels),
            back_flat,
            CONTRACT_ROWS,
            preferred_element_type=jnp.float32,
        )
        side_grad = lax.dot_general(
            source[..., channels:].reshape(-1, channels),
            back_next,
            CONTRACT_ROWS,
            preferred_element_type=jnp.float32,
        )
        row_list.append(jnp.stack([side_grad, pair_grad[:channels], pair_grad[channels:]], axis=0))
    return jnp.stack(row_list, axis=0)


def group_total(values):
    return values.reshape(GROUPS, -1).sum(axis=1)


def widen_groups(values, channels):
    return jnp.repeat(values, channels // GROUPS)


def delayed_clip(values, steps):
    shaped = values.reshape((-1, FRAMES) + values.shape[1:])
    zeros = jnp.zeros((shaped.shape[0], steps) + values.shape[1:], values.dtype)
    return jnp.concatenate([zeros, shaped[:, :-steps]], axis=1).reshape(values.shape)


def advanced_clip(values, steps):
    shaped = values.reshape((-1, FRAMES) + values.shape[1:])
    zeros = jnp.zeros((shaped.shape[0], steps) + values.shape[1:], values.dtype)
    return jnp.concatenate([shaped[:, steps:], zeros], axis=1).reshape(values.shape)


def pick_slot(onehot, summed):
    return jnp.sum(onehot[:, None] * summed, axis=0)


def temporal_block(forward_in, backward_in, cot_used, w_temporal, loss_scale):
    channels = w_temporal.shape[1]
    forward_flat = forward_in.reshape(-1, 3 * channels)
    forward_kernel = w_temporal.reshape(3 * channels, channels)
    backward_kernel = jnp.transpose(w_temporal, (0, 2, 1)).reshape(3 * channels, channels)
    encoded_part = jnp.dot(forward_flat, forward_kernel, preferred_element_type=jnp.float32).astype(
        jnp.bfloat16
    )
    grad_temporal = (
        lax.dot_general(
            forward_flat,
            cot_used.reshape(-1, channels),
            CONTRACT_ROWS,
            preferred_element_type=jnp.float32,
        )
        * loss_scale
    )
    back_part = jnp.dot(
        backward_in.reshape(-1, 3 * channels), backward_kernel, preferred_element_type=jnp.float32
    ).astype(jnp.bfloat16)
    return (encoded_part.reshape(cot_used.shape), back_part.reshape(cot_used.shape), grad_temporal)


def on_device(video_in, w_spatial, w_temporal, norm_gain, norm_shift, cotangent):
    frames = video_in[0]
    frame_count = frames.shape[0]
    height = frames.shape[1]
    width = frames.shape[2]
    channels = frames.shape[3]
    out_rows = height // 2
    out_cols = width // 2
    seq_size = lax.axis_size("seq")
    clip_slots = frame_count * seq_size // FRAMES
    first_frame = lax.axis_index("seq") * frame_count
    slot = first_frame // FRAMES
    onehot = (jnp.arange(clip_slots, dtype=jnp.int32) == slot).astype(jnp.float32)
    loss_scale = float(lax.axis_size("dp") * seq_size * frame_count * out_rows * out_cols) ** (-0.5)
    sources = row_sources(frames)
    spatial = spatial_forward(sources, w_spatial, channels)
    local_members = frame_count * out_rows * out_cols * (channels // GROUPS)
    members = local_members * (FRAMES // frame_count)
    local_sums = group_total(spatial.sum(axis=(0, 1, 2)))
    summed = lax.psum(onehot[:, None] * local_sums[None, :], "seq")
    group_mean = pick_slot(onehot, summed) / members
    centered = spatial - widen_groups(group_mean, channels)
    local_square = group_total((centered * centered).sum(axis=(0, 1, 2)))
    squared = lax.psum(onehot[:, None] * local_square[None, :], "seq")
    group_var = pick_slot(onehot, squared) / members
    inv_std = widen_groups(lax.rsqrt(group_var + 1e-05), channels)
    normed = centered * inv_std
    before_act = normed * norm_gain + norm_shift
    activation = jax.nn.silu(before_act).astype(jnp.bfloat16)
    cot_local = cotangent[0]
    act_rows, cot_rows = (
        lax.all_to_all(activation, "seq", split_axis=1, concat_axis=0, tiled=True),
        lax.all_to_all(cot_local, "seq", split_axis=1, concat_axis=0, tiled=True),
    )
    forward_in = jnp.concatenate(
        [act_rows, delayed_clip(act_rows, 1), delayed_clip(act_rows, 2)], axis=-1
    )
    backward_in = jnp.concatenate(
        [cot_rows, advanced_clip(cot_rows, 1), advanced_clip(cot_rows, 2)], axis=-1
    )
    encoded_rows, back_rows, grad_temporal = temporal_block(
        forward_in, backward_in, cot_rows, w_temporal, loss_scale
    )
    back_act, encoded = (
        lax.all_to_all(back_rows, "seq", split_axis=0, concat_axis=1, tiled=True),
        lax.all_to_all(encoded_rows, "seq", split_axis=0, concat_axis=1, tiled=True),
    )
    gate_sig = jax.nn.sigmoid(before_act)
    back_pre = (
        back_act.astype(jnp.float32) * loss_scale * gate_sig * (1.0 + before_act * (1.0 - gate_sig))
    )
    local_shift = back_pre.sum(axis=(0, 1, 2))
    local_gain = (back_pre * normed).sum(axis=(0, 1, 2))
    slot_shift, slot_gain = lax.psum(
        (onehot[:, None] * local_shift[None, :], onehot[:, None] * local_gain[None, :]), "seq"
    )
    clip_shift = pick_slot(onehot, slot_shift)
    clip_gain = pick_slot(onehot, slot_gain)
    group_shift = group_total(norm_gain * clip_shift) / members
    group_gain = group_total(norm_gain * clip_gain) / members
    back_spatial = (
        norm_gain * back_pre
        - widen_groups(group_shift, channels)
        - normed * widen_groups(group_gain, channels)
    ) * inv_std
    back_spatial = back_spatial.astype(jnp.bfloat16)
    grad_spatial = spatial_backward(sources, back_spatial, channels)
    grad_spatial, grad_temporal, grad_gain, grad_shift = lax.psum(
        (grad_spatial, grad_temporal, local_gain, local_shift), ("dp", "seq")
    )
    return (
        encoded[None],
        grad_spatial,
        grad_temporal.reshape(3, channels, channels),
        grad_gain,
        grad_shift,
    )


def solution(mesh):
    placed = (
        P("dp", "seq", None, None, None),
        P(),
        P(),
        P(),
        P(),
        P("dp", "seq", None, None, None),
    )
    return jax.shard_map(
        on_device,
        mesh=mesh,
        in_specs=placed,
        out_specs=(P("dp", "seq", None, None, None), P(), P(), P(), P()),
        check_vma=False,
    )
```

profile of v0, /device:TPU:0, one launch (start us, length us, event | category | flops | bytes accessed | tf_op | source)
XLA Modules:
  0.0 262.3 jit_solution(17052522429406327220)
XLA Ops:
  7.2 1.8 copy.117
  8.9 7.3 %all-to-all-start.2 = ((bf16[2,16,32,128]{3,2,0,1:T(8,128)(2,1)}), bf16[2,16,32,128]{3,2,0,1:T(8,128)(2,1)}, u32[]{:S(2)}, u32[]{:S(2)}) async-start(bf16[2,16,32,128]{3,2,0,1:T(8,128)(2,1)} %bitcast.150), calls=%async_computation.2 | async-start | bytes 524288 | tf_op jit(solution)/shard_map/all_to_all | solution.py:150
  16.2 0.4 reshape_squeeze.11
  16.6 1.1 slice_bitcast_fusion.12
  17.9 0.8 slice.126
  19.6 1.0 copy.81
  20.6 1.2 fusion.12
  21.8 1.2 fusion.7
  23.0 0.4 fusion.45
  23.7 21.8 %psum.56 = f32[2,32]{1,0:T(2,128)S(1)} all-reduce(f32[2,32]{1,0:T(2,128)S(1)} %broadcast_multiply_fusion.3), channel_id=1, replica_groups=mesh['dp'=4,'seq'=8] {'seq'}, use_global_device_ids=true, to_apply=%region_2.3 | all-reduce | flops 64 | bytes 512 | tf_op jit(solution)/shard_map/psum | solution.py:137
  46.3 1.0 copy.90
  47.4 1.1 convolution_convert_fusion
  48.5 3.4 %all-to-all-start.3 = ((bf16[16,2,32,128]{3,2,1,0:T(8,128)(2,1)}), bf16[16,2,32,128]{3,2,1,0:T(8,128)(2,1)S(1)}, u32[]{:S(2)}, u32[]{:S(2)}) async-start(bf16[16,2,32,128]{3,2,1,0:T(8,128)(2,1)} %bitcast.51), calls=%async_computation.3 | async-start | bytes 524288 | tf_op jit(solution)/shard_map/all_to_all | solution.py:162
  52.0 21.8 %psum.57 = f32[2,32]{1,0:T(2,128)S(1)} all-reduce(f32[2,32]{1,0:T(2,128)S(1)} %broadcast_multiply_fusion.2), channel_id=1, replica_groups=mesh['dp'=4,'seq'=8] {'seq'}, use_global_device_ids=true, to_apply=%region_6.7 | all-reduce | flops 64 | bytes 512 | tf_op jit(solution)/shard_map/psum | solution.py:141
  74.6 17.1 %all-reduce.11 = (f32[2,128]{1,0:T(2,128)S(1)}, f32[2,128]{1,0:T(2,128)S(1)}) all-reduce(f32[2,128]{1,0:T(2,128)S(1)} %get-tuple-element.36, f32[2,128]{1,0:T(2,128)S(1)} %get-tuple-element.35), channel_id=1, replica_groups=mesh['dp'=4,'seq'=8] {'seq'}, use_global_device_ids=true, to_apply=%region_9.10 | all-reduce | flops 512 | bytes 4096 | tf_op jit(solution)/shard_map/psum | solution.py:171
  92.9 0.3 convolution_bitcast_fusion.2
  93.5 0.4 copy-done.1
  94.2 0.3 convolution_bitcast_fusion.3
  94.5 0.3 convolution_bitcast_fusion.4
  95.5 0.7 copy.83
  96.2 3.4 %all-to-all-start = ((bf16[2,16,32,128]{3,2,0,1:T(8,128)(2,1)}), bf16[2,16,32,128]{3,2,0,1:T(8,128)(2,1)S(1)}, u32[]{:S(2)}, u32[]{:S(2)}) async-start(bf16[2,16,32,128]{3,2,0,1:T(8,128)(2,1)} %copy.83), calls=%async_computation | async-start | bytes 524288 | tf_op jit(solution)/shard_map/all_to_all | solution.py:149
  99.8 0.9 pad_maximum_fusion.1
  100.6 9.0 %all-to-all-done = bf16[2,16,32,128]{3,2,0,1:T(8,128)(2,1)S(1)} async-done(((bf16[2,16,32,128]{3,2,0,1:T(8,128)(2,1)}), bf16[2,16,32,128]{3,2,0,1:T(8,128)(2,1)S(1)}, u32[]{:S(2)}, u32[]{:S(2)}) %all-to-all-start) | async-done | bytes 262176 | tf_op jit(solution)/shard_map/all_to_all | solution.py:149
  109.8 0.8 copy-done.7
  110.5 1.1 convolution_convert_fusion.1
  111.6 3.6 %all-to-all-start.1 = ((bf16[16,2,32,128]{3,2,1,0:T(8,128)(2,1)}), bf16[16,2,32,128]{3,2,1,0:T(8,128)(2,1)S(1)}, u32[]{:S(2)}, u32[]{:S(2)}) async-start(bf16[16,2,32,128]{3,2,1,0:T(8,128)(2,1)} %bitcast.35), calls=%async_computation.1 | async-start | bytes 524288 | tf_op jit(solution)/shard_map/all_to_all | solution.py:163
  115.3 1.1 convolution_multiply_fusion
  116.4 40.8 %all-reduce.9 = (f32[128]{0:T(128)}, f32[128]{0:T(128)}) all-reduce(f32[128]{0:T(128)S(1)} %get-tuple-element.6, f32[128]{0:T(128)S(1)} %get-tuple-element.5), channel_id=1, replica_groups=mesh['dp'=4,'seq'=8] {'dp','seq'}, use_global_device_ids=true, to_apply=%region_18.19 | all-reduce | flops 256 | bytes 2048 | tf_op jit(solution)/shard_map/psum | solution.py:185
  157.2 0.7 copy.87
  157.9 94.9 %all-reduce.14.cloned.1.call-done = (f32[3,3,128,128]{3,2,1,0:T(8,128)}, f32[3,128,128]{2,1,0:T(8,128)}) async-done(((f32[3,3,128,128]{3,2,1,0:T(8,128)}, f32[3,128,128]{2,1,0:T(8,128)}), (f32[3,3,128,128]{3,2,1,0:T(8,128)}, f32[3,128,128]{2,1,0:T(8,128)})) %all-reduce.14.cloned.1.call-update) | async-done | bytes 786448 | tf_op jit(solution)/shard_map/psum | solution.py:185
  252.8 2.0 copy.120
  254.8 0.7 copy.121
  (80 shorter events, 5.6 us)
Async XLA Ops:
  7.2 9.0 %copy-start.3 = (bf16[1,2,32,64,128]{4,3,2,1,0:T(8,128)(2,1)S(1)}, bf16[1,2,32,64,128]{4,3,2,1,0:T(8,128)(2,1)}, u32[]{:S(2)}) copy-start(bf16[1,2,32,64,128]{4,3,2,1,0:T(8,128)(2,1)} %param.6) | copy-start | bytes 3145732
  8.9 37.3 %all-to-all-start.2 = ((bf16[2,16,32,128]{3,2,0,1:T(8,128)(2,1)}), bf16[2,16,32,128]{3,2,0,1:T(8,128)(2,1)}, u32[]{:S(2)}, u32[]{:S(2)}) async-start(bf16[2,16,32,128]{3,2,0,1:T(8,128)(2,1)} %bitcast.150), calls=%async_computation.2 | async-start | bytes 524288 | tf_op jit(solution)/shard_map/all_to_all | solution.py:150
  16.6 1.1 copy-start.4
  20.6 2.4 copy-start
  22.9 23.2 %copy-start.6 = (bf16[3,128,128]{2,1,0:T(8,128)(2,1)S(1)}, bf16[3,128,128]{2,1,0:T(8,128)(2,1)}, u32[]{:S(2)}) copy-start(bf16[3,128,128]{2,1,0:T(8,128)(2,1)} %param.8) | copy-start | bytes 294916
  48.5 25.6 %all-to-all-start.3 = ((bf16[16,2,32,128]{3,2,1,0:T(8,128)(2,1)}), bf16[16,2,32,128]{3,2,1,0:T(8,128)(2,1)S(1)}, u32[]{:S(2)}, u32[]{:S(2)}) async-start(bf16[16,2,32,128]{3,2,1,0:T(8,128)(2,1)} %bitcast.51), calls=%async_computation.3 | async-start | bytes 524288 | tf_op jit(solution)/shard_map/all_to_all | solution.py:162
  51.9 22.3 %copy-start.8 = (f32[128]{0:T(128)S(1)}, f32[128]{0:T(128)}, u32[]{:S(2)}) copy-start(f32[128]{0:T(128)} %param.9) | copy-start | bytes 1540
  51.9 22.3 %copy-start.9 = (f32[128]{0:T(128)S(1)}, f32[128]{0:T(128)}, u32[]{:S(2)}) copy-start(f32[128]{0:T(128)} %param.10) | copy-start | bytes 1540
  92.9 1.0 copy-start.1
  94.2 1.0 copy-start.2
  96.2 13.4 %all-to-all-start = ((bf16[2,16,32,128]{3,2,0,1:T(8,128)(2,1)}), bf16[2,16,32,128]{3,2,0,1:T(8,128)(2,1)S(1)}, u32[]{:S(2)}, u32[]{:S(2)}) async-start(bf16[2,16,32,128]{3,2,0,1:T(8,128)(2,1)} %copy.83), calls=%async_computation | async-start | bytes 524288 | tf_op jit(solution)/shard_map/all_to_all | solution.py:149
  109.6 0.9 copy-start.7
  111.6 45.6 %all-to-all-start.1 = ((bf16[16,2,32,128]{3,2,1,0:T(8,128)(2,1)}), bf16[16,2,32,128]{3,2,1,0:T(8,128)(2,1)S(1)}, u32[]{:S(2)}, u32[]{:S(2)}) async-start(bf16[16,2,32,128]{3,2,1,0:T(8,128)(2,1)} %bitcast.35), calls=%async_computation.1 | async-start | bytes 524288 | tf_op jit(solution)/shard_map/all_to_all | solution.py:163
  115.2 137.6 %all-reduce.14.cloned.1.call-start = ((), (), s32[]{:S(2)}) async-start(), calls=%async_computation.4 | async-start | bytes 1572864 | tf_op jit(solution)/shard_map/psum | solution.py:185
  252.8 2.0 copy-start.5
Sparse Core Ops, SparseCore 0:
  122.0 130.8 all-reduce.13
where the time goes:
time: 263 us; the launch traced here: 262 us
  waiting for transfers between devices  104 us (40%)
  blocking collectives  102 us (39%)
  starting transfers between devices  17.7 us (7%)
  between operations  14.5 us (6%)
  local copies, waits for them, and re-layouts  13.4 us (5%)
  matrix products  8.66 us (3%)
    psum x1, waiting for transfers between devices, on_device(): lax.psum((grad_spatial, grad_temporal, local_gain, local_shift), ('dp', '...  94.9 us
    psum x1, blocking collectives, on_device(): lax.psum((grad_spatial, grad_temporal, local_gain, local_shift), ('dp', '...  40.8 us
    psum x1, blocking collectives, on_device(): summed = lax.psum(onehot[:, None] * local_sums[None, :], 'seq')  21.8 us
    psum x1, blocking collectives, on_device(): squared = lax.psum(onehot[:, None] * local_square[None, :], 'seq')  21.8 us
    psum x1, blocking collectives, on_device(): lax.psum((onehot[:, None] * local_shift[None, :], onehot[:, None] * local...  17.1 us
    all_to_all x1, waiting for transfers between devices, on_device(): lax.all_to_all(activation, 'seq', split_axis=1, concat_axis=0, tiled=True)  9.02 us
    all_to_all x1, starting transfers between devices, on_device(): lax.all_to_all(cot_local, 'seq', split_axis=1, concat_axis=0, tiled=True)  7.25 us
    unnamed x24, local copies, waits for them, and re-layouts  6.05 us
  transfers between devices with their start and end apart: 5, of which 2 were waited for; matrix products, arithmetic and copies ran while one was open for 4% of the time, Pallas kernels for 0%

commit v1 on v0

v1 whole, which is shorter than its diff:
```python
import functools

import jax
import jax.numpy as jnp
from jax import lax
from jax.experimental import pallas as pl
from jax.experimental.pallas import tpu as pltpu
from jax.sharding import PartitionSpec as P

GROUPS = 32
FRAMES = 8
STEP_ROWS = 8
VMEM_BYTES = 48 * 1024 * 1024

WHOLE = pl.BlockSpec(memory_space=pltpu.VMEM)
SCALAR = pl.BlockSpec(memory_space=pltpu.SMEM)


def dot(left, right):
    return jnp.dot(left, right, preferred_element_type=jnp.float32)


def dot_transposed(left, right):
    return lax.dot_general(
        left, right, (((1,), (1,)), ((), ())), preferred_element_type=jnp.float32
    )


def each(count, body):
    if count <= 8:
        for step in range(count):
            body(step)
    else:
        lax.fori_loop(0, count, lambda step, carry: (body(step), carry)[1], 0)


def call(kernel, out_shape, in_specs, scratch=(), flops=0, moved=0):
    return pl.pallas_call(
        kernel,
        out_shape=out_shape,
        in_specs=in_specs,
        out_specs=jax.tree.map(lambda _: WHOLE, out_shape),
        scratch_shapes=list(scratch),
        compiler_params=pltpu.CompilerParams(vmem_limit_bytes=VMEM_BYTES),
        cost_estimate=pl.CostEstimate(flops=flops, bytes_accessed=moved, transcendentals=0),
    )


def group_spread(values, lanes):
    channels = values.shape[-1]
    shift = 1
    while shift < lanes:
        values = values + pltpu.roll(values, channels - shift, 1)
        shift *= 2
    lane = lax.broadcasted_iota(jnp.int32, values.shape, 1)
    values = jnp.where(lax.rem(lane, lanes) == 0, values, 0.0)
    shift = 1
    while shift < lanes:
        values = values + pltpu.roll(values, shift, 1)
        shift *= 2
    return values


def conv_kernel(video, weights, spatial, stats, odd, even, wide):
    frames, height, width, channels = video.shape
    out_rows, out_cols = height // 2, width // 2
    positions = frames * out_rows * out_cols
    for slot in range(2 * STEP_ROWS):
        wide[slot, 0:8] = jnp.zeros((8, channels), jnp.float32)

    for frame in range(frames):
        odd[frame, 0] = jnp.zeros((out_cols, 3 * channels), jnp.bfloat16)

        def separate(step, frame=frame):
            for row in range(STEP_ROWS):
                for parity in range(2):
                    slot = 2 * row + parity
                    wide[slot, 8 : 8 + width] = video[
                        frame, 2 * (step * STEP_ROWS + row) + parity
                    ].astype(jnp.float32)
            for row in range(STEP_ROWS):
                for parity in range(2):
                    slot = 2 * row + parity
                    for tap in range(3):
                        value = wide[slot, pl.ds(7 + tap, out_cols, stride=2), :].astype(
                            jnp.bfloat16
                        )
                        lanes = slice(tap * channels, (tap + 1) * channels)
                        if parity:
                            odd[frame, step * STEP_ROWS + row + 1, :, lanes] = value
                        else:
                            even[frame, step * STEP_ROWS + row, :, lanes] = value

        each(out_rows // STEP_ROWS, separate)

        def multiply(step, frame=frame):
            flat = (STEP_ROWS * out_cols, 3 * channels)
            first = step * STEP_ROWS
            total = dot(odd[frame, pl.ds(first, STEP_ROWS)].reshape(flat), weights[0])
            total += dot(even[frame, pl.ds(first, STEP_ROWS)].reshape(flat), weights[1])
            total += dot(odd[frame, pl.ds(first + 1, STEP_ROWS)].reshape(flat), weights[2])
            spatial[frame, pl.ds(first, STEP_ROWS)] = total.reshape(STEP_ROWS, out_cols, channels)

        each(out_rows // STEP_ROWS, multiply)

    steps = positions // (STEP_ROWS * out_cols)
    per_frame = out_rows // STEP_ROWS

    def block(step):
        return spatial[step // per_frame, pl.ds((step % per_frame) * STEP_ROWS, STEP_ROWS)]

    def fold(values):
        return values.reshape(-1, 8, channels).sum(axis=0)

    def fold_all(term):
        if steps <= 8:
            total = term(0)
            for step in range(1, steps):
                total += term(step)
            return total
        return lax.fori_loop(
            0, steps, lambda step, total: total + term(step), jnp.zeros((8, channels), jnp.float32)
        )

    mean = fold_all(lambda step: fold(block(step))).sum(axis=0, keepdims=True) / positions
    square = fold_all(lambda step: fold((block(step) - mean) ** 2)).sum(axis=0, keepdims=True)
    row = lax.broadcasted_iota(jnp.int32, (8, channels), 0)
    packed = jnp.where(row == 0, mean, jnp.where(row == 1, square, 0.0))
    for slot in range(stats.shape[0]):
        stats[slot] = packed


def clip_norm(stats, positions, lanes):
    cells = stats.shape[0] * lanes
    means = [stats[member, 0:1] for member in range(stats.shape[0])]
    squares = [stats[member, 1:2] for member in range(stats.shape[0])]
    mean = group_spread(jnp.broadcast_to(sum(means), (8, means[0].shape[-1])), lanes)[0:1] / cells
    square = sum(squares)
    for value in means:
        square = square + positions * (value - mean) ** 2
    square = group_spread(jnp.broadcast_to(square, (8, square.shape[-1])), lanes)[0:1]
    return mean, lax.rsqrt(square / (cells * positions) + 1e-05)


def act_kernel(
    loss_scale, spatial, stats, cot, halo, weights, gain, shift, act, normed, pre, inv, sums
):
    frames, out_rows, out_cols, channels = spatial.shape
    positions = frames * out_rows * out_cols
    mean, inv_std = clip_norm(stats, positions, channels // GROUPS)
    inv[...] = inv_std
    flat = (STEP_ROWS * out_cols, channels)
    shaped = (STEP_ROWS, out_cols, channels)
    sums_shift = jnp.zeros((8, channels), jnp.float32)
    sums_gain = jnp.zeros((8, channels), jnp.float32)

    def fold(values):
        return values.reshape(-1, 8, channels).sum(axis=0)

    for frame in range(frames):

        def cot_block(later, rows):
            if frame + later < frames:
                return cot[frame + later, rows].reshape(flat)
            return halo[frame + later - frames, rows].reshape(flat)

        def one(step, carry):
            rows = pl.ds(step * STEP_ROWS, STEP_ROWS)
            norm = (spatial[frame, rows].reshape(flat) - mean) * inv_std
            before = norm * gain[...] + shift[...]
            sig = jax.nn.sigmoid(before)
            act[frame, rows] = (before * sig).astype(jnp.bfloat16).reshape(shaped)
            back = dot_transposed(cot_block(0, rows), weights[0])
            back += dot_transposed(cot_block(1, rows), weights[1])
            back += dot_transposed(cot_block(2, rows), weights[2])
            back = back.astype(jnp.bfloat16).astype(jnp.float32)
            back_pre = back * loss_scale * sig * (1.0 + before * (1.0 - sig))
            normed[frame, rows] = norm.reshape(shaped)
            pre[frame, rows] = back_pre.reshape(shaped)
            return (carry[0] + fold(back_pre), carry[1] + fold(back_pre * norm))

        steps = out_rows // STEP_ROWS
        if steps <= 4:
            for step in range(steps):
                sums_shift, sums_gain = one(step, (sums_shift, sums_gain))
        else:
            sums_shift, sums_gain = lax.fori_loop(0, steps, one, (sums_shift, sums_gain))

    row = lax.broadcasted_iota(jnp.int32, (8, channels), 0)
    packed = jnp.where(
        row == 0,
        sums_shift.sum(axis=0, keepdims=True),
        jnp.where(row == 1, sums_gain.sum(axis=0, keepdims=True), 0.0),
    )

    def put(slot):
        sums[slot] = packed

    each(sums.shape[0], put)


def grad_kernel(
    per_clip, loss_scale, first, odd, even, normed, pre, inv, sums, gain, act, cot, halo, grads,
    grad_gain, grad_shift,
):
    frames, out_rows, out_cols, channels = normed.shape
    lanes = channels // GROUPS
    members = per_clip * frames * out_rows * out_cols * lanes
    clip = sums[first[0]]
    for member in range(1, per_clip):
        clip = clip + sums[first[0] + member]
    group = group_spread(clip * gain[...], lanes) / members
    group_shift, group_gain = group[0:1], group[1:2]
    total = jnp.sum(sums[...], axis=0)
    grad_shift[...] = total[0:1]
    grad_gain[...] = total[1:2]
    flat = (out_rows * out_cols, channels)
    flat_wide = (out_rows * out_cols, 3 * channels)
    parts = [None, None, None]
    temporal = None
    for frame in range(frames):
        back = (
            gain[...] * pre[frame].reshape(flat)
            - group_shift
            - normed[frame].reshape(flat) * group_gain
        ) * inv[...]
        back = back.astype(jnp.bfloat16).T
        for tap, source in enumerate(
            (odd.at[frame, pl.ds(0, out_rows)], even.at[frame], odd.at[frame, pl.ds(1, out_rows)])
        ):
            term = dot(back, source[...].reshape(flat_wide))
            parts[tap] = term if parts[tap] is None else parts[tap] + term
        act_turned = act[frame].reshape(flat).T
        cots = [
            cot[frame + later] if frame + later < frames else halo[frame + later - frames]
            for later in range(3)
        ]
        terms = [dot(act_turned, value.reshape(flat)) for value in cots]
        temporal = terms if temporal is None else [a + b for a, b in zip(temporal, terms)]
    for tap in range(3):
        for side in range(3):
            block = parts[tap][:, side * channels : (side + 1) * channels].T
            grads[pl.ds((3 * tap + side) * channels, channels)] = block.astype(jnp.bfloat16)
    for tap in range(3):
        grads[pl.ds((9 + tap) * channels, channels)] = (temporal[tap] * loss_scale).astype(
            jnp.bfloat16
        )
    if grads.shape[0] > 12 * channels:
        rest = grads.shape[0] - 12 * channels
        grads[pl.ds(12 * channels, rest)] = jnp.zeros((rest, channels), jnp.bfloat16)


def sum_kernel(arrived, spread):
    count, rows, channels = arrived.shape
    total = jnp.sum(arrived[...].astype(jnp.float32), axis=0).astype(jnp.bfloat16)

    def put(slot):
        spread[slot] = total

    each(count, put)


def final_kernel(arrived, grad_spatial, grad_temporal):
    rows = grad_spatial.shape[0]
    grad_spatial[...] = arrived[pl.ds(0, rows)].astype(jnp.float32)
    grad_temporal[...] = arrived[pl.ds(rows, grad_temporal.shape[0])].astype(jnp.float32)


def encode_kernel(act, halo, weights, encoded):
    frames, out_rows, out_cols, channels = act.shape
    flat = (STEP_ROWS * out_cols, channels)
    for frame in range(frames):

        def one(step, frame=frame):
            rows = pl.ds(step * STEP_ROWS, STEP_ROWS)
            total = None
            for tap in range(3):
                source = (
                    act[frame - tap, rows] if frame >= tap else halo[frames + frame - tap, rows]
                )
                term = dot(source.reshape(flat), weights[tap])
                total = term if total is None else total + term
            encoded[frame, rows] = total.astype(jnp.bfloat16).reshape(
                STEP_ROWS, out_cols, channels
            )

        each(out_rows // STEP_ROWS, one)


def on_device(video_in, w_spatial, w_temporal, norm_gain, norm_shift, cotangent):
    frames, height, width, channels = video_in.shape[1:]
    out_rows, out_cols = height // 2, width // 2
    dp_size, seq_size = lax.axis_size("dp"), lax.axis_size("seq")
    devices = dp_size * seq_size
    per_clip = FRAMES // frames
    assert frames >= 2 and FRAMES % frames == 0
    loss_scale = float(devices * frames * out_rows * out_cols) ** (-0.5)
    shape = (frames, out_rows, out_cols, channels)
    video = video_in[0]
    cot = cotangent[0]
    gain = norm_gain[None]
    shift = norm_shift[None]
    f32, bf16 = jnp.float32, jnp.bfloat16
    struct = jax.ShapeDtypeStruct
    positions = frames * out_rows * out_cols

    back_pairs = [(s, s - 1) for s in range(seq_size) if s % per_clip]
    ahead_pairs = [(s - 1, s) for s in range(seq_size) if s % per_clip]
    clips = [
        list(range(first, first + per_clip)) for first in range(0, seq_size, per_clip)
    ]

    cot_halo = lax.ppermute(cot, "seq", back_pairs)

    spatial, stats, odd, even = call(
        conv_kernel,
        (
            struct(shape, f32),
            struct((per_clip, 8, channels), f32),
            struct((frames, out_rows + 1, out_cols, 3 * channels), bf16),
            struct((frames, out_rows, out_cols, 3 * channels), bf16),
        ),
        [WHOLE] * 2,
        [pltpu.VMEM((2 * STEP_ROWS, 8 + width, channels), f32)],
        flops=2 * positions * 9 * channels * channels,
        moved=video.size * 6,
    )(video, w_spatial.reshape(3, 3 * channels, channels))

    stats = lax.all_to_all(stats, "seq", 0, 0, axis_index_groups=clips, tiled=True)

    act, normed, pre, inv, sums = call(
        functools.partial(act_kernel, loss_scale),
        (
            struct(shape, bf16),
            struct(shape, f32),
            struct(shape, f32),
            struct((1, channels), f32),
            struct((devices, 8, channels), f32),
        ),
        [WHOLE] * 7,
        flops=2 * positions * 3 * channels * channels,
        moved=positions * channels * 20,
    )(spatial, stats, cot, cot_halo, w_temporal, gain, shift)

    act_halo = lax.ppermute(act, "seq", ahead_pairs)
    sums = lax.all_to_all(sums, ("dp", "seq"), 0, 0, tiled=True)

    chunk = -(-12 * channels // (16 * devices)) * 16
    seq_index = lax.axis_index("seq")
    first = lax.axis_index("dp") * seq_size + seq_index // per_clip * per_clip
    grads, grad_gain, grad_shift = call(
        functools.partial(grad_kernel, per_clip, loss_scale),
        (
            struct((devices * chunk, channels), bf16),
            struct((1, channels), f32),
            struct((1, channels), f32),
        ),
        [SCALAR] + [WHOLE] * 10,
        flops=2 * positions * 12 * channels * channels,
        moved=positions * channels * 24,
    )(first.astype(jnp.int32)[None], odd, even, normed, pre, inv, sums, gain, act, cot, cot_halo)

    grads = lax.all_to_all(
        grads.reshape(devices, chunk, channels), ("dp", "seq"), 0, 0, tiled=True
    )
    grads = call(
        sum_kernel, struct((devices, chunk, channels), bf16), [WHOLE], moved=grads.size * 4
    )(grads)
    grads = lax.all_to_all(grads, ("dp", "seq"), 0, 0, tiled=True)
    encoded = call(
        encode_kernel,
        struct(shape, bf16),
        [WHOLE] * 3,
        flops=2 * positions * 3 * channels * channels,
        moved=positions * channels * 6,
    )(act, act_halo, w_temporal)
    grad_spatial, grad_temporal = call(
        final_kernel,
        (struct((9 * channels, channels), f32), struct((3 * channels, channels), f32)),
        [WHOLE],
        moved=12 * channels * channels * 6,
    )(grads.reshape(devices * chunk, channels))
    return (
        encoded[None],
        grad_spatial.reshape(3, 3, channels, channels),
        grad_temporal.reshape(3, channels, channels),
        grad_gain[0],
        grad_shift[0],
    )


def solution(mesh):
    placed = P("dp", "seq", None, None, None)
    return jax.shard_map(
        on_device,
        mesh=mesh,
        in_specs=(placed, P(), P(), P(), P(), placed),
        out_specs=(placed, P(), P(), P(), P()),
        check_vma=False,
    )
```

time: 263 us -> 69.5 us (0.26)
  the two profiles are of different devices: /device:TPU:0 before, /device:TPU:8 now
where the time goes in v1:
time: 69.5 us; the launch traced here: 69.1 us
  blocking collectives  22.1 us (32%)
  waiting for transfers between devices  19.1 us (27%)
  starting transfers between devices  15.3 us (22%)
  Pallas kernels  7.26 us (10%)
  local copies, waits for them, and re-layouts  4.68 us (7%)
  between operations  0.71 us (1%)
    all_to_all x1, blocking collectives, on_device(): lax.all_to_all(grads.reshape(devices, chunk, channels), ('dp', 'seq'), 0,...  15.6 us
    ppermute x1, waiting for transfers between devices, on_device(): act_halo = lax.ppermute(act, 'seq', ahead_pairs)  12.1 us
    all_to_all x1, waiting for transfers between devices, on_device(): sums = lax.all_to_all(sums, ('dp', 'seq'), 0, 0, tiled=True)  6.97 us
    all_to_all x1, blocking collectives, on_device(): lax.all_to_all(stats, 'seq', 0, 0, axis_index_groups=clips, tiled=True)  6.49 us
    all_to_all x1, starting transfers between devices, on_device(): sums = lax.all_to_all(sums, ('dp', 'seq'), 0, 0, tiled=True)  5.12 us
    unnamed x16, local copies, waits for them, and re-layouts  4.68 us
    all_to_all x1, starting transfers between devices, on_device(): grads = lax.all_to_all(grads, ('dp', 'seq'), 0, 0, tiled=True)  3.5 us
    ppermute x1, starting transfers between devices, on_device(): act_halo = lax.ppermute(act, 'seq', ahead_pairs)  3.39 us
  transfers between devices with their start and end apart: 4, of which 2 were waited for; matrix products, arithmetic and copies ran while one was open for 0% of the time, Pallas kernels for 3%

profile of v1, /device:TPU:8, one launch (start us, length us, event | category | flops | bytes accessed | tf_op | source)
XLA Modules:
  0.0 69.1 jit_solution(18248027769266808619)
XLA Ops:
  0.6 3.3 %collective-permute-start = (bf16[2,16,32,128]{3,2,1,0:T(8,128)(2,1)}, bf16[2,16,32,128]{3,2,1,0:T(8,128)(2,1)S(1)}, u32[]{:S(2)}, u32[]{:S(2)}) collective-permute-start(bf16[2,16,32,128]{3,2,1,0:T(8,128)(2,1)} %bitcast.15), channel_id=1, source_target_pairs={{1,0},{2,1},{3,2},{5,4},{6,5},{7,6},{9,8},{10,9},{11,10},{13,12},{... | collective-permute-start | bytes 786440 | tf_op jit(solution)/shard_map/ppermute | solution.py:313
  3.9 0.0 copy-start
  3.9 1.2 %copy-done = bf16[1,2,32,64,128]{4,3,2,1,0:T(8,128)(2,1)S(1)} copy-done((bf16[1,2,32,64,128]{4,3,2,1,0:T(8,128)(2,1)S(1)}, bf16[1,2,32,64,128]{4,3,2,1,0:T(8,128)(2,1)}, u32[]{:S(2)}) %copy-start) | copy-done | bytes 1048600
  5.2 0.0 copy-start.5
  5.2 1.0 %copy-done.5 = bf16[3,3,128,128]{3,2,1,0:T(8,128)(2,1)S(1)} copy-done((bf16[3,3,128,128]{3,2,1,0:T(8,128)(2,1)S(1)}, bf16[3,3,128,128]{3,2,1,0:T(8,128)(2,1)}, u32[]{:S(2)}) %copy-start.5) | copy-done | bytes 294936
  6.1 0.0 copy-start.1
  6.1 0.0 copy-start.4
  6.1 0.9 %shard_map.101 = (f32[2,16,32,128]{3,2,1,0:T(8,128)S(1)}, f32[4,8,128]{2,1,0:T(8,128)S(1)}, bf16[2,17,32,384]{3,2,1,0:T(8,128)(2,1)S(1)}, bf16[2,16,32,384]{3,2,1,0:T(8,128)(2,1)S(1)}) custom-call(bf16[2,32,64,128]{3,2,1,0:T(8,128)(2,1)S(1)} %bitcast.14, bf16[3,384,128]{2,1,0:T(8,128)(2,1)S(1)} %bitcast.19), custom_call_target="tpu_custom_call" | custom-call | flops 301989888 | bytes 3145728 | tf_op jit(solution)/shard_map/pallas_call | solution.py:315
  7.0 6.5 %all_to_all.20.stats = f32[4,8,128]{2,1,0:T(8,128)S(1)} all-to-all(f32[4,8,128]{2,1,0:T(8,128)S(1)} %get-tuple-element.20), channel_id=1, replica_groups={{0,1,2,3},{4,5,6,7},{8,9,10,11},{12,13,14,15},{16,17,18,19},{20,21,22,2..., dimensions={0} | all-to-all | bytes 32768 | tf_op jit(solution)/shard_map/all_to_all | solution.py:329
  13.5 0.0 collective-permute-done.halo
  13.5 0.0 copy-start.6
  13.5 0.0 copy-start.7
  13.5 0.0 copy-done.1
  13.5 0.0 copy-done.4
  13.5 0.6 copy-done.6
  14.2 0.0 copy-done.7
  14.2 1.8 %shard_map.102 = (bf16[2,16,32,128]{3,2,1,0:T(8,128)(2,1)S(1)}, f32[2,16,32,128]{3,2,1,0:T(8,128)S(1)}, f32[2,16,32,128]{3,2,1,0:T(8,128)S(1)}, f32[1,128]{1,0:T(1,128)S(1)}, f32[32,8,128]{2,1,0:T(8,128)}) custom-call(f32[2,16,32,128]{3,2,1,0:T(8,128)S(1)} %get-tuple-element.19.spatial, f32[4,8,128]{2,1,0:T(8,128)S(1)} %all_to_all.20.stats, ...), custom_call_target="tpu_custom_call" | custom-call | flops 100663296 | bytes 2621440 | tf_op jit(solution)/shard_map/pallas_call | solution.py:331
  16.0 0.0 copy-start.2
  16.0 0.8 %copy-done.2 = f32[2,16,32,128]{3,2,1,0:T(8,128)} copy-done((f32[2,16,32,128]{3,2,1,0:T(8,128)}, f32[2,16,32,128]{3,2,1,0:T(8,128)S(1)}, u32[]{:S(2)}) %copy-start.2) | copy-done | bytes 524312
  16.8 5.1 %all-to-all-start.1 = ((f32[32,8,128]{2,1,0:T(8,128)}), f32[32,8,128]{2,1,0:T(8,128)S(1)}, u32[]{:S(2)}, u32[]{:S(2)}) async-start(f32[32,8,128]{2,1,0:T(8,128)} %get-tuple-element.27), calls=%async_computation.1 | async-start | bytes 262144 | tf_op jit(solution)/shard_map/all_to_all | solution.py:346
  21.9 7.0 %all-to-all-done.1.sums = f32[32,8,128]{2,1,0:T(8,128)S(1)} async-done(((f32[32,8,128]{2,1,0:T(8,128)}), f32[32,8,128]{2,1,0:T(8,128)S(1)}, u32[]{:S(2)}, u32[]{:S(2)}) %all-to-all-start.1) | async-done | bytes 131104 | tf_op jit(solution)/shard_map/all_to_all | solution.py:346
  28.9 0.0 copy-start.3
  28.9 1.0 %copy-done.3 = f32[2,16,32,128]{3,2,1,0:T(8,128)S(1)} copy-done((f32[2,16,32,128]{3,2,1,0:T(8,128)S(1)}, f32[2,16,32,128]{3,2,1,0:T(8,128)}, u32[]{:S(2)}) %copy-start.3) | copy-done | bytes 524312
  29.9 1.6 %shard_map.104 = (bf16[1536,128]{1,0:T(8,128)(2,1)S(1)}, f32[1,128]{1,0:T(1,128)}, f32[1,128]{1,0:T(1,128)}) custom-call(s32[1]{0:T(128)} %bitcast.6.first, bf16[2,17,32,384]{3,2,1,0:T(8,128)(2,1)S(1)} %get-tuple-element.22.odd, bf16[2,16,32,384]{3,2,1,0:T(8,128)(2,1)S(1)} %get-tuple-element.23.even, f32[2,16,32,128]{3,2,1,0:T(8,128)S(1)} %get-tuple-element.24.normed, ...), custom_call_target="tpu_custom_call" | custom-call | flops 402653184 | bytes 3145728 | tf_op jit(solution)/shard_map/pallas_call | solution.py:351
  31.5 15.6 %all_to_all.21.arrived = bf16[32,48,128]{2,1,0:T(8,128)(2,1)S(1)} all-to-all(bf16[32,48,128]{2,1,0:T(8,128)(2,1)S(1)} %bitcast.18), channel_id=1, replica_groups=mesh['dp'=4,'seq'=8] {'dp','seq'}, dimensions={0} | all-to-all | bytes 786432 | tf_op jit(solution)/shard_map/all_to_all | solution.py:363
  47.1 1.0 %shard_map.105 = bf16[32,48,128]{2,1,0:T(8,128)(2,1)} custom-call(bf16[32,48,128]{2,1,0:T(8,128)(2,1)S(1)} %all_to_all.21.arrived), custom_call_target="tpu_custom_call" | custom-call | bytes 786432 | tf_op jit(solution)/shard_map/pallas_call | solution.py:366
  48.1 3.5 %all-to-all-start.3 = ((bf16[32,48,128]{2,1,0:T(8,128)(2,1)}), bf16[32,48,128]{2,1,0:T(8,128)(2,1)S(1)}, u32[]{:S(2)}, u32[]{:S(2)}) async-start(bf16[32,48,128]{2,1,0:T(8,128)(2,1)} %shard_map.105), calls=%async_computation.3 | async-start | bytes 786432 | tf_op jit(solution)/shard_map/all_to_all | solution.py:369
  51.6 3.4 %collective-permute-start.1 = (bf16[2,16,32,128]{3,2,1,0:T(8,128)(2,1)S(1)}, bf16[2,16,32,128]{3,2,1,0:T(8,128)(2,1)S(1)}, u32[]{:S(2)}, u32[]{:S(2)}) collective-permute-start(bf16[2,16,32,128]{3,2,1,0:T(8,128)(2,1)S(1)} %get-tuple-element.21.act), channel_id=1, source_target_pairs={{0,1},{1,2},{2,3},{4,5},{5,6},{6,7},{8,9},{9,10},{10,11},{12,13},{... | collective-permute-start | bytes 786440 | tf_op jit(solution)/shard_map/ppermute | solution.py:345
  55.0 12.1 %collective-permute-done.1.halo = bf16[2,16,32,128]{3,2,1,0:T(8,128)(2,1)S(1)} collective-permute-done((bf16[2,16,32,128]{3,2,1,0:T(8,128)(2,1)S(1)}, bf16[2,16,32,128]{3,2,1,0:T(8,128)(2,1)S(1)}, u32[]{:S(2)}, u32[]{:S(2)}) %collective-permute-start.1) | collective-permute-done | bytes 262176 | tf_op jit(solution)/shard_map/ppermute | solution.py:345
  67.1 1.1 %shard_map.103 = bf16[2,16,32,128]{3,2,1,0:T(8,128)(2,1)} custom-call(bf16[2,16,32,128]{3,2,1,0:T(8,128)(2,1)S(1)} %get-tuple-element.21.act, bf16[2,16,32,128]{3,2,1,0:T(8,128)(2,1)S(1)} %collective-permute-done.1.halo, bf16[3,128,128]{2,1,0:T(8,128)(2,1)S(1)} %copy-done.4), custom_call_target="tpu_custom_call" | custom-call | flops 100663296 | bytes 786432 | tf_op jit(solution)/shard_map/pallas_call | solution.py:370
  68.2 0.0 all-to-all-done.3
  68.2 0.9 %shard_map.106 = (f32[1152,128]{1,0:T(8,128)}, f32[384,128]{1,0:T(8,128)}) custom-call(bf16[1536,128]{1,0:T(8,128)(2,1)S(1)} %bitcast.13), custom_call_target="tpu_custom_call" | custom-call | bytes 1179648 | tf_op jit(solution)/shard_map/pallas_call | solution.py:377
Async XLA Ops:
  0.6 12.9 %collective-permute-start = (bf16[2,16,32,128]{3,2,1,0:T(8,128)(2,1)}, bf16[2,16,32,128]{3,2,1,0:T(8,128)(2,1)S(1)}, u32[]{:S(2)}, u32[]{:S(2)}) collective-permute-start(bf16[2,16,32,128]{3,2,1,0:T(8,128)(2,1)} %bitcast.15), channel_id=1, source_target_pairs={{1,0},{2,1},{3,2},{5,4},{6,5},{7,6},{9,8},{10,9},{11,10},{13,12},{... | collective-permute-start | bytes 786440 | tf_op jit(solution)/shard_map/ppermute | solution.py:313
  3.9 1.2 %copy-start = (bf16[1,2,32,64,128]{4,3,2,1,0:T(8,128)(2,1)S(1)}, bf16[1,2,32,64,128]{4,3,2,1,0:T(8,128)(2,1)}, u32[]{:S(2)}) copy-start(bf16[1,2,32,64,128]{4,3,2,1,0:T(8,128)(2,1)} %param.6) | copy-start | bytes 3145732
  5.2 1.0 %copy-start.5 = (bf16[3,3,128,128]{3,2,1,0:T(8,128)(2,1)S(1)}, bf16[3,3,128,128]{3,2,1,0:T(8,128)(2,1)}, u32[]{:S(2)}) copy-start(bf16[3,3,128,128]{3,2,1,0:T(8,128)(2,1)} %param.7) | copy-start | bytes 884740
  6.1 7.4 %copy-start.1 = (bf16[1,2,16,32,128]{4,3,2,1,0:T(8,128)(2,1)S(1)}, bf16[1,2,16,32,128]{4,3,2,1,0:T(8,128)(2,1)}, u32[]{:S(2)}) copy-start(bf16[1,2,16,32,128]{4,3,2,1,0:T(8,128)(2,1)} %param.11) | copy-start | bytes 786436
  6.1 7.4 %copy-start.4 = (bf16[3,128,128]{2,1,0:T(8,128)(2,1)S(1)}, bf16[3,128,128]{2,1,0:T(8,128)(2,1)}, u32[]{:S(2)}) copy-start(bf16[3,128,128]{2,1,0:T(8,128)(2,1)} %weights.3) | copy-start | bytes 294916
  13.5 0.7 copy-start.6
  13.5 0.7 copy-start.7
  16.0 0.8 %copy-start.2 = (f32[2,16,32,128]{3,2,1,0:T(8,128)}, f32[2,16,32,128]{3,2,1,0:T(8,128)S(1)}, u32[]{:S(2)}) copy-start(f32[2,16,32,128]{3,2,1,0:T(8,128)S(1)} %get-tuple-element.25.pre) | copy-start | bytes 1572868
  16.8 12.1 %all-to-all-start.1 = ((f32[32,8,128]{2,1,0:T(8,128)}), f32[32,8,128]{2,1,0:T(8,128)S(1)}, u32[]{:S(2)}, u32[]{:S(2)}) async-start(f32[32,8,128]{2,1,0:T(8,128)} %get-tuple-element.27), calls=%async_computation.1 | async-start | bytes 262144 | tf_op jit(solution)/shard_map/all_to_all | solution.py:346
  28.9 1.0 %copy-start.3 = (f32[2,16,32,128]{3,2,1,0:T(8,128)S(1)}, f32[2,16,32,128]{3,2,1,0:T(8,128)}, u32[]{:S(2)}) copy-start(f32[2,16,32,128]{3,2,1,0:T(8,128)} %copy-done.2) | copy-start | bytes 1572868
  48.1 20.1 %all-to-all-start.3 = ((bf16[32,48,128]{2,1,0:T(8,128)(2,1)}), bf16[32,48,128]{2,1,0:T(8,128)(2,1)S(1)}, u32[]{:S(2)}, u32[]{:S(2)}) async-start(bf16[32,48,128]{2,1,0:T(8,128)(2,1)} %shard_map.105), calls=%async_computation.3 | async-start | bytes 786432 | tf_op jit(solution)/shard_map/all_to_all | solution.py:369
  51.6 15.5 %collective-permute-start.1 = (bf16[2,16,32,128]{3,2,1,0:T(8,128)(2,1)S(1)}, bf16[2,16,32,128]{3,2,1,0:T(8,128)(2,1)S(1)}, u32[]{:S(2)}, u32[]{:S(2)}) collective-permute-start(bf16[2,16,32,128]{3,2,1,0:T(8,128)(2,1)S(1)} %get-tuple-element.21.act), channel_id=1, source_target_pairs={{0,1},{1,2},{2,3},{4,5},{5,6},{6,7},{8,9},{9,10},{10,11},{12,13},{... | collective-permute-start | bytes 786440 | tf_op jit(solution)/shard_map/ppermute | solution.py:345

commit v2 on v1

--- a/solution.py
+++ b/solution.py
@@ -1,4 +1,5 @@
 import functools
+import math
 
 import jax
 import jax.numpy as jnp
@@ -10,10 +11,11 @@
 GROUPS = 32
 FRAMES = 8
 STEP_ROWS = 8
-VMEM_BYTES = 48 * 1024 * 1024
+EXTRA = 16
+SPARE_BYTES = 4 * 1024 * 1024
 
 WHOLE = pl.BlockSpec(memory_space=pltpu.VMEM)
-SCALAR = pl.BlockSpec(memory_space=pltpu.SMEM)
+FAR = pl.BlockSpec(memory_space=pltpu.HBM)
 
 
 def dot(left, right):
@@ -34,16 +36,21 @@
         lax.fori_loop(0, count, lambda step, carry: (body(step), carry)[1], 0)
 
 
-def call(kernel, out_shape, in_specs, scratch=(), flops=0, moved=0):
+def call(kernel, out_shape, operands, specs=None, scratch=(), flops=0):
+    sizes = [value.size * value.dtype.itemsize for value in operands]
+    sizes += [value.size * value.dtype.itemsize for value in jax.tree.leaves(out_shape)]
+    held = sum(math.prod(item.shape) * 4 for item in scratch if hasattr(item, "shape"))
     return pl.pallas_call(
         kernel,
         out_shape=out_shape,
-        in_specs=in_specs,
+        in_specs=specs or [WHOLE] * len(operands),
         out_specs=jax.tree.map(lambda _: WHOLE, out_shape),
         scratch_shapes=list(scratch),
-        compiler_params=pltpu.CompilerParams(vmem_limit_bytes=VMEM_BYTES),
-        cost_estimate=pl.CostEstimate(flops=flops, bytes_accessed=moved, transcendentals=0),
-    )
+        compiler_params=pltpu.CompilerParams(vmem_limit_bytes=sum(sizes) + held + SPARE_BYTES),
+        cost_estimate=pl.CostEstimate(
+            flops=flops, bytes_accessed=sum(sizes), transcendentals=0
+        ),
+    )(*operands)
 
 
 def group_spread(values, lanes):
@@ -61,17 +68,45 @@
     return values
 
 
-def conv_kernel(video, weights, spatial, stats, odd, even, wide):
+def conv_kernel(
+    video_far, weights_far, gain_far, shift_far, spatial, stats, odd, even, params, wide, video,
+    weights, arrived,
+):
     frames, height, width, channels = video.shape
     out_rows, out_cols = height // 2, width // 2
     positions = frames * out_rows * out_cols
+    pieces = arrived.shape[0] - 3
+    half = height * frames // pieces
+    copies = []
+    for piece in range(pieces):
+        rows = pl.ds(piece * half % height, half)
+        at = (piece * half // height, rows)
+        copies.append(pltpu.make_async_copy(video_far.at[at], video.at[at], arrived.at[piece]))
+    small = [
+        pltpu.make_async_copy(source, target, arrived.at[pieces + index])
+        for index, (source, target) in enumerate(
+            ((weights_far, weights), (gain_far, params.at[0:1]), (shift_far, params.at[1:2]))
+        )
+    ]
+    copies[0].start()
+    small[0].start()
+    for copy in copies[1:]:
+        copy.start()
+    for copy in small[1:]:
+        copy.start()
     for slot in range(2 * STEP_ROWS):
         wide[slot, 0:8] = jnp.zeros((8, channels), jnp.float32)
 
     for frame in range(frames):
         odd[frame, 0] = jnp.zeros((out_cols, 3 * channels), jnp.bfloat16)
 
-        def separate(step, frame=frame):
+    for piece in range(pieces):
+        frame = piece * half // height
+        base = piece * half % height // 2 // STEP_ROWS
+        copies[piece].wait()
+
+        def separate(step, frame=frame, base=base):
+            step = base + step
             for row in range(STEP_ROWS):
                 for parity in range(2):
                     slot = 2 * row + parity
@@ -91,9 +126,12 @@
                         else:
                             even[frame, step * STEP_ROWS + row, :, lanes] = value
 
-        each(out_rows // STEP_ROWS, separate)
-
-        def multiply(step, frame=frame):
+        each(half // 2 // STEP_ROWS, separate)
+        if piece == 0:
+            small[0].wait()
+
+        def multiply(step, frame=frame, base=base):
+            step = base + step
             flat = (STEP_ROWS * out_cols, 3 * channels)
             first = step * STEP_ROWS
             total = dot(odd[frame, pl.ds(first, STEP_ROWS)].reshape(flat), weights[0])
@@ -101,7 +139,7 @@
             total += dot(odd[frame, pl.ds(first + 1, STEP_ROWS)].reshape(flat), weights[2])
             spatial[frame, pl.ds(first, STEP_ROWS)] = total.reshape(STEP_ROWS, out_cols, channels)
 
-        each(out_rows // STEP_ROWS, multiply)
+        each(half // 2 // STEP_ROWS, multiply)
 
     steps = positions // (STEP_ROWS * out_cols)
     per_frame = out_rows // STEP_ROWS
@@ -128,6 +166,8 @@
     packed = jnp.where(row == 0, mean, jnp.where(row == 1, square, 0.0))
     for slot in range(stats.shape[0]):
         stats[slot] = packed
+    for copy in small[1:]:
+        copy.wait()
 
 
 def clip_norm(stats, positions, lanes):
@@ -143,12 +183,13 @@
 
 
 def act_kernel(
-    loss_scale, spatial, stats, cot, halo, weights, gain, shift, act, normed, pre, inv, sums
+    loss_scale, spatial, stats, cot, halo, weights, params, act, normed, pre, inv, sums
 ):
     frames, out_rows, out_cols, channels = spatial.shape
     positions = frames * out_rows * out_cols
     mean, inv_std = clip_norm(stats, positions, channels // GROUPS)
     inv[...] = inv_std
+    gain, shift = params[0:1], params[1:2]
     flat = (STEP_ROWS * out_cols, channels)
     shaped = (STEP_ROWS, out_cols, channels)
     sums_shift = jnp.zeros((8, channels), jnp.float32)
@@ -167,7 +208,7 @@
         def one(step, carry):
             rows = pl.ds(step * STEP_ROWS, STEP_ROWS)
             norm = (spatial[frame, rows].reshape(flat) - mean) * inv_std
-            before = norm * gain[...] + shift[...]
+            before = norm * gain + shift
             sig = jax.nn.sigmoid(before)
             act[frame, rows] = (before * sig).astype(jnp.bfloat16).reshape(shaped)
             back = dot_transposed(cot_block(0, rows), weights[0])
@@ -199,28 +240,55 @@
     each(sums.shape[0], put)
 
 
+def split_rows(values, rows):
+    pieces = []
+    for value in values:
+        rest = value
+        for _ in range(3):
+            piece = rest.astype(jnp.bfloat16).astype(jnp.float32)
+            pieces.append(piece)
+            rest = rest - piece
+    row = lax.broadcasted_iota(jnp.int32, (rows, values[0].shape[-1]), 0)
+    packed = jnp.zeros((rows, values[0].shape[-1]), jnp.float32)
+    for index, piece in enumerate(pieces):
+        packed = jnp.where(row == index, piece, packed)
+    return packed.astype(jnp.bfloat16)
+
+
+def join_rows(packed, count):
+    return [
+        packed[3 * i : 3 * i + 1] + packed[3 * i + 1 : 3 * i + 2] + packed[3 * i + 2 : 3 * i + 3]
+        for i in range(count)
+    ]
+
+
+def store_rows(chunks, rows, first, values):
+    done = 0
+    while done < values.shape[0]:
+        chunk, at = divmod(first + done, rows)
+        count = min(rows - at, values.shape[0] - done)
+        chunks[chunk, pl.ds(at, count)] = values[done : done + count]
+        done += count
+
+
 def grad_kernel(
-    per_clip, loss_scale, first, odd, even, normed, pre, inv, sums, gain, act, cot, halo, grads,
-    grad_gain, grad_shift,
+    loss_scale, odd, even, normed, pre, inv, own, sums, params, act, cot, halo, grads
 ):
     frames, out_rows, out_cols, channels = normed.shape
     lanes = channels // GROUPS
-    members = per_clip * frames * out_rows * out_cols * lanes
-    clip = sums[first[0]]
-    for member in range(1, per_clip):
-        clip = clip + sums[first[0] + member]
-    group = group_spread(clip * gain[...], lanes) / members
+    members = sums.shape[0] * frames * out_rows * out_cols * lanes
+    gain = params[0:1]
+    clip = jnp.sum(sums[...], axis=0)
+    group = group_spread(clip * gain, lanes) / members
     group_shift, group_gain = group[0:1], group[1:2]
-    total = jnp.sum(sums[...], axis=0)
-    grad_shift[...] = total[0:1]
-    grad_gain[...] = total[1:2]
     flat = (out_rows * out_cols, channels)
     flat_wide = (out_rows * out_cols, 3 * channels)
+    rows = grads.shape[1] - EXTRA
     parts = [None, None, None]
     temporal = None
     for frame in range(frames):
         back = (
-            gain[...] * pre[frame].reshape(flat)
+            gain * pre[frame].reshape(flat)
             - group_shift
             - normed[frame].reshape(flat) * group_gain
         ) * inv[...]
@@ -240,24 +308,47 @@
     for tap in range(3):
         for side in range(3):
             block = parts[tap][:, side * channels : (side + 1) * channels].T
-            grads[pl.ds((3 * tap + side) * channels, channels)] = block.astype(jnp.bfloat16)
+            store_rows(grads, rows, (3 * tap + side) * channels, block.astype(jnp.bfloat16))
     for tap in range(3):
-        grads[pl.ds((9 + tap) * channels, channels)] = (temporal[tap] * loss_scale).astype(
+        block = (temporal[tap] * loss_scale).astype(jnp.bfloat16)
+        store_rows(grads, rows, (9 + tap) * channels, block)
+    rest = grads.shape[0] * rows - 12 * channels
+    if rest:
+        store_rows(grads, rows, 12 * channels, jnp.zeros((rest, channels), jnp.bfloat16))
+    extra = split_rows([own[0, 1:2], own[0, 0:1]], EXTRA)
+    for chunk in range(grads.shape[0]):
+        grads[chunk, pl.ds(rows, EXTRA)] = extra
+
+
+def total_of(arrived, first, count):
+    total = arrived[0, pl.ds(first, count)].astype(jnp.float32)
+    for chunk in range(1, arrived.shape[0]):
+        total += arrived[chunk, pl.ds(first, count)].astype(jnp.float32)
+    return total
+
+
+def near_sum_kernel(arrived, chunks):
+    rows = arrived.shape[1] - EXTRA
+    count = chunks.shape[1] - EXTRA
+    extra = split_rows(join_rows(total_of(arrived, rows, EXTRA), 2), EXTRA)
+    for chunk in range(chunks.shape[0]):
+        chunks[chunk, pl.ds(0, count)] = total_of(arrived, chunk * count, count).astype(
             jnp.bfloat16
         )
-    if grads.shape[0] > 12 * channels:
-        rest = grads.shape[0] - 12 * channels
-        grads[pl.ds(12 * channels, rest)] = jnp.zeros((rest, channels), jnp.bfloat16)
-
-
-def sum_kernel(arrived, spread):
-    count, rows, channels = arrived.shape
-    total = jnp.sum(arrived[...].astype(jnp.float32), axis=0).astype(jnp.bfloat16)
-
-    def put(slot):
+        chunks[chunk, pl.ds(count, EXTRA)] = extra
+
+
+def far_sum_kernel(arrived, spread, grad_gain, grad_shift):
+    count = spread.shape[1]
+    total = total_of(arrived, 0, count).astype(jnp.bfloat16)
+    for slot in range(spread.shape[0]):
         spread[slot] = total
-
-    each(count, put)
+    grad_gain[...], grad_shift[...] = join_rows(total_of(arrived, count, EXTRA), 2)
+
+
+def spread_kernel(arrived, spread):
+    for slot in range(spread.shape[0]):
+        spread[slot] = arrived[...]
 
 
 def final_kernel(arrived, grad_spatial, grad_temporal):
@@ -296,90 +387,112 @@
     assert frames >= 2 and FRAMES % frames == 0
     loss_scale = float(devices * frames * out_rows * out_cols) ** (-0.5)
     shape = (frames, out_rows, out_cols, channels)
+    positions = frames * out_rows * out_cols
     video = video_in[0]
     cot = cotangent[0]
-    gain = norm_gain[None]
-    shift = norm_shift[None]
     f32, bf16 = jnp.float32, jnp.bfloat16
     struct = jax.ShapeDtypeStruct
-    positions = frames * out_rows * out_cols
 
     back_pairs = [(s, s - 1) for s in range(seq_size) if s % per_clip]
     ahead_pairs = [(s - 1, s) for s in range(seq_size) if s % per_clip]
-    clips = [
-        list(range(first, first + per_clip)) for first in range(0, seq_size, per_clip)
+    clips = [list(range(first, first + per_clip)) for first in range(0, seq_size, per_clip)]
+    pair = 2 if seq_size % 2 == 0 else 1
+    near = [
+        [d * seq_size + s + p for d in range(dp_size) for p in range(pair)]
+        for s in range(0, seq_size, pair)
     ]
+    far = [
+        [d * seq_size + s + p for s in range(0, seq_size, pair)]
+        for d in range(dp_size)
+        for p in range(pair)
+    ]
+    near_count, far_count = dp_size * pair, seq_size // pair
+
+    def exchange(value, axes, groups):
+        return lax.all_to_all(value, axes, 0, 0, axis_index_groups=groups, tiled=True)
 
     cot_halo = lax.ppermute(cot, "seq", back_pairs)
 
-    spatial, stats, odd, even = call(
+    pieces = 2 * frames
+    spatial, stats, odd, even, params = call(
         conv_kernel,
         (
             struct(shape, f32),
             struct((per_clip, 8, channels), f32),
             struct((frames, out_rows + 1, out_cols, 3 * channels), bf16),
             struct((frames, out_rows, out_cols, 3 * channels), bf16),
+            struct((8, channels), f32),
         ),
-        [WHOLE] * 2,
-        [pltpu.VMEM((2 * STEP_ROWS, 8 + width, channels), f32)],
+        (
+            video,
+            w_spatial.reshape(3, 3 * channels, channels),
+            norm_gain[None],
+            norm_shift[None],
+        ),
+        specs=[FAR] * 4,
+        scratch=[
+            pltpu.VMEM((2 * STEP_ROWS, 8 + width, channels), f32),
+            pltpu.VMEM(video.shape, bf16),
+            pltpu.VMEM((3, 3 * channels, channels), bf16),
+            pltpu.SemaphoreType.DMA((pieces + 3,)),
+        ],
         flops=2 * positions * 9 * channels * channels,
-        moved=video.size * 6,
-    )(video, w_spatial.reshape(3, 3 * channels, channels))
-
-    stats = lax.all_to_all(stats, "seq", 0, 0, axis_index_groups=clips, tiled=True)
-
-    act, normed, pre, inv, sums = call(
+    )
+    stats = exchange(stats, "seq", clips)
+    act, normed, pre, inv, own = call(
         functools.partial(act_kernel, loss_scale),
         (
             struct(shape, bf16),
             struct(shape, f32),
             struct(shape, f32),
             struct((1, channels), f32),
-            struct((devices, 8, channels), f32),
+            struct((per_clip, 8, channels), f32),
         ),
-        [WHOLE] * 7,
+        (spatial, stats, cot, cot_halo, w_temporal, params),
         flops=2 * positions * 3 * channels * channels,
-        moved=positions * channels * 20,
-    )(spatial, stats, cot, cot_halo, w_temporal, gain, shift)
-
+    )
     act_halo = lax.ppermute(act, "seq", ahead_pairs)
-    sums = lax.all_to_all(sums, ("dp", "seq"), 0, 0, tiled=True)
-
-    chunk = -(-12 * channels // (16 * devices)) * 16
-    seq_index = lax.axis_index("seq")
-    first = lax.axis_index("dp") * seq_size + seq_index // per_clip * per_clip
+    sums = exchange(own, "seq", clips)
+    far_rows = -(-12 * channels // (16 * devices)) * 16
+    near_rows = far_rows * far_count
+    grads = call(
+        functools.partial(grad_kernel, loss_scale),
+        struct((near_count, near_rows + EXTRA, channels), bf16),
+        (odd, even, normed, pre, inv, own, sums, params, act, cot, cot_halo),
+        flops=2 * positions * 12 * channels * channels,
+    )
+    grads = exchange(grads, ("dp", "seq"), near)
+    grads = call(
+        near_sum_kernel, struct((far_count, far_rows + EXTRA, channels), bf16), (grads,)
+    )
+    grads = exchange(grads, ("dp", "seq"), far)
     grads, grad_gain, grad_shift = call(
-        functools.partial(grad_kernel, per_clip, loss_scale),
+        far_sum_kernel,
         (
-            struct((devices * chunk, channels), bf16),
+            struct((far_count, far_rows, channels), bf16),
             struct((1, channels), f32),
             struct((1, channels), f32),
         ),
-        [SCALAR] + [WHOLE] * 10,
-        flops=2 * positions * 12 * channels * channels,
-        moved=positions * channels * 24,
-    )(first.astype(jnp.int32)[None], odd, even, normed, pre, inv, sums, gain, act, cot, cot_halo)
-
-    grads = lax.all_to_all(
-        grads.reshape(devices, chunk, channels), ("dp", "seq"), 0, 0, tiled=True
-    )
+        (grads,),
+    )
+    grads = exchange(grads, ("dp", "seq"), far)
     grads = call(
-        sum_kernel, struct((devices, chunk, channels), bf16), [WHOLE], moved=grads.size * 4
-    )(grads)
-    grads = lax.all_to_all(grads, ("dp", "seq"), 0, 0, tiled=True)
+        spread_kernel,
+        struct((near_count, near_rows, channels), bf16),
+        (grads.reshape(near_rows, channels),),
+    )
+    grads = exchange(grads, ("dp", "seq"), near)
     encoded = call(
         encode_kernel,
         struct(shape, bf16),
-        [WHOLE] * 3,
+        (act, act_halo, w_temporal),
         flops=2 * positions * 3 * channels * channels,
-        moved=positions * channels * 6,
-    )(act, act_halo, w_temporal)
+    )
     grad_spatial, grad_temporal = call(
         final_kernel,
         (struct((9 * channels, channels), f32), struct((3 * channels, channels), f32)),
-        [WHOLE],
-        moved=12 * channels * channels * 6,
-    )(grads.reshape(devices * chunk, channels))
+        (grads.reshape(near_count * near_rows, channels),),
+    )
     return (
         encoded[None],
         grad_spatial.reshape(3, 3, channels, channels),

time: 69.5 us -> 73.3 us (1.055)
  the two profiles are of different devices: /device:TPU:8 before, /device:TPU:0 now
where the time goes in v2:
time: 73.3 us; the launch traced here: 72.8 us
  blocking collectives  46.3 us (63%)
  starting transfers between devices  8.57 us (12%)
  Pallas kernels  7.33 us (10%)
  waiting for transfers between devices  7.01 us (10%)
  local copies, waits for them, and re-layouts  2.85 us (4%)
    all_to_all x5, blocking collectives, exchange(): lax.all_to_all(value, axes, 0, 0, axis_index_groups=groups, tiled=True)  46.3 us
    pallas_call x8, Pallas kernels, call(): pl.pallas_call(kernel, out_shape=out_shape, in_specs=specs or [WHOLE] * l...  7.33 us
    ppermute x1, waiting for transfers between devices, on_device(): act_halo = lax.ppermute(act, 'seq', ahead_pairs)  7.01 us
    ppermute x1, starting transfers between devices, on_device(): act_halo = lax.ppermute(act, 'seq', ahead_pairs)  3.83 us
    all_to_all x1, starting transfers between devices, exchange(): lax.all_to_all(value, axes, 0, 0, axis_index_groups=groups, tiled=True)  3.45 us
    unnamed x12, local copies, waits for them, and re-layouts  2.85 us
  transfers between devices with their start and end apart: 3, of which 1 were waited for; matrix products, arithmetic and copies ran while one was open for 0% of the time, Pallas kernels for 4%

profile of v2, /device:TPU:0, one launch (start us, length us, event | category | flops | bytes accessed | tf_op | source)
XLA Modules:
  0.0 72.8 jit_solution(14255536900207598338)
XLA Ops:
  0.6 1.3 %collective-permute-start = (bf16[2,16,32,128]{3,2,1,0:T(8,128)(2,1)}, bf16[2,16,32,128]{3,2,1,0:T(8,128)(2,1)S(1)}, u32[]{:S(2)}, u32[]{:S(2)}) collective-permute-start(bf16[2,16,32,128]{3,2,1,0:T(8,128)(2,1)} %bitcast.14), channel_id=1, source_target_pairs={{1,0},{2,1},{3,2},{5,4},{6,5},{7,6},{9,8},{10,9},{11,10},{13,12},{... | collective-permute-start | bytes 786440 | tf_op jit(solution)/shard_map/ppermute | solution.py:414
  1.9 0.0 copy-start.4
  1.9 0.0 copy-start.5
  2.0 0.6 copy-done.4
  2.6 0.0 copy-done.5
  2.6 0.0 copy-start
  2.6 1.2 %copy-done = bf16[1,2,32,64,128]{4,3,2,1,0:T(8,128)(2,1)S(1)} copy-done((bf16[1,2,32,64,128]{4,3,2,1,0:T(8,128)(2,1)S(1)}, bf16[1,2,32,64,128]{4,3,2,1,0:T(8,128)(2,1)}, u32[]{:S(2)}) %copy-start) | copy-done | bytes 1048600
  3.8 0.0 copy-start.3
  3.8 1.0 %copy-done.3 = bf16[3,3,128,128]{3,2,1,0:T(8,128)(2,1)S(1)} copy-done((bf16[3,3,128,128]{3,2,1,0:T(8,128)(2,1)S(1)}, bf16[3,3,128,128]{3,2,1,0:T(8,128)(2,1)}, u32[]{:S(2)}) %copy-start.3) | copy-done | bytes 294936
  4.8 0.0 copy-start.1
  4.8 0.0 copy-start.2
  4.8 1.9 %shard_map.101 = (f32[2,16,32,128]{3,2,1,0:T(8,128)S(1)}, f32[4,8,128]{2,1,0:T(8,128)S(1)}, bf16[2,17,32,384]{3,2,1,0:T(8,128)(2,1)S(1)}, bf16[2,16,32,384]{3,2,1,0:T(8,128)(2,1)S(1)}, f32[8,128]{1,0:T(8,128)S(1)}) custom-call(bf16[2,32,64,128]{3,2,1,0:T(8,128)(2,1)S(1)} %bitcast.13, bf16[3,384,128]{2,1,0:T(8,128)(2,1)S(1)} %bitcast.17, ...), custom_call_target="tpu_custom_call" | custom-call | flops 301989888 | bytes 3511296 | tf_op jit(solution)/shard_map/pallas_call | solution.py:43
  6.7 10.9 %all_to_all.30.stats = f32[4,8,128]{2,1,0:T(8,128)S(1)} all-to-all(f32[4,8,128]{2,1,0:T(8,128)S(1)} %get-tuple-element.21), channel_id=1, replica_groups={{0,1,2,3},{4,5,6,7},{8,9,10,11},{12,13,14,15},{16,17,18,19},{20,21,22,2..., dimensions={0} | all-to-all | bytes 32768 | tf_op jit(solution)/shard_map/all_to_all | solution.py:412
  17.6 0.0 collective-permute-done.halo
  17.6 0.0 copy-done.1
  17.6 0.0 copy-done.2
  17.6 1.0 %shard_map.102 = (bf16[2,16,32,128]{3,2,1,0:T(8,128)(2,1)S(1)}, f32[2,16,32,128]{3,2,1,0:T(8,128)S(1)}, f32[2,16,32,128]{3,2,1,0:T(8,128)S(1)}, f32[1,128]{1,0:T(1,128)S(1)}, f32[4,8,128]{2,1,0:T(8,128)S(1)}) custom-call(f32[2,16,32,128]{3,2,1,0:T(8,128)S(1)} %get-tuple-element.20.spatial, f32[4,8,128]{2,1,0:T(8,128)S(1)} %all_to_all.30.stats, ...), custom_call_target="tpu_custom_call" | custom-call | flops 100663296 | bytes 2494976 | tf_op jit(solution)/shard_map/pallas_call | solution.py:43
  18.6 7.1 %all_to_all.31.sums = f32[4,8,128]{2,1,0:T(8,128)S(1)} all-to-all(f32[4,8,128]{2,1,0:T(8,128)S(1)} %get-tuple-element.29.own), channel_id=1, replica_groups={{0,1,2,3},{4,5,6,7},{8,9,10,11},{12,13,14,15},{16,17,18,19},{20,21,22,2..., dimensions={0} | all-to-all | bytes 32768 | tf_op jit(solution)/shard_map/all_to_all | solution.py:412
  25.6 1.1 %shard_map.104 = bf16[8,208,128]{2,1,0:T(8,128)(2,1)S(1)} custom-call(bf16[2,17,32,384]{3,2,1,0:T(8,128)(2,1)S(1)} %get-tuple-element.24.odd, bf16[2,16,32,384]{3,2,1,0:T(8,128)(2,1)S(1)} %get-tuple-element.25.even, f32[2,16,32,128]{3,2,1,0:T(8,128)S(1)} %get-tuple-element.26.normed, f32[2,16,32,128]{3,2,1,0:T(8,128)S(1)} %get-tuple-element.27.pre, ...), custom_call_target="tpu_custom_call" | custom-call | flops 402653184 | bytes 3920384 | tf_op jit(solution)/shard_map/pallas_call | solution.py:43
  26.8 10.9 %all_to_all.32.arrived = bf16[8,208,128]{2,1,0:T(8,128)(2,1)S(1)} all-to-all(bf16[8,208,128]{2,1,0:T(8,128)(2,1)S(1)} %shard_map.104), channel_id=1, replica_groups={{0,1,8,9,16,17,24,25},{2,3,10,11,18,19,26,27},{4,5,12,13,20,21,28,29},{..., dimensions={0} | all-to-all | bytes 851968 | tf_op jit(solution)/shard_map/all_to_all | solution.py:412
  37.7 0.1 shard_map.105
  37.7 9.4 %all_to_all.33.arrived = bf16[4,64,128]{2,1,0:T(8,128)(2,1)S(1)} all-to-all(bf16[4,64,128]{2,1,0:T(8,128)(2,1)S(1)} %shard_map.105), channel_id=1, replica_groups={{0,2,4,6},{1,3,5,7},{8,10,12,14},{9,11,13,15},{16,18,20,22},{17,19,21,2..., dimensions={0} | all-to-all | bytes 131072 | tf_op jit(solution)/shard_map/all_to_all | solution.py:412
  47.1 0.5 shard_map.106
  47.6 8.0 %all_to_all.34 = bf16[4,48,128]{2,1,0:T(8,128)(2,1)S(1)} all-to-all(bf16[4,48,128]{2,1,0:T(8,128)(2,1)S(1)} %get-tuple-element.30), channel_id=1, replica_groups={{0,2,4,6},{1,3,5,7},{8,10,12,14},{9,11,13,15},{16,18,20,22},{17,19,21,2..., dimensions={0} | all-to-all | bytes 98304 | tf_op jit(solution)/shard_map/all_to_all | solution.py:412
  55.7 0.8 %shard_map.107 = bf16[8,192,128]{2,1,0:T(8,128)(2,1)} custom-call(bf16[192,128]{1,0:T(8,128)(2,1)S(1)} %bitcast.18), custom_call_target="tpu_custom_call" | custom-call | bytes 442368 | tf_op jit(solution)/shard_map/pallas_call | solution.py:43
  56.5 3.5 %all-to-all-start.5 = ((bf16[8,192,128]{2,1,0:T(8,128)(2,1)}), bf16[8,192,128]{2,1,0:T(8,128)(2,1)S(1)}, u32[]{:S(2)}, u32[]{:S(2)}) async-start(bf16[8,192,128]{2,1,0:T(8,128)(2,1)} %shard_map.107), calls=%async_computation.5 | async-start | bytes 786432 | tf_op jit(solution)/shard_map/all_to_all | solution.py:412
  60.0 3.8 %collective-permute-start.1 = (bf16[2,16,32,128]{3,2,1,0:T(8,128)(2,1)S(1)}, bf16[2,16,32,128]{3,2,1,0:T(8,128)(2,1)S(1)}, u32[]{:S(2)}, u32[]{:S(2)}) collective-permute-start(bf16[2,16,32,128]{3,2,1,0:T(8,128)(2,1)S(1)} %get-tuple-element.23.act), channel_id=1, source_target_pairs={{0,1},{1,2},{2,3},{4,5},{5,6},{6,7},{8,9},{9,10},{10,11},{12,13},{... | collective-permute-start | bytes 786440 | tf_op jit(solution)/shard_map/ppermute | solution.py:454
  63.8 7.0 %collective-permute-done.1.halo = bf16[2,16,32,128]{3,2,1,0:T(8,128)(2,1)S(1)} collective-permute-done((bf16[2,16,32,128]{3,2,1,0:T(8,128)(2,1)S(1)}, bf16[2,16,32,128]{3,2,1,0:T(8,128)(2,1)S(1)}, u32[]{:S(2)}, u32[]{:S(2)}) %collective-permute-start.1) | collective-permute-done | bytes 262176 | tf_op jit(solution)/shard_map/ppermute | solution.py:454
  70.8 1.1 %shard_map.103 = bf16[2,16,32,128]{3,2,1,0:T(8,128)(2,1)} custom-call(bf16[2,16,32,128]{3,2,1,0:T(8,128)(2,1)S(1)} %get-tuple-element.23.act, bf16[2,16,32,128]{3,2,1,0:T(8,128)(2,1)S(1)} %collective-permute-done.1.halo, bf16[3,128,128]{2,1,0:T(8,128)(2,1)S(1)} %copy-done.2), custom_call_target="tpu_custom_call" | custom-call | flops 100663296 | bytes 884736 | tf_op jit(solution)/shard_map/pallas_call | solution.py:43
  71.8 0.0 all-to-all-done.5
  71.9 0.9 %shard_map.108 = (f32[1152,128]{1,0:T(8,128)}, f32[384,128]{1,0:T(8,128)}) custom-call(bf16[1536,128]{1,0:T(8,128)(2,1)S(1)} %bitcast.12), custom_call_target="tpu_custom_call" | custom-call | bytes 1179648 | tf_op jit(solution)/shard_map/pallas_call | solution.py:43
Async XLA Ops:
  0.6 17.0 %collective-permute-start = (bf16[2,16,32,128]{3,2,1,0:T(8,128)(2,1)}, bf16[2,16,32,128]{3,2,1,0:T(8,128)(2,1)S(1)}, u32[]{:S(2)}, u32[]{:S(2)}) collective-permute-start(bf16[2,16,32,128]{3,2,1,0:T(8,128)(2,1)} %bitcast.14), channel_id=1, source_target_pairs={{1,0},{2,1},{3,2},{5,4},{6,5},{7,6},{9,8},{10,9},{11,10},{13,12},{... | collective-permute-start | bytes 786440 | tf_op jit(solution)/shard_map/ppermute | solution.py:414
  1.9 0.7 copy-start.4
  1.9 0.7 copy-start.5
  2.6 1.2 %copy-start = (bf16[1,2,32,64,128]{4,3,2,1,0:T(8,128)(2,1)S(1)}, bf16[1,2,32,64,128]{4,3,2,1,0:T(8,128)(2,1)}, u32[]{:S(2)}) copy-start(bf16[1,2,32,64,128]{4,3,2,1,0:T(8,128)(2,1)} %param.6) | copy-start | bytes 3145732
  3.8 1.0 %copy-start.3 = (bf16[3,3,128,128]{3,2,1,0:T(8,128)(2,1)S(1)}, bf16[3,3,128,128]{3,2,1,0:T(8,128)(2,1)}, u32[]{:S(2)}) copy-start(bf16[3,3,128,128]{3,2,1,0:T(8,128)(2,1)} %param.7) | copy-start | bytes 884740
  4.8 12.8 %copy-start.1 = (bf16[1,2,16,32,128]{4,3,2,1,0:T(8,128)(2,1)S(1)}, bf16[1,2,16,32,128]{4,3,2,1,0:T(8,128)(2,1)}, u32[]{:S(2)}) copy-start(bf16[1,2,16,32,128]{4,3,2,1,0:T(8,128)(2,1)} %param.11) | copy-start | bytes 786436
  4.8 12.8 %copy-start.2 = (bf16[3,128,128]{2,1,0:T(8,128)(2,1)S(1)}, bf16[3,128,128]{2,1,0:T(8,128)(2,1)}, u32[]{:S(2)}) copy-start(bf16[3,128,128]{2,1,0:T(8,128)(2,1)} %weights.3) | copy-start | bytes 294916
  56.5 15.4 %all-to-all-start.5 = ((bf16[8,192,128]{2,1,0:T(8,128)(2,1)}), bf16[8,192,128]{2,1,0:T(8,128)(2,1)S(1)}, u32[]{:S(2)}, u32[]{:S(2)}) async-start(bf16[8,192,128]{2,1,0:T(8,128)(2,1)} %shard_map.107), calls=%async_computation.5 | async-start | bytes 786432 | tf_op jit(solution)/shard_map/all_to_all | solution.py:412
  60.0 10.8 %collective-permute-start.1 = (bf16[2,16,32,128]{3,2,1,0:T(8,128)(2,1)S(1)}, bf16[2,16,32,128]{3,2,1,0:T(8,128)(2,1)S(1)}, u32[]{:S(2)}, u32[]{:S(2)}) collective-permute-start(bf16[2,16,32,128]{3,2,1,0:T(8,128)(2,1)S(1)} %get-tuple-element.23.act), channel_id=1, source_target_pairs={{0,1},{1,2},{2,3},{4,5},{5,6},{6,7},{8,9},{9,10},{10,11},{12,13},{... | collective-permute-start | bytes 786440 | tf_op jit(solution)/shard_map/ppermute | solution.py:454

commit v3 on v2

--- a/solution.py
+++ b/solution.py
@@ -11,7 +11,7 @@
 GROUPS = 32
 FRAMES = 8
 STEP_ROWS = 8
-EXTRA = 16
+EXTRA = 8
 SPARE_BYTES = 4 * 1024 * 1024
 
 WHOLE = pl.BlockSpec(memory_space=pltpu.VMEM)
@@ -327,28 +327,12 @@
     return total
 
 
-def near_sum_kernel(arrived, chunks):
-    rows = arrived.shape[1] - EXTRA
-    count = chunks.shape[1] - EXTRA
-    extra = split_rows(join_rows(total_of(arrived, rows, EXTRA), 2), EXTRA)
-    for chunk in range(chunks.shape[0]):
-        chunks[chunk, pl.ds(0, count)] = total_of(arrived, chunk * count, count).astype(
-            jnp.bfloat16
-        )
-        chunks[chunk, pl.ds(count, EXTRA)] = extra
-
-
-def far_sum_kernel(arrived, spread, grad_gain, grad_shift):
+def sum_kernel(arrived, spread, grad_gain, grad_shift):
     count = spread.shape[1]
     total = total_of(arrived, 0, count).astype(jnp.bfloat16)
     for slot in range(spread.shape[0]):
         spread[slot] = total
     grad_gain[...], grad_shift[...] = join_rows(total_of(arrived, count, EXTRA), 2)
-
-
-def spread_kernel(arrived, spread):
-    for slot in range(spread.shape[0]):
-        spread[slot] = arrived[...]
 
 
 def final_kernel(arrived, grad_spatial, grad_temporal):
@@ -396,20 +380,12 @@
     back_pairs = [(s, s - 1) for s in range(seq_size) if s % per_clip]
     ahead_pairs = [(s - 1, s) for s in range(seq_size) if s % per_clip]
     clips = [list(range(first, first + per_clip)) for first in range(0, seq_size, per_clip)]
-    pair = 2 if seq_size % 2 == 0 else 1
-    near = [
-        [d * seq_size + s + p for d in range(dp_size) for p in range(pair)]
-        for s in range(0, seq_size, pair)
-    ]
-    far = [
-        [d * seq_size + s + p for s in range(0, seq_size, pair)]
-        for d in range(dp_size)
-        for p in range(pair)
-    ]
-    near_count, far_count = dp_size * pair, seq_size // pair
-
-    def exchange(value, axes, groups):
+
+    def exchange(value, axes, groups=None):
         return lax.all_to_all(value, axes, 0, 0, axis_index_groups=groups, tiled=True)
+
+    def far(value):
+        return pltpu.with_memory_space_constraint(value, pltpu.HBM)
 
     cot_halo = lax.ppermute(cot, "seq", back_pairs)
 
@@ -424,10 +400,10 @@
             struct((8, channels), f32),
         ),
         (
-            video,
-            w_spatial.reshape(3, 3 * channels, channels),
-            norm_gain[None],
-            norm_shift[None],
+            far(video),
+            far(w_spatial.reshape(3, 3 * channels, channels)),
+            far(norm_gain[None]),
+            far(norm_shift[None]),
         ),
         specs=[FAR] * 4,
         scratch=[
@@ -453,45 +429,35 @@
     )
     act_halo = lax.ppermute(act, "seq", ahead_pairs)
     sums = exchange(own, "seq", clips)
-    far_rows = -(-12 * channels // (16 * devices)) * 16
-    near_rows = far_rows * far_count
-    grads = call(
-        functools.partial(grad_kernel, loss_scale),
-        struct((near_count, near_rows + EXTRA, channels), bf16),
-        (odd, even, normed, pre, inv, own, sums, params, act, cot, cot_halo),
-        flops=2 * positions * 12 * channels * channels,
-    )
-    grads = exchange(grads, ("dp", "seq"), near)
-    grads = call(
-        near_sum_kernel, struct((far_count, far_rows + EXTRA, channels), bf16), (grads,)
-    )
-    grads = exchange(grads, ("dp", "seq"), far)
-    grads, grad_gain, grad_shift = call(
-        far_sum_kernel,
-        (
-            struct((far_count, far_rows, channels), bf16),
-            struct((1, channels), f32),
-            struct((1, channels), f32),
-        ),
-        (grads,),
-    )
-    grads = exchange(grads, ("dp", "seq"), far)
-    grads = call(
-        spread_kernel,
-        struct((near_count, near_rows, channels), bf16),
-        (grads.reshape(near_rows, channels),),
-    )
-    grads = exchange(grads, ("dp", "seq"), near)
     encoded = call(
         encode_kernel,
         struct(shape, bf16),
         (act, act_halo, w_temporal),
         flops=2 * positions * 3 * channels * channels,
     )
+    encoded, sums = lax.optimization_barrier((encoded, sums))
+    rows = -(-12 * channels // (16 * devices)) * 16
+    grads = call(
+        functools.partial(grad_kernel, loss_scale),
+        struct((devices, rows + EXTRA, channels), bf16),
+        (odd, even, normed, pre, inv, own, sums, params, act, cot, cot_halo),
+        flops=2 * positions * 12 * channels * channels,
+    )
+    grads = exchange(grads, ("dp", "seq"))
+    grads, grad_gain, grad_shift = call(
+        sum_kernel,
+        (
+            struct((devices, rows, channels), bf16),
+            struct((1, channels), f32),
+            struct((1, channels), f32),
+        ),
+        (grads,),
+    )
+    grads = exchange(grads, ("dp", "seq"))
     grad_spatial, grad_temporal = call(
         final_kernel,
         (struct((9 * channels, channels), f32), struct((3 * channels, channels), f32)),
-        (grads.reshape(near_count * near_rows, channels),),
+        (grads.reshape(devices * rows, channels),),
     )
     return (
         encoded[None],

time: 73.3 us -> 69.1 us (0.943)
  waiting for transfers between devices: 7.01 us -> 2.76 us
  Pallas kernels: 7.33 us -> 9.02 us
  blocking collectives: 46.3 us -> 45.2 us
    ppermute x1, waiting for transfers between devices: 7.01 us -> 0.01 us  [on_device(): act_halo = lax.ppermute(act, 'seq', ahead_pairs)]
    all_to_all x1, waiting for transfers between devices: 0.01 us -> 2.76 us  [exchange(): lax.all_to_all(value, axes, 0, 0, axis_index_groups=groups, tiled=True)]
    pallas_call x8 -> x6, Pallas kernels: 7.33 us -> 9.02 us  [call(): pl.pallas_call(kernel, out_shape=out_shape, in_specs=specs or [WHOLE] * l...]
    all_to_all x5 -> x3, blocking collectives: 46.3 us -> 45.2 us  [exchange(): lax.all_to_all(value, axes, 0, 0, axis_index_groups=groups, tiled=True)]
    unnamed x12 -> x16, local copies, waits for them, and re-layouts: 2.85 us -> 2.53 us
  transfers between devices with their start and end apart: 3 -> 3, of which waited for: 1 -> 1; matrix products, arithmetic and copies ran while one was open for 0% -> 0% of each run, Pallas kernels for 4% -> 7%
where the time goes in v3:
time: 69.1 us; the launch traced here: 68.6 us
  blocking collectives  45.2 us (65%)
  Pallas kernels  9.02 us (13%)
  starting transfers between devices  8.36 us (12%)
  waiting for transfers between devices  2.76 us (4%)
  local copies, waits for them, and re-layouts  2.53 us (4%)
  between operations  0.72 us (1%)
    all_to_all x3, blocking collectives, exchange(): lax.all_to_all(value, axes, 0, 0, axis_index_groups=groups, tiled=True)  45.2 us
    pallas_call x6, Pallas kernels, call(): pl.pallas_call(kernel, out_shape=out_shape, in_specs=specs or [WHOLE] * l...  9.02 us
    all_to_all x1, starting transfers between devices, exchange(): lax.all_to_all(value, axes, 0, 0, axis_index_groups=groups, tiled=True)  3.86 us
    ppermute x1, starting transfers between devices, on_device(): act_halo = lax.ppermute(act, 'seq', ahead_pairs)  3.21 us
    all_to_all x1, waiting for transfers between devices, exchange(): lax.all_to_all(value, axes, 0, 0, axis_index_groups=groups, tiled=True)  2.76 us
    unnamed x16, local copies, waits for them, and re-layouts  2.53 us
  transfers between devices with their start and end apart: 3, of which 1 were waited for; matrix products, arithmetic and copies ran while one was open for 0% of the time, Pallas kernels for 7%

profile of v3, /device:TPU:0, one launch (start us, length us, event | category | flops | bytes accessed | tf_op | source)
XLA Modules:
  0.0 68.6 jit_solution(540762950322151827)
XLA Ops:
  0.6 1.3 %collective-permute-start = (bf16[2,16,32,128]{3,2,1,0:T(8,128)(2,1)}, bf16[2,16,32,128]{3,2,1,0:T(8,128)(2,1)S(1)}, u32[]{:S(2)}, u32[]{:S(2)}) collective-permute-start(bf16[2,16,32,128]{3,2,1,0:T(8,128)(2,1)} %bitcast.12), channel_id=1, source_target_pairs={{1,0},{2,1},{3,2},{5,4},{6,5},{7,6},{9,8},{10,9},{11,10},{13,12},{... | collective-permute-start | bytes 786440 | tf_op jit(solution)/shard_map/ppermute | solution.py:390
  1.9 0.0 copy-start
  1.9 0.0 copy-start.1
  2.0 2.7 %shard_map.101 = (f32[2,16,32,128]{3,2,1,0:T(8,128)S(1)}, f32[4,8,128]{2,1,0:T(8,128)S(1)}, bf16[2,17,32,384]{3,2,1,0:T(8,128)(2,1)S(1)}, bf16[2,16,32,384]{3,2,1,0:T(8,128)(2,1)S(1)}, f32[8,128]{1,0:T(8,128)S(1)}) custom-call(bf16[2,32,64,128]{3,2,1,0:T(8,128)(2,1)} %bitcast.15, bf16[3,384,128]{2,1,0:T(8,128)(2,1)} %bitcast.16, f32[1,128]{1,0:T(1,128)} %bitcast.18, ...), custom_call_target="tpu_custom_call" | custom-call | flops 301989888 | bytes 3511296 | tf_op jit(solution)/shard_map/pallas_call | solution.py:43
  4.7 0.0 copy-start.4
  4.7 10.9 %all_to_all.20.stats = f32[4,8,128]{2,1,0:T(8,128)S(1)} all-to-all(f32[4,8,128]{2,1,0:T(8,128)S(1)} %get-tuple-element.23), channel_id=1, replica_groups={{0,1,2,3},{4,5,6,7},{8,9,10,11},{12,13,14,15},{16,17,18,19},{20,21,22,2..., dimensions={0} | all-to-all | bytes 32768 | tf_op jit(solution)/shard_map/all_to_all | solution.py:385
  15.6 0.0 collective-permute-done.halo
  15.6 0.0 copy-done.4
  15.6 0.0 copy-done
  15.6 0.0 copy-done.1
  15.6 1.0 %shard_map.102 = (bf16[2,16,32,128]{3,2,1,0:T(8,128)(2,1)S(1)}, f32[2,16,32,128]{3,2,1,0:T(8,128)S(1)}, f32[2,16,32,128]{3,2,1,0:T(8,128)S(1)}, f32[1,128]{1,0:T(1,128)S(1)}, f32[4,8,128]{2,1,0:T(8,128)S(1)}) custom-call(f32[2,16,32,128]{3,2,1,0:T(8,128)S(1)} %get-tuple-element.22.spatial, f32[4,8,128]{2,1,0:T(8,128)S(1)} %all_to_all.20.stats, ...), custom_call_target="tpu_custom_call" | custom-call | flops 100663296 | bytes 2494976 | tf_op jit(solution)/shard_map/pallas_call | solution.py:43
  16.6 0.0 copy-start.2
  16.6 0.6 copy-done.2
  17.2 0.0 copy-start.6
  17.2 0.5 copy-done.6
  17.7 3.2 %collective-permute-start.1 = (bf16[2,16,32,128]{3,2,1,0:T(8,128)(2,1)S(1)}, bf16[2,16,32,128]{3,2,1,0:T(8,128)(2,1)}, u32[]{:S(2)}, u32[]{:S(2)}) collective-permute-start(bf16[2,16,32,128]{3,2,1,0:T(8,128)(2,1)S(1)} %get-tuple-element.25.act), channel_id=1, source_target_pairs={{0,1},{1,2},{2,3},{4,5},{5,6},{6,7},{8,9},{9,10},{10,11},{12,13},{... | collective-permute-start | bytes 786440 | tf_op jit(solution)/shard_map/ppermute | solution.py:430
  20.9 3.9 %all-to-all-start.1 = ((f32[4,8,128]{2,1,0:T(8,128)}), f32[4,8,128]{2,1,0:T(8,128)}, u32[]{:S(2)}, u32[]{:S(2)}) async-start(f32[4,8,128]{2,1,0:T(8,128)} %copy-done.2), calls=%async_computation.1 | async-start | bytes 32768 | tf_op jit(solution)/shard_map/all_to_all | solution.py:385
  24.8 0.0 collective-permute-done.1.halo
  24.8 2.0 %shard_map.103 = bf16[2,16,32,128]{3,2,1,0:T(8,128)(2,1)} custom-call(bf16[2,16,32,128]{3,2,1,0:T(8,128)(2,1)S(1)} %get-tuple-element.25.act, bf16[2,16,32,128]{3,2,1,0:T(8,128)(2,1)} %collective-permute-done.1.halo, bf16[3,128,128]{2,1,0:T(8,128)(2,1)S(1)} %copy-done.1), custom_call_target="tpu_custom_call" | custom-call | flops 100663296 | bytes 884736 | tf_op jit(solution)/shard_map/pallas_call | solution.py:43
  26.8 2.8 %all-to-all-done.1.sums = f32[4,8,128]{2,1,0:T(8,128)} async-done(((f32[4,8,128]{2,1,0:T(8,128)}), f32[4,8,128]{2,1,0:T(8,128)}, u32[]{:S(2)}, u32[]{:S(2)}) %all-to-all-start.1) | async-done | bytes 16416 | tf_op jit(solution)/shard_map/all_to_all | solution.py:385
  29.6 0.0 copy-start.5
  29.6 0.0 copy-start.7
  29.6 0.7 copy-done.5
  30.3 0.0 copy-done.7
  30.3 0.0 copy-start.3
  30.3 0.7 %copy-done.3 = f32[4,8,128]{2,1,0:T(8,128)S(1)} copy-done((f32[4,8,128]{2,1,0:T(8,128)S(1)}, f32[4,8,128]{2,1,0:T(8,128)}, u32[]{:S(2)}) %copy-start.3) | copy-done | bytes 16408
  31.0 1.8 %shard_map.104 = bf16[32,56,128]{2,1,0:T(8,128)(2,1)S(1)} custom-call(bf16[2,17,32,384]{3,2,1,0:T(8,128)(2,1)S(1)} %get-tuple-element.28.odd, bf16[2,16,32,384]{3,2,1,0:T(8,128)(2,1)S(1)} %get-tuple-element.29.even, f32[2,16,32,128]{3,2,1,0:T(8,128)S(1)} %get-tuple-element.30.normed, f32[2,16,32,128]{3,2,1,0:T(8,128)S(1)} %get-tuple-element.31.pre, ...), custom_call_target="tpu_custom_call" | custom-call | flops 402653184 | bytes 3953152 | tf_op jit(solution)/shard_map/pallas_call | solution.py:43
  32.8 18.7 %all_to_all.21.arrived = bf16[32,56,128]{2,1,0:T(8,128)(2,1)S(1)} all-to-all(bf16[32,56,128]{2,1,0:T(8,128)(2,1)S(1)} %shard_map.104), channel_id=1, replica_groups=mesh['dp'=4,'seq'=8] {'dp','seq'}, dimensions={0} | all-to-all | bytes 917504 | tf_op jit(solution)/shard_map/all_to_all | solution.py:385
  51.5 0.6 shard_map.105
  52.1 15.6 %all_to_all.22 = bf16[32,48,128]{2,1,0:T(8,128)(2,1)S(1)} all-to-all(bf16[32,48,128]{2,1,0:T(8,128)(2,1)S(1)} %get-tuple-element.34), channel_id=1, replica_groups=mesh['dp'=4,'seq'=8] {'dp','seq'}, dimensions={0} | all-to-all | bytes 786432 | tf_op jit(solution)/shard_map/all_to_all | solution.py:385
  67.7 0.9 %shard_map.106 = (f32[1152,128]{1,0:T(8,128)}, f32[384,128]{1,0:T(8,128)}) custom-call(bf16[1536,128]{1,0:T(8,128)(2,1)S(1)} %bitcast.11), custom_call_target="tpu_custom_call" | custom-call | bytes 1179648 | tf_op jit(solution)/shard_map/pallas_call | solution.py:43
Async XLA Ops:
  0.6 15.0 %collective-permute-start = (bf16[2,16,32,128]{3,2,1,0:T(8,128)(2,1)}, bf16[2,16,32,128]{3,2,1,0:T(8,128)(2,1)S(1)}, u32[]{:S(2)}, u32[]{:S(2)}) collective-permute-start(bf16[2,16,32,128]{3,2,1,0:T(8,128)(2,1)} %bitcast.12), channel_id=1, source_target_pairs={{1,0},{2,1},{3,2},{5,4},{6,5},{7,6},{9,8},{10,9},{11,10},{13,12},{... | collective-permute-start | bytes 786440 | tf_op jit(solution)/shard_map/ppermute | solution.py:390
  1.9 13.7 %copy-start = (bf16[1,2,16,32,128]{4,3,2,1,0:T(8,128)(2,1)S(1)}, bf16[1,2,16,32,128]{4,3,2,1,0:T(8,128)(2,1)}, u32[]{:S(2)}) copy-start(bf16[1,2,16,32,128]{4,3,2,1,0:T(8,128)(2,1)} %param.11) | copy-start | bytes 786436
  1.9 13.7 %copy-start.1 = (bf16[3,128,128]{2,1,0:T(8,128)(2,1)S(1)}, bf16[3,128,128]{2,1,0:T(8,128)(2,1)}, u32[]{:S(2)}) copy-start(bf16[3,128,128]{2,1,0:T(8,128)(2,1)} %weights.3) | copy-start | bytes 294916
  4.7 10.9 %copy-start.4 = (f32[8,128]{1,0:T(8,128)}, f32[8,128]{1,0:T(8,128)S(1)}, u32[]{:S(2)}) copy-start(f32[8,128]{1,0:T(8,128)S(1)} %get-tuple-element.24.params) | copy-start | bytes 12292
  16.6 0.6 copy-start.2
  17.2 0.5 copy-start.6
  17.7 7.1 %collective-permute-start.1 = (bf16[2,16,32,128]{3,2,1,0:T(8,128)(2,1)S(1)}, bf16[2,16,32,128]{3,2,1,0:T(8,128)(2,1)}, u32[]{:S(2)}, u32[]{:S(2)}) collective-permute-start(bf16[2,16,32,128]{3,2,1,0:T(8,128)(2,1)S(1)} %get-tuple-element.25.act), channel_id=1, source_target_pairs={{0,1},{1,2},{2,3},{4,5},{5,6},{6,7},{8,9},{9,10},{10,11},{12,13},{... | collective-permute-start | bytes 786440 | tf_op jit(solution)/shard_map/ppermute | solution.py:430
  20.9 8.6 %all-to-all-start.1 = ((f32[4,8,128]{2,1,0:T(8,128)}), f32[4,8,128]{2,1,0:T(8,128)}, u32[]{:S(2)}, u32[]{:S(2)}) async-start(f32[4,8,128]{2,1,0:T(8,128)} %copy-done.2), calls=%async_computation.1 | async-start | bytes 32768 | tf_op jit(solution)/shard_map/all_to_all | solution.py:385
  29.6 0.7 %copy-start.5 = (f32[8,128]{1,0:T(8,128)S(1)}, f32[8,128]{1,0:T(8,128)}, u32[]{:S(2)}) copy-start(f32[8,128]{1,0:T(8,128)} %copy-done.4) | copy-start | bytes 12292
  29.6 0.7 %copy-start.7 = (f32[1,128]{1,0:T(1,128)S(1)}, f32[1,128]{1,0:T(1,128)}, u32[]{:S(2)}) copy-start(f32[1,128]{1,0:T(1,128)} %copy-done.6) | copy-start | bytes 1540
  30.3 0.7 %copy-start.3 = (f32[4,8,128]{2,1,0:T(8,128)S(1)}, f32[4,8,128]{2,1,0:T(8,128)}, u32[]{:S(2)}) copy-start(f32[4,8,128]{2,1,0:T(8,128)} %copy-done.2) | copy-start | bytes 49156

commit v4 on v3

--- a/solution.py
+++ b/solution.py
@@ -183,12 +183,11 @@
 
 
 def act_kernel(
-    loss_scale, spatial, stats, cot, halo, weights, params, act, normed, pre, inv, sums
+    loss_scale, spatial, stats, cot, halo, weights, params, act, normed, pre, temporal, sums
 ):
     frames, out_rows, out_cols, channels = spatial.shape
     positions = frames * out_rows * out_cols
     mean, inv_std = clip_norm(stats, positions, channels // GROUPS)
-    inv[...] = inv_std
     gain, shift = params[0:1], params[1:2]
     flat = (STEP_ROWS * out_cols, channels)
     shaped = (STEP_ROWS, out_cols, channels)
@@ -217,7 +216,7 @@
             back = back.astype(jnp.bfloat16).astype(jnp.float32)
             back_pre = back * loss_scale * sig * (1.0 + before * (1.0 - sig))
             normed[frame, rows] = norm.reshape(shaped)
-            pre[frame, rows] = back_pre.reshape(shaped)
+            pre[frame, rows] = (back_pre * (gain * inv_std)).reshape(shaped)
             return (carry[0] + fold(back_pre), carry[1] + fold(back_pre * norm))
 
         steps = out_rows // STEP_ROWS
@@ -227,17 +226,29 @@
         else:
             sums_shift, sums_gain = lax.fori_loop(0, steps, one, (sums_shift, sums_gain))
 
+    sums_shift = sums_shift.sum(axis=0, keepdims=True)
+    sums_gain = sums_gain.sum(axis=0, keepdims=True)
     row = lax.broadcasted_iota(jnp.int32, (8, channels), 0)
-    packed = jnp.where(
-        row == 0,
-        sums_shift.sum(axis=0, keepdims=True),
-        jnp.where(row == 1, sums_gain.sum(axis=0, keepdims=True), 0.0),
-    )
-
-    def put(slot):
+    packed = jnp.zeros((8, channels), jnp.float32)
+    for index, value in enumerate(
+        (sums_shift, sums_gain, gain * sums_shift, gain * sums_gain, inv_std)
+    ):
+        packed = jnp.where(row == index, value, packed)
+    for slot in range(sums.shape[0]):
         sums[slot] = packed
 
-    each(sums.shape[0], put)
+    all_rows = (out_rows * out_cols, channels)
+    parts = [None, None, None]
+    for frame in range(frames):
+        turned = act[frame].reshape(all_rows).T
+        for later in range(3):
+            value = cot[frame + later] if frame + later < frames else halo[frame + later - frames]
+            term = dot(turned, value.reshape(all_rows))
+            parts[later] = term if parts[later] is None else parts[later] + term
+    for later in range(3):
+        temporal[pl.ds(later * channels, channels)] = (parts[later] * loss_scale).astype(
+            jnp.bfloat16
+        )
 
 
 def split_rows(values, rows):
@@ -272,52 +283,44 @@
 
 
 def grad_kernel(
-    loss_scale, odd, even, normed, pre, inv, own, sums, params, act, cot, halo, grads
+    odd, even, normed, pre, sums, temporal, act, act_halo, weights, grads, encoded
 ):
     frames, out_rows, out_cols, channels = normed.shape
     lanes = channels // GROUPS
     members = sums.shape[0] * frames * out_rows * out_cols * lanes
-    gain = params[0:1]
     clip = jnp.sum(sums[...], axis=0)
-    group = group_spread(clip * gain, lanes) / members
-    group_shift, group_gain = group[0:1], group[1:2]
+    inv_std = sums[0, 4:5]
+    group = group_spread(clip, lanes) * inv_std / members
+    group_shift, group_gain = group[2:3], group[3:4]
     flat = (out_rows * out_cols, channels)
     flat_wide = (out_rows * out_cols, 3 * channels)
     rows = grads.shape[1] - EXTRA
     parts = [None, None, None]
-    temporal = None
     for frame in range(frames):
         back = (
-            gain * pre[frame].reshape(flat)
-            - group_shift
-            - normed[frame].reshape(flat) * group_gain
-        ) * inv[...]
+            pre[frame].reshape(flat) - group_shift - normed[frame].reshape(flat) * group_gain
+        )
         back = back.astype(jnp.bfloat16).T
         for tap, source in enumerate(
             (odd.at[frame, pl.ds(0, out_rows)], even.at[frame], odd.at[frame, pl.ds(1, out_rows)])
         ):
             term = dot(back, source[...].reshape(flat_wide))
             parts[tap] = term if parts[tap] is None else parts[tap] + term
-        act_turned = act[frame].reshape(flat).T
-        cots = [
-            cot[frame + later] if frame + later < frames else halo[frame + later - frames]
-            for later in range(3)
-        ]
-        terms = [dot(act_turned, value.reshape(flat)) for value in cots]
-        temporal = terms if temporal is None else [a + b for a, b in zip(temporal, terms)]
     for tap in range(3):
         for side in range(3):
             block = parts[tap][:, side * channels : (side + 1) * channels].T
             store_rows(grads, rows, (3 * tap + side) * channels, block.astype(jnp.bfloat16))
     for tap in range(3):
-        block = (temporal[tap] * loss_scale).astype(jnp.bfloat16)
+        block = temporal[pl.ds(tap * channels, channels)]
         store_rows(grads, rows, (9 + tap) * channels, block)
     rest = grads.shape[0] * rows - 12 * channels
     if rest:
         store_rows(grads, rows, 12 * channels, jnp.zeros((rest, channels), jnp.bfloat16))
-    extra = split_rows([own[0, 1:2], own[0, 0:1]], EXTRA)
+    share = clip * (1.0 / sums.shape[0])
+    extra = split_rows([share[1:2], share[0:1]], EXTRA)
     for chunk in range(grads.shape[0]):
         grads[chunk, pl.ds(rows, EXTRA)] = extra
+    encode(act, act_halo, weights, encoded)
 
 
 def total_of(arrived, first, count):
@@ -341,7 +344,7 @@
     grad_temporal[...] = arrived[pl.ds(rows, grad_temporal.shape[0])].astype(jnp.float32)
 
 
-def encode_kernel(act, halo, weights, encoded):
+def encode(act, halo, weights, encoded):
     frames, out_rows, out_cols, channels = act.shape
     flat = (STEP_ROWS * out_cols, channels)
     for frame in range(frames):
@@ -415,13 +418,13 @@
         flops=2 * positions * 9 * channels * channels,
     )
     stats = exchange(stats, "seq", clips)
-    act, normed, pre, inv, own = call(
+    act, normed, pre, temporal, own = call(
         functools.partial(act_kernel, loss_scale),
         (
             struct(shape, bf16),
             struct(shape, f32),
             struct(shape, f32),
-            struct((1, channels), f32),
+            struct((3 * channels, channels), bf16),
             struct((per_clip, 8, channels), f32),
         ),
         (spatial, stats, cot, cot_halo, w_temporal, params),
@@ -429,18 +432,11 @@
     )
     act_halo = lax.ppermute(act, "seq", ahead_pairs)
     sums = exchange(own, "seq", clips)
-    encoded = call(
-        encode_kernel,
-        struct(shape, bf16),
-        (act, act_halo, w_temporal),
-        flops=2 * positions * 3 * channels * channels,
-    )
-    encoded, sums = lax.optimization_barrier((encoded, sums))
     rows = -(-12 * channels // (16 * devices)) * 16
-    grads = call(
-        functools.partial(grad_kernel, loss_scale),
-        struct((devices, rows + EXTRA, channels), bf16),
-        (odd, even, normed, pre, inv, own, sums, params, act, cot, cot_halo),
+    grads, encoded = call(
+        grad_kernel,
+        (struct((devices, rows + EXTRA, channels), bf16), struct(shape, bf16)),
+        (odd, even, normed, pre, sums, temporal, act, act_halo, w_temporal),
         flops=2 * positions * 12 * channels * channels,
     )
     grads = exchange(grads, ("dp", "seq"))

time: 69.1 us -> 64.7 us (0.936)
  blocking collectives: 45.2 us -> 52.4 us
  starting transfers between devices: 8.36 us -> 3.82 us
  waiting for transfers between devices: 2.76 us -> 0.01 us
  local copies, waits for them, and re-layouts: 2.53 us -> 0.01 us
  Pallas kernels: 9.02 us -> 7.44 us
    all_to_all x3 -> x4, blocking collectives: 45.2 us -> 52.4 us  [exchange(): lax.all_to_all(value, axes, 0, 0, axis_index_groups=groups, tiled=True)]
    all_to_all x1 -> x0, starting transfers between devices: 3.86 us -> none  [exchange(): lax.all_to_all(value, axes, 0, 0, axis_index_groups=groups, tiled=True)]
    all_to_all x1 -> x0, waiting for transfers between devices: 2.76 us -> none  [exchange(): lax.all_to_all(value, axes, 0, 0, axis_index_groups=groups, tiled=True)]
    unnamed x16 -> x4, local copies, waits for them, and re-layouts: 2.53 us -> 0.01 us
    pallas_call x6 -> x5, Pallas kernels: 9.02 us -> 7.44 us  [call(): pl.pallas_call(kernel, out_shape=out_shape, in_specs=specs or [WHOLE] * l...]
  transfers between devices with their start and end apart: 3 -> 2, of which waited for: 1 -> 0; matrix products, arithmetic and copies ran while one was open for 0% -> 0% of each run, Pallas kernels for 7% -> 4%
where the time goes in v4:
time: 64.7 us; the launch traced here: 64.4 us
  blocking collectives  52.4 us (81%)
  Pallas kernels  7.44 us (11%)
  starting transfers between devices  3.82 us (6%)
  between operations  0.69 us (1%)
    all_to_all x4, blocking collectives, exchange(): lax.all_to_all(value, axes, 0, 0, axis_index_groups=groups, tiled=True)  52.4 us
    pallas_call x5, Pallas kernels, call(): pl.pallas_call(kernel, out_shape=out_shape, in_specs=specs or [WHOLE] * l...  7.44 us
    ppermute x1, starting transfers between devices, on_device(): act_halo = lax.ppermute(act, 'seq', ahead_pairs)  2.53 us
  transfers between devices with their start and end apart: 2, of which 0 were waited for; matrix products, arithmetic and copies ran while one was open for 0% of the time, Pallas kernels for 4%

profile of v4, /device:TPU:0, one launch (start us, length us, event | category | flops | bytes accessed | tf_op | source)
XLA Modules:
  0.0 64.4 jit_solution(9519494756931747399)
XLA Ops:
  0.6 1.3 %collective-permute-start = (bf16[2,16,32,128]{3,2,1,0:T(8,128)(2,1)}, bf16[2,16,32,128]{3,2,1,0:T(8,128)(2,1)S(1)}, u32[]{:S(2)}, u32[]{:S(2)}) collective-permute-start(bf16[2,16,32,128]{3,2,1,0:T(8,128)(2,1)} %bitcast.12), channel_id=1, source_target_pairs={{1,0},{2,1},{3,2},{5,4},{6,5},{7,6},{9,8},{10,9},{11,10},{13,12},{... | collective-permute-start | bytes 786440 | tf_op jit(solution)/shard_map/ppermute | solution.py:393
  1.9 0.0 copy-start
  1.9 0.0 copy-start.1
  2.0 2.8 %shard_map.101 = (f32[2,16,32,128]{3,2,1,0:T(8,128)S(1)}, f32[4,8,128]{2,1,0:T(8,128)S(1)}, bf16[2,17,32,384]{3,2,1,0:T(8,128)(2,1)S(1)}, bf16[2,16,32,384]{3,2,1,0:T(8,128)(2,1)S(1)}, f32[8,128]{1,0:T(8,128)S(1)}) custom-call(bf16[2,32,64,128]{3,2,1,0:T(8,128)(2,1)} %bitcast.14, bf16[3,384,128]{2,1,0:T(8,128)(2,1)} %bitcast.15, f32[1,128]{1,0:T(1,128)} %bitcast.16, ...), custom_call_target="tpu_custom_call" | custom-call | flops 301989888 | bytes 3511296 | tf_op jit(solution)/shard_map/pallas_call | solution.py:43
  4.7 10.9 %all_to_all.20.stats = f32[4,8,128]{2,1,0:T(8,128)S(1)} all-to-all(f32[4,8,128]{2,1,0:T(8,128)S(1)} %get-tuple-element.25), channel_id=1, replica_groups={{0,1,2,3},{4,5,6,7},{8,9,10,11},{12,13,14,15},{16,17,18,19},{20,21,22,2..., dimensions={0} | all-to-all | bytes 32768 | tf_op jit(solution)/shard_map/all_to_all | solution.py:388
  15.6 0.0 collective-permute-done.halo
  15.6 0.0 copy-done
  15.6 0.0 copy-done.1
  15.6 1.4 %shard_map.102 = (bf16[2,16,32,128]{3,2,1,0:T(8,128)(2,1)S(1)}, f32[2,16,32,128]{3,2,1,0:T(8,128)S(1)}, f32[2,16,32,128]{3,2,1,0:T(8,128)S(1)}, bf16[384,128]{1,0:T(8,128)(2,1)S(1)}, f32[4,8,128]{2,1,0:T(8,128)S(1)}) custom-call(f32[2,16,32,128]{3,2,1,0:T(8,128)S(1)} %get-tuple-element.24.spatial, f32[4,8,128]{2,1,0:T(8,128)S(1)} %all_to_all.20.stats, ...), custom_call_target="tpu_custom_call" | custom-call | flops 100663296 | bytes 2592768 | tf_op jit(solution)/shard_map/pallas_call | solution.py:43
  17.0 2.5 %collective-permute-start.1 = (bf16[2,16,32,128]{3,2,1,0:T(8,128)(2,1)S(1)}, bf16[2,16,32,128]{3,2,1,0:T(8,128)(2,1)S(1)}, u32[]{:S(2)}, u32[]{:S(2)}) collective-permute-start(bf16[2,16,32,128]{3,2,1,0:T(8,128)(2,1)S(1)} %get-tuple-element.31.act), channel_id=1, source_target_pairs={{0,1},{1,2},{2,3},{4,5},{5,6},{6,7},{8,9},{9,10},{10,11},{12,13},{... | collective-permute-start | bytes 786440 | tf_op jit(solution)/shard_map/ppermute | solution.py:433
  19.5 7.2 %all_to_all.21.sums = f32[4,8,128]{2,1,0:T(8,128)S(1)} all-to-all(f32[4,8,128]{2,1,0:T(8,128)S(1)} %get-tuple-element.29), channel_id=1, replica_groups={{0,1,2,3},{4,5,6,7},{8,9,10,11},{12,13,14,15},{16,17,18,19},{20,21,22,2..., dimensions={0} | all-to-all | bytes 32768 | tf_op jit(solution)/shard_map/all_to_all | solution.py:388
  26.8 0.0 collective-permute-done.1.act_halo
  26.8 1.8 %shard_map.103 = (bf16[32,56,128]{2,1,0:T(8,128)(2,1)S(1)}, bf16[2,16,32,128]{3,2,1,0:T(8,128)(2,1)}) custom-call(bf16[2,17,32,384]{3,2,1,0:T(8,128)(2,1)S(1)} %get-tuple-element.22.odd, bf16[2,16,32,384]{3,2,1,0:T(8,128)(2,1)S(1)} %get-tuple-element.23.even, f32[2,16,32,128]{3,2,1,0:T(8,128)S(1)} %get-tuple-element.27.normed, ...), custom_call_target="tpu_custom_call" | custom-call | flops 402653184 | bytes 4128768 | tf_op jit(solution)/shard_map/pallas_call | solution.py:43
  28.6 18.7 %all_to_all.22.arrived = bf16[32,56,128]{2,1,0:T(8,128)(2,1)S(1)} all-to-all(bf16[32,56,128]{2,1,0:T(8,128)(2,1)S(1)} %get-tuple-element.33), channel_id=1, replica_groups=mesh['dp'=4,'seq'=8] {'dp','seq'}, dimensions={0} | all-to-all | bytes 917504 | tf_op jit(solution)/shard_map/all_to_all | solution.py:388
  47.3 0.6 shard_map.104
  47.9 15.6 %all_to_all.23 = bf16[32,48,128]{2,1,0:T(8,128)(2,1)S(1)} all-to-all(bf16[32,48,128]{2,1,0:T(8,128)(2,1)S(1)} %get-tuple-element.34), channel_id=1, replica_groups=mesh['dp'=4,'seq'=8] {'dp','seq'}, dimensions={0} | all-to-all | bytes 786432 | tf_op jit(solution)/shard_map/all_to_all | solution.py:388
  63.5 0.9 %shard_map.105 = (f32[1152,128]{1,0:T(8,128)}, f32[384,128]{1,0:T(8,128)}) custom-call(bf16[1536,128]{1,0:T(8,128)(2,1)S(1)} %bitcast.11), custom_call_target="tpu_custom_call" | custom-call | bytes 1179648 | tf_op jit(solution)/shard_map/pallas_call | solution.py:43
Async XLA Ops:
  0.6 15.0 %collective-permute-start = (bf16[2,16,32,128]{3,2,1,0:T(8,128)(2,1)}, bf16[2,16,32,128]{3,2,1,0:T(8,128)(2,1)S(1)}, u32[]{:S(2)}, u32[]{:S(2)}) collective-permute-start(bf16[2,16,32,128]{3,2,1,0:T(8,128)(2,1)} %bitcast.12), channel_id=1, source_target_pairs={{1,0},{2,1},{3,2},{5,4},{6,5},{7,6},{9,8},{10,9},{11,10},{13,12},{... | collective-permute-start | bytes 786440 | tf_op jit(solution)/shard_map/ppermute | solution.py:393
  1.9 13.7 %copy-start = (bf16[3,128,128]{2,1,0:T(8,128)(2,1)S(1)}, bf16[3,128,128]{2,1,0:T(8,128)(2,1)}, u32[]{:S(2)}) copy-start(bf16[3,128,128]{2,1,0:T(8,128)(2,1)} %weights.3) | copy-start | bytes 294916
  1.9 13.7 %copy-start.1 = (bf16[1,2,16,32,128]{4,3,2,1,0:T(8,128)(2,1)S(1)}, bf16[1,2,16,32,128]{4,3,2,1,0:T(8,128)(2,1)}, u32[]{:S(2)}) copy-start(bf16[1,2,16,32,128]{4,3,2,1,0:T(8,128)(2,1)} %param.11) | copy-start | bytes 786436
  17.0 9.8 %collective-permute-start.1 = (bf16[2,16,32,128]{3,2,1,0:T(8,128)(2,1)S(1)}, bf16[2,16,32,128]{3,2,1,0:T(8,128)(2,1)S(1)}, u32[]{:S(2)}, u32[]{:S(2)}) collective-permute-start(bf16[2,16,32,128]{3,2,1,0:T(8,128)(2,1)S(1)} %get-tuple-element.31.act), channel_id=1, source_target_pairs={{0,1},{1,2},{2,3},{4,5},{5,6},{6,7},{8,9},{9,10},{10,11},{12,13},{... | collective-permute-start | bytes 786440 | tf_op jit(solution)/shard_map/ppermute | solution.py:433

commit v5 on v4

--- a/solution.py
+++ b/solution.py
@@ -331,10 +331,9 @@
 
 
 def sum_kernel(arrived, spread, grad_gain, grad_shift):
-    count = spread.shape[1]
+    count = spread.shape[0]
     total = total_of(arrived, 0, count).astype(jnp.bfloat16)
-    for slot in range(spread.shape[0]):
-        spread[slot] = total
+    spread[...] = total
     grad_gain[...], grad_shift[...] = join_rows(total_of(arrived, count, EXTRA), 2)
 
 
@@ -443,17 +442,17 @@
     grads, grad_gain, grad_shift = call(
         sum_kernel,
         (
-            struct((devices, rows, channels), bf16),
+            struct((rows, channels), bf16),
             struct((1, channels), f32),
             struct((1, channels), f32),
         ),
         (grads,),
     )
-    grads = exchange(grads, ("dp", "seq"))
+    grads = lax.all_gather(grads, ("dp", "seq"), axis=0, tiled=True)
     grad_spatial, grad_temporal = call(
         final_kernel,
         (struct((9 * channels, channels), f32), struct((3 * channels, channels), f32)),
-        (grads.reshape(devices * rows, channels),),
+        (grads,),
     )
     return (
         encoded[None],

time: 64.7 us -> 115 us (1.78)
  blocking collectives: 52.4 us -> 103 us
    all_gather x0 -> x1, blocking collectives: none -> 66.4 us  [on_device(): grads = lax.all_gather(grads, ('dp', 'seq'), axis=0, tiled=True)]
    all_to_all x4 -> x3, blocking collectives: 52.4 us -> 36.8 us  [exchange(): lax.all_to_all(value, axes, 0, 0, axis_index_groups=groups, tiled=True)]
  transfers between devices with their start and end apart: 2 -> 2, of which waited for: 0 -> 0; matrix products, arithmetic and copies ran while one was open for 0% -> 0% of each run, Pallas kernels for 4% -> 2%
where the time goes in v5:
time: 115 us
  blocking collectives  103 us (90%)
  Pallas kernels  7.44 us (6%)
  starting transfers between devices  3.82 us (3%)
    all_gather x1, blocking collectives, on_device(): grads = lax.all_gather(grads, ('dp', 'seq'), axis=0, tiled=True)  66.4 us
    all_to_all x3, blocking collectives, exchange(): lax.all_to_all(value, axes, 0, 0, axis_index_groups=groups, tiled=True)  36.8 us
    pallas_call x5, Pallas kernels, call(): pl.pallas_call(kernel, out_shape=out_shape, in_specs=specs or [WHOLE] * l...  7.44 us
    ppermute x1, starting transfers between devices, on_device(): act_halo = lax.ppermute(act, 'seq', ahead_pairs)  2.53 us
  transfers between devices with their start and end apart: 2, of which 0 were waited for; matrix products, arithmetic and copies ran while one was open for 0% of the time, Pallas kernels for 2%

profile of v5, /device:TPU:0, one launch (start us, length us, event | category | flops | bytes accessed | tf_op | source)
XLA Modules:
  0.0 115.2 jit_solution(5038876745845151556)
XLA Ops:
  0.6 1.3 %collective-permute-start = (bf16[2,16,32,128]{3,2,1,0:T(8,128)(2,1)}, bf16[2,16,32,128]{3,2,1,0:T(8,128)(2,1)S(1)}, u32[]{:S(2)}, u32[]{:S(2)}) collective-permute-start(bf16[2,16,32,128]{3,2,1,0:T(8,128)(2,1)} %bitcast.10), channel_id=1, source_target_pairs={{1,0},{2,1},{3,2},{5,4},{6,5},{7,6},{9,8},{10,9},{11,10},{13,12},{... | collective-permute-start | bytes 786440 | tf_op jit(solution)/shard_map/ppermute | solution.py:392
  1.9 0.0 copy-start
  1.9 0.0 copy-start.1
  2.0 2.8 %shard_map.101 = (f32[2,16,32,128]{3,2,1,0:T(8,128)S(1)}, f32[4,8,128]{2,1,0:T(8,128)S(1)}, bf16[2,17,32,384]{3,2,1,0:T(8,128)(2,1)S(1)}, bf16[2,16,32,384]{3,2,1,0:T(8,128)(2,1)S(1)}, f32[8,128]{1,0:T(8,128)S(1)}) custom-call(bf16[2,32,64,128]{3,2,1,0:T(8,128)(2,1)} %bitcast.12, bf16[3,384,128]{2,1,0:T(8,128)(2,1)} %bitcast.13, f32[1,128]{1,0:T(1,128)} %bitcast.14, ...), custom_call_target="tpu_custom_call" | custom-call | flops 301989888 | bytes 3511296 | tf_op jit(solution)/shard_map/pallas_call | solution.py:43
  4.7 10.9 %all_to_all.15.stats = f32[4,8,128]{2,1,0:T(8,128)S(1)} all-to-all(f32[4,8,128]{2,1,0:T(8,128)S(1)} %get-tuple-element.25), channel_id=1, replica_groups={{0,1,2,3},{4,5,6,7},{8,9,10,11},{12,13,14,15},{16,17,18,19},{20,21,22,2..., dimensions={0} | all-to-all | bytes 32768 | tf_op jit(solution)/shard_map/all_to_all | solution.py:387
  15.6 0.0 collective-permute-done.halo
  15.6 0.0 copy-done
  15.6 0.0 copy-done.1
  15.6 1.4 %shard_map.102 = (bf16[2,16,32,128]{3,2,1,0:T(8,128)(2,1)S(1)}, f32[2,16,32,128]{3,2,1,0:T(8,128)S(1)}, f32[2,16,32,128]{3,2,1,0:T(8,128)S(1)}, bf16[384,128]{1,0:T(8,128)(2,1)S(1)}, f32[4,8,128]{2,1,0:T(8,128)S(1)}) custom-call(f32[2,16,32,128]{3,2,1,0:T(8,128)S(1)} %get-tuple-element.24.spatial, f32[4,8,128]{2,1,0:T(8,128)S(1)} %all_to_all.15.stats, ...), custom_call_target="tpu_custom_call" | custom-call | flops 100663296 | bytes 2592768 | tf_op jit(solution)/shard_map/pallas_call | solution.py:43
  17.0 2.5 %collective-permute-start.1 = (bf16[2,16,32,128]{3,2,1,0:T(8,128)(2,1)S(1)}, bf16[2,16,32,128]{3,2,1,0:T(8,128)(2,1)S(1)}, u32[]{:S(2)}, u32[]{:S(2)}) collective-permute-start(bf16[2,16,32,128]{3,2,1,0:T(8,128)(2,1)S(1)} %get-tuple-element.31.act), channel_id=1, source_target_pairs={{0,1},{1,2},{2,3},{4,5},{5,6},{6,7},{8,9},{9,10},{10,11},{12,13},{... | collective-permute-start | bytes 786440 | tf_op jit(solution)/shard_map/ppermute | solution.py:432
  19.5 7.2 %all_to_all.16.sums = f32[4,8,128]{2,1,0:T(8,128)S(1)} all-to-all(f32[4,8,128]{2,1,0:T(8,128)S(1)} %get-tuple-element.29), channel_id=1, replica_groups={{0,1,2,3},{4,5,6,7},{8,9,10,11},{12,13,14,15},{16,17,18,19},{20,21,22,2..., dimensions={0} | all-to-all | bytes 32768 | tf_op jit(solution)/shard_map/all_to_all | solution.py:387
  26.8 0.0 collective-permute-done.1.act_halo
  26.8 1.8 %shard_map.103 = (bf16[32,56,128]{2,1,0:T(8,128)(2,1)S(1)}, bf16[2,16,32,128]{3,2,1,0:T(8,128)(2,1)}) custom-call(bf16[2,17,32,384]{3,2,1,0:T(8,128)(2,1)S(1)} %get-tuple-element.22.odd, bf16[2,16,32,384]{3,2,1,0:T(8,128)(2,1)S(1)} %get-tuple-element.23.even, f32[2,16,32,128]{3,2,1,0:T(8,128)S(1)} %get-tuple-element.27.normed, ...), custom_call_target="tpu_custom_call" | custom-call | flops 402653184 | bytes 4128768 | tf_op jit(solution)/shard_map/pallas_call | solution.py:43
  28.6 18.7 %all_to_all.17.arrived = bf16[32,56,128]{2,1,0:T(8,128)(2,1)S(1)} all-to-all(bf16[32,56,128]{2,1,0:T(8,128)(2,1)S(1)} %get-tuple-element.33), channel_id=1, replica_groups=mesh['dp'=4,'seq'=8] {'dp','seq'}, dimensions={0} | all-to-all | bytes 917504 | tf_op jit(solution)/shard_map/all_to_all | solution.py:387
  47.3 0.6 shard_map.104
  47.9 66.4 %all_gather.3.arrived = bf16[1536,128]{1,0:T(8,128)(2,1)S(1)} all-gather(bf16[48,128]{1,0:T(8,128)(2,1)S(1)} %get-tuple-element.34), channel_id=1, replica_groups=mesh['dp'=4,'seq'=8] {'dp','seq'}, dimensions={0}, use_global_device_ids=true | all-gather | bytes 405504 | tf_op jit(solution)/shard_map/all_gather | solution.py:451
  114.3 0.9 shard_map.105
Async XLA Ops:
  0.6 15.0 %collective-permute-start = (bf16[2,16,32,128]{3,2,1,0:T(8,128)(2,1)}, bf16[2,16,32,128]{3,2,1,0:T(8,128)(2,1)S(1)}, u32[]{:S(2)}, u32[]{:S(2)}) collective-permute-start(bf16[2,16,32,128]{3,2,1,0:T(8,128)(2,1)} %bitcast.10), channel_id=1, source_target_pairs={{1,0},{2,1},{3,2},{5,4},{6,5},{7,6},{9,8},{10,9},{11,10},{13,12},{... | collective-permute-start | bytes 786440 | tf_op jit(solution)/shard_map/ppermute | solution.py:392
  1.9 13.7 %copy-start = (bf16[3,128,128]{2,1,0:T(8,128)(2,1)S(1)}, bf16[3,128,128]{2,1,0:T(8,128)(2,1)}, u32[]{:S(2)}) copy-start(bf16[3,128,128]{2,1,0:T(8,128)(2,1)} %weights.3) | copy-start | bytes 294916
  1.9 13.7 %copy-start.1 = (bf16[1,2,16,32,128]{4,3,2,1,0:T(8,128)(2,1)S(1)}, bf16[1,2,16,32,128]{4,3,2,1,0:T(8,128)(2,1)}, u32[]{:S(2)}) copy-start(bf16[1,2,16,32,128]{4,3,2,1,0:T(8,128)(2,1)} %param.11) | copy-start | bytes 786436
  17.0 9.8 %collective-permute-start.1 = (bf16[2,16,32,128]{3,2,1,0:T(8,128)(2,1)S(1)}, bf16[2,16,32,128]{3,2,1,0:T(8,128)(2,1)S(1)}, u32[]{:S(2)}, u32[]{:S(2)}) collective-permute-start(bf16[2,16,32,128]{3,2,1,0:T(8,128)(2,1)S(1)} %get-tuple-element.31.act), channel_id=1, source_target_pairs={{0,1},{1,2},{2,3},{4,5},{5,6},{6,7},{8,9},{9,10},{10,11},{12,13},{... | collective-permute-start | bytes 786440 | tf_op jit(solution)/shard_map/ppermute | solution.py:432

commit v6 on v4

--- a/solution.py
+++ b/solution.py
@@ -330,12 +330,22 @@
     return total
 
 
-def sum_kernel(arrived, spread, grad_gain, grad_shift):
+def half_kernel(arrived, chunk):
+    count = chunk.shape[0] - EXTRA
+    chunk[pl.ds(0, count)] = total_of(arrived, 0, count).astype(jnp.bfloat16)
+    sums = join_rows(total_of(arrived, count, EXTRA), 2)
+    chunk[pl.ds(count, EXTRA)] = split_rows(sums, EXTRA)
+
+
+def sum_kernel(mine, other, spread, grad_gain, grad_shift):
     count = spread.shape[1]
-    total = total_of(arrived, 0, count).astype(jnp.bfloat16)
+    wide = [source[...].astype(jnp.float32) for source in (mine, other)]
+    total = (wide[0][:count] + wide[1][:count]).astype(jnp.bfloat16)
     for slot in range(spread.shape[0]):
         spread[slot] = total
-    grad_gain[...], grad_shift[...] = join_rows(total_of(arrived, count, EXTRA), 2)
+    sums = [join_rows(source[count:], 2) for source in wide]
+    grad_gain[...] = sums[0][0] + sums[1][0]
+    grad_shift[...] = sums[0][1] + sums[1][1]
 
 
 def final_kernel(arrived, grad_spatial, grad_temporal):
@@ -432,28 +442,40 @@
     )
     act_halo = lax.ppermute(act, "seq", ahead_pairs)
     sums = exchange(own, "seq", clips)
-    rows = -(-12 * channels // (16 * devices)) * 16
+    halves = 2 if seq_size % 2 == 0 else 1
+    half = seq_size // halves
+    near = [
+        [d * seq_size + s for d in range(dp_size) for s in range(first, first + half)]
+        for first in range(0, seq_size, half)
+    ]
+    count = dp_size * half
+    rows = -(-12 * channels // (16 * count)) * 16
     grads, encoded = call(
         grad_kernel,
-        (struct((devices, rows + EXTRA, channels), bf16), struct(shape, bf16)),
+        (struct((count, rows + EXTRA, channels), bf16), struct(shape, bf16)),
         (odd, even, normed, pre, sums, temporal, act, act_halo, w_temporal),
         flops=2 * positions * 12 * channels * channels,
     )
-    grads = exchange(grads, ("dp", "seq"))
+    grads = exchange(grads, ("dp", "seq"), near)
+    mine = call(half_kernel, struct((rows + EXTRA, channels), bf16), (grads,))
+    if halves == 2:
+        other = lax.ppermute(mine, "seq", [(s, (s + half) % seq_size) for s in range(seq_size)])
+    else:
+        other = jnp.zeros_like(mine)
     grads, grad_gain, grad_shift = call(
         sum_kernel,
         (
-            struct((devices, rows, channels), bf16),
+            struct((count, rows, channels), bf16),
             struct((1, channels), f32),
             struct((1, channels), f32),
         ),
-        (grads,),
-    )
-    grads = exchange(grads, ("dp", "seq"))
+        (mine, other),
+    )
+    grads = exchange(grads, ("dp", "seq"), near)
     grad_spatial, grad_temporal = call(
         final_kernel,
         (struct((9 * channels, channels), f32), struct((3 * channels, channels), f32)),
-        (grads.reshape(devices * rows, channels),),
+        (grads.reshape(count * rows, channels),),
     )
     return (
         encoded[None],

time: 64.7 us -> 57.3 us (0.89)
  blocking collectives: 52.4 us -> 40.1 us
  starting transfers between devices: 3.82 us -> 6.47 us
  waiting for transfers between devices: 0.01 us -> 2.27 us
    all_to_all x4, blocking collectives: 52.4 us -> 40.1 us  [exchange(): lax.all_to_all(value, axes, 0, 0, axis_index_groups=groups, tiled=True)]
    ppermute x0 -> x1, starting transfers between devices: none -> 2.65 us  [on_device(): lax.ppermute(mine, 'seq', [(s, (s + half) % seq_size) for s in range(seq_...]
    ppermute x0 -> x1, waiting for transfers between devices: none -> 2.26 us  [on_device(): lax.ppermute(mine, 'seq', [(s, (s + half) % seq_size) for s in range(seq_...]
    pallas_call x5 -> x6, Pallas kernels: 7.44 us -> 7.49 us  [call(): pl.pallas_call(kernel, out_shape=out_shape, in_specs=specs or [WHOLE] * l...]
  transfers between devices with their start and end apart: 2 -> 3, of which waited for: 0 -> 1; matrix products, arithmetic and copies ran while one was open for 0% -> 0% of each run, Pallas kernels for 4% -> 5%
where the time goes in v6:
time: 57.3 us; the launch traced here: 57 us
  blocking collectives  40.1 us (70%)
  Pallas kernels  7.49 us (13%)
  starting transfers between devices  6.47 us (11%)
  waiting for transfers between devices  2.27 us (4%)
  between operations  0.69 us (1%)
    all_to_all x4, blocking collectives, exchange(): lax.all_to_all(value, axes, 0, 0, axis_index_groups=groups, tiled=True)  40.1 us
    pallas_call x6, Pallas kernels, call(): pl.pallas_call(kernel, out_shape=out_shape, in_specs=specs or [WHOLE] * l...  7.49 us
    ppermute x1, starting transfers between devices, on_device(): lax.ppermute(mine, 'seq', [(s, (s + half) % seq_size) for s in range(seq_...  2.65 us
    ppermute x1, starting transfers between devices, on_device(): act_halo = lax.ppermute(act, 'seq', ahead_pairs)  2.53 us
    ppermute x1, waiting for transfers between devices, on_device(): lax.ppermute(mine, 'seq', [(s, (s + half) % seq_size) for s in range(seq_...  2.26 us
    ppermute x1, starting transfers between devices, on_device(): cot_halo = lax.ppermute(cot, 'seq', back_pairs)  1.29 us
  transfers between devices with their start and end apart: 3, of which 1 were waited for; matrix products, arithmetic and copies ran while one was open for 0% of the time, Pallas kernels for 5%

profile of v6, /device:TPU:0, one launch (start us, length us, event | category | flops | bytes accessed | tf_op | source)
XLA Modules:
  0.0 57.0 jit_solution(18412850837949557560)
XLA Ops:
  0.6 1.3 %collective-permute-start = (bf16[2,16,32,128]{3,2,1,0:T(8,128)(2,1)}, bf16[2,16,32,128]{3,2,1,0:T(8,128)(2,1)S(1)}, u32[]{:S(2)}, u32[]{:S(2)}) collective-permute-start(bf16[2,16,32,128]{3,2,1,0:T(8,128)(2,1)} %bitcast.12), channel_id=1, source_target_pairs={{1,0},{2,1},{3,2},{5,4},{6,5},{7,6},{9,8},{10,9},{11,10},{13,12},{... | collective-permute-start | bytes 786440 | tf_op jit(solution)/shard_map/ppermute | solution.py:403
  1.9 0.0 copy-start
  1.9 0.0 copy-start.1
  2.0 2.8 %shard_map.101 = (f32[2,16,32,128]{3,2,1,0:T(8,128)S(1)}, f32[4,8,128]{2,1,0:T(8,128)S(1)}, bf16[2,17,32,384]{3,2,1,0:T(8,128)(2,1)S(1)}, bf16[2,16,32,384]{3,2,1,0:T(8,128)(2,1)S(1)}, f32[8,128]{1,0:T(8,128)S(1)}) custom-call(bf16[2,32,64,128]{3,2,1,0:T(8,128)(2,1)} %bitcast.14, bf16[3,384,128]{2,1,0:T(8,128)(2,1)} %bitcast.15, f32[1,128]{1,0:T(1,128)} %bitcast.16, ...), custom_call_target="tpu_custom_call" | custom-call | flops 301989888 | bytes 3511296 | tf_op jit(solution)/shard_map/pallas_call | solution.py:43
  4.7 10.9 %all_to_all.20.stats = f32[4,8,128]{2,1,0:T(8,128)S(1)} all-to-all(f32[4,8,128]{2,1,0:T(8,128)S(1)} %get-tuple-element.25), channel_id=1, replica_groups={{0,1,2,3},{4,5,6,7},{8,9,10,11},{12,13,14,15},{16,17,18,19},{20,21,22,2..., dimensions={0} | all-to-all | bytes 32768 | tf_op jit(solution)/shard_map/all_to_all | solution.py:398
  15.6 0.0 collective-permute-done.halo
  15.6 0.0 copy-done
  15.6 0.0 copy-done.1
  15.6 1.4 %shard_map.102 = (bf16[2,16,32,128]{3,2,1,0:T(8,128)(2,1)S(1)}, f32[2,16,32,128]{3,2,1,0:T(8,128)S(1)}, f32[2,16,32,128]{3,2,1,0:T(8,128)S(1)}, bf16[384,128]{1,0:T(8,128)(2,1)S(1)}, f32[4,8,128]{2,1,0:T(8,128)S(1)}) custom-call(f32[2,16,32,128]{3,2,1,0:T(8,128)S(1)} %get-tuple-element.24.spatial, f32[4,8,128]{2,1,0:T(8,128)S(1)} %all_to_all.20.stats, ...), custom_call_target="tpu_custom_call" | custom-call | flops 100663296 | bytes 2592768 | tf_op jit(solution)/shard_map/pallas_call | solution.py:43
  17.0 2.5 %collective-permute-start.1 = (bf16[2,16,32,128]{3,2,1,0:T(8,128)(2,1)S(1)}, bf16[2,16,32,128]{3,2,1,0:T(8,128)(2,1)S(1)}, u32[]{:S(2)}, u32[]{:S(2)}) collective-permute-start(bf16[2,16,32,128]{3,2,1,0:T(8,128)(2,1)S(1)} %get-tuple-element.31.act), channel_id=1, source_target_pairs={{0,1},{1,2},{2,3},{4,5},{5,6},{6,7},{8,9},{9,10},{10,11},{12,13},{... | collective-permute-start | bytes 786440 | tf_op jit(solution)/shard_map/ppermute | solution.py:443
  19.5 7.2 %all_to_all.21.sums = f32[4,8,128]{2,1,0:T(8,128)S(1)} all-to-all(f32[4,8,128]{2,1,0:T(8,128)S(1)} %get-tuple-element.29), channel_id=1, replica_groups={{0,1,2,3},{4,5,6,7},{8,9,10,11},{12,13,14,15},{16,17,18,19},{20,21,22,2..., dimensions={0} | all-to-all | bytes 32768 | tf_op jit(solution)/shard_map/all_to_all | solution.py:398
  26.8 0.0 collective-permute-done.1.act_halo
  26.8 1.8 %shard_map.103 = (bf16[16,104,128]{2,1,0:T(8,128)(2,1)S(1)}, bf16[2,16,32,128]{3,2,1,0:T(8,128)(2,1)}) custom-call(bf16[2,17,32,384]{3,2,1,0:T(8,128)(2,1)S(1)} %get-tuple-element.22.odd, bf16[2,16,32,384]{3,2,1,0:T(8,128)(2,1)S(1)} %get-tuple-element.23.even, f32[2,16,32,128]{3,2,1,0:T(8,128)S(1)} %get-tuple-element.27.normed, ...), custom_call_target="tpu_custom_call" | custom-call | flops 402653184 | bytes 4096000 | tf_op jit(solution)/shard_map/pallas_call | solution.py:43
  28.6 11.0 %all_to_all.22.arrived = bf16[16,104,128]{2,1,0:T(8,128)(2,1)S(1)} all-to-all(bf16[16,104,128]{2,1,0:T(8,128)(2,1)S(1)} %get-tuple-element.33), channel_id=1, replica_groups={{0,1,2,3,8,9,10,11,16,17,18,19,24,25,26,27},{4,5,6,7,12,13,14,15,20,21,..., dimensions={0} | all-to-all | bytes 851968 | tf_op jit(solution)/shard_map/all_to_all | solution.py:398
  39.7 0.1 shard_map.104.mine
  39.7 2.6 %collective-permute-start.2 = (bf16[104,128]{1,0:T(8,128)(2,1)S(1)}, bf16[104,128]{1,0:T(8,128)(2,1)S(1)}, u32[]{:S(2)}, u32[]{:S(2)}) collective-permute-start(bf16[104,128]{1,0:T(8,128)(2,1)S(1)} %shard_map.104.mine), channel_id=1, source_target_pairs={{0,4},{1,5},{2,6},{3,7},{4,0},{5,1},{6,2},{7,3},{8,12},{9,13},{10,... | collective-permute-start | bytes 79880 | tf_op jit(solution)/shard_map/ppermute | solution.py:462
  42.4 2.3 %collective-permute-done.2.other = bf16[104,128]{1,0:T(8,128)(2,1)S(1)} collective-permute-done((bf16[104,128]{1,0:T(8,128)(2,1)S(1)}, bf16[104,128]{1,0:T(8,128)(2,1)S(1)}, u32[]{:S(2)}, u32[]{:S(2)}) %collective-permute-start.2) | collective-permute-done | bytes 26656 | tf_op jit(solution)/shard_map/ppermute | solution.py:462
  44.7 0.5 shard_map.105
  45.2 10.9 %all_to_all.23 = bf16[16,96,128]{2,1,0:T(8,128)(2,1)S(1)} all-to-all(bf16[16,96,128]{2,1,0:T(8,128)(2,1)S(1)} %get-tuple-element.34), channel_id=1, replica_groups={{0,1,2,3,8,9,10,11,16,17,18,19,24,25,26,27},{4,5,6,7,12,13,14,15,20,21,..., dimensions={0} | all-to-all | bytes 786432 | tf_op jit(solution)/shard_map/all_to_all | solution.py:398
  56.1 0.9 %shard_map.106 = (f32[1152,128]{1,0:T(8,128)}, f32[384,128]{1,0:T(8,128)}) custom-call(bf16[1536,128]{1,0:T(8,128)(2,1)S(1)} %bitcast.11), custom_call_target="tpu_custom_call" | custom-call | bytes 1179648 | tf_op jit(solution)/shard_map/pallas_call | solution.py:43
Async XLA Ops:
  0.6 15.0 %collective-permute-start = (bf16[2,16,32,128]{3,2,1,0:T(8,128)(2,1)}, bf16[2,16,32,128]{3,2,1,0:T(8,128)(2,1)S(1)}, u32[]{:S(2)}, u32[]{:S(2)}) collective-permute-start(bf16[2,16,32,128]{3,2,1,0:T(8,128)(2,1)} %bitcast.12), channel_id=1, source_target_pairs={{1,0},{2,1},{3,2},{5,4},{6,5},{7,6},{9,8},{10,9},{11,10},{13,12},{... | collective-permute-start | bytes 786440 | tf_op jit(solution)/shard_map/ppermute | solution.py:403
  1.9 13.7 %copy-start = (bf16[3,128,128]{2,1,0:T(8,128)(2,1)S(1)}, bf16[3,128,128]{2,1,0:T(8,128)(2,1)}, u32[]{:S(2)}) copy-start(bf16[3,128,128]{2,1,0:T(8,128)(2,1)} %weights.3) | copy-start | bytes 294916
  1.9 13.7 %copy-start.1 = (bf16[1,2,16,32,128]{4,3,2,1,0:T(8,128)(2,1)S(1)}, bf16[1,2,16,32,128]{4,3,2,1,0:T(8,128)(2,1)}, u32[]{:S(2)}) copy-start(bf16[1,2,16,32,128]{4,3,2,1,0:T(8,128)(2,1)} %param.11) | copy-start | bytes 786436
  17.0 9.8 %collective-permute-start.1 = (bf16[2,16,32,128]{3,2,1,0:T(8,128)(2,1)S(1)}, bf16[2,16,32,128]{3,2,1,0:T(8,128)(2,1)S(1)}, u32[]{:S(2)}, u32[]{:S(2)}) collective-permute-start(bf16[2,16,32,128]{3,2,1,0:T(8,128)(2,1)S(1)} %get-tuple-element.31.act), channel_id=1, source_target_pairs={{0,1},{1,2},{2,3},{4,5},{5,6},{6,7},{8,9},{9,10},{10,11},{12,13},{... | collective-permute-start | bytes 786440 | tf_op jit(solution)/shard_map/ppermute | solution.py:443
  39.7 4.9 %collective-permute-start.2 = (bf16[104,128]{1,0:T(8,128)(2,1)S(1)}, bf16[104,128]{1,0:T(8,128)(2,1)S(1)}, u32[]{:S(2)}, u32[]{:S(2)}) collective-permute-start(bf16[104,128]{1,0:T(8,128)(2,1)S(1)} %shard_map.104.mine), channel_id=1, source_target_pairs={{0,4},{1,5},{2,6},{3,7},{4,0},{5,1},{6,2},{7,3},{8,12},{9,13},{10,... | collective-permute-start | bytes 79880 | tf_op jit(solution)/shard_map/ppermute | solution.py:462

commit v7 on v6

--- a/solution.py
+++ b/solution.py
@@ -282,9 +282,7 @@
         done += count
 
 
-def grad_kernel(
-    odd, even, normed, pre, sums, temporal, act, act_halo, weights, grads, encoded
-):
+def grad_kernel(odd, even, normed, pre, sums, temporal, grads):
     frames, out_rows, out_cols, channels = normed.shape
     lanes = channels // GROUPS
     members = sums.shape[0] * frames * out_rows * out_cols * lanes
@@ -320,7 +318,6 @@
     extra = split_rows([share[1:2], share[0:1]], EXTRA)
     for chunk in range(grads.shape[0]):
         grads[chunk, pl.ds(rows, EXTRA)] = extra
-    encode(act, act_halo, weights, encoded)
 
 
 def total_of(arrived, first, count):
@@ -348,26 +345,34 @@
     grad_shift[...] = sums[0][1] + sums[1][1]
 
 
-def final_kernel(arrived, grad_spatial, grad_temporal):
-    rows = grad_spatial.shape[0]
-    grad_spatial[...] = arrived[pl.ds(0, rows)].astype(jnp.float32)
-    grad_temporal[...] = arrived[pl.ds(rows, grad_temporal.shape[0])].astype(jnp.float32)
-
-
-def encode(act, halo, weights, encoded):
+def near_encode_kernel(act, weights, part):
     frames, out_rows, out_cols, channels = act.shape
     flat = (STEP_ROWS * out_cols, channels)
     for frame in range(frames):
 
         def one(step, frame=frame):
             rows = pl.ds(step * STEP_ROWS, STEP_ROWS)
-            total = None
-            for tap in range(3):
-                source = (
-                    act[frame - tap, rows] if frame >= tap else halo[frames + frame - tap, rows]
-                )
-                term = dot(source.reshape(flat), weights[tap])
-                total = term if total is None else total + term
+            total = dot(act[frame, rows].reshape(flat), weights[0])
+            for tap in range(1, min(frame, 2) + 1):
+                total += dot(act[frame - tap, rows].reshape(flat), weights[tap])
+            part[frame, rows] = total.reshape(part[frame, rows].shape)
+
+        each(out_rows // STEP_ROWS, one)
+
+
+def final_kernel(arrived, part, halo, weights, grad_spatial, grad_temporal, encoded):
+    count = grad_spatial.shape[0]
+    grad_spatial[...] = arrived[pl.ds(0, count)].astype(jnp.float32)
+    grad_temporal[...] = arrived[pl.ds(count, grad_temporal.shape[0])].astype(jnp.float32)
+    frames, out_rows, out_cols, channels = halo.shape
+    flat = (STEP_ROWS * out_cols, channels)
+    for frame in range(frames):
+
+        def one(step, frame=frame):
+            rows = pl.ds(step * STEP_ROWS, STEP_ROWS)
+            total = part[frame, rows].reshape(flat)
+            for tap in range(frame + 1, 3):
+                total += dot(halo[frames + frame - tap, rows].reshape(flat), weights[tap])
             encoded[frame, rows] = total.astype(jnp.bfloat16).reshape(
                 STEP_ROWS, out_cols, channels
             )
@@ -440,7 +445,6 @@
         (spatial, stats, cot, cot_halo, w_temporal, params),
         flops=2 * positions * 3 * channels * channels,
     )
-    act_halo = lax.ppermute(act, "seq", ahead_pairs)
     sums = exchange(own, "seq", clips)
     halves = 2 if seq_size % 2 == 0 else 1
     half = seq_size // halves
@@ -450,11 +454,11 @@
     ]
     count = dp_size * half
     rows = -(-12 * channels // (16 * count)) * 16
-    grads, encoded = call(
+    grads = call(
         grad_kernel,
-        (struct((count, rows + EXTRA, channels), bf16), struct(shape, bf16)),
-        (odd, even, normed, pre, sums, temporal, act, act_halo, w_temporal),
-        flops=2 * positions * 12 * channels * channels,
+        struct((count, rows + EXTRA, channels), bf16),
+        (odd, even, normed, pre, sums, temporal),
+        flops=2 * positions * 9 * channels * channels,
     )
     grads = exchange(grads, ("dp", "seq"), near)
     mine = call(half_kernel, struct((rows + EXTRA, channels), bf16), (grads,))
@@ -462,6 +466,16 @@
         other = lax.ppermute(mine, "seq", [(s, (s + half) % seq_size) for s in range(seq_size)])
     else:
         other = jnp.zeros_like(mine)
+    act, _ = lax.optimization_barrier((act, mine))
+    part = call(
+        near_encode_kernel,
+        struct(shape, f32),
+        (act, w_temporal),
+        flops=2 * positions * 2 * channels * channels,
+    )
+    act, part = lax.optimization_barrier((act, part))
+    act_halo = lax.ppermute(act, "seq", ahead_pairs)
+    other, part = lax.optimization_barrier((other, part))
     grads, grad_gain, grad_shift = call(
         sum_kernel,
         (
@@ -472,10 +486,15 @@
         (mine, other),
     )
     grads = exchange(grads, ("dp", "seq"), near)
-    grad_spatial, grad_temporal = call(
+    grad_spatial, grad_temporal, encoded = call(
         final_kernel,
-        (struct((9 * channels, channels), f32), struct((3 * channels, channels), f32)),
-        (grads.reshape(count * rows, channels),),
+        (
+            struct((9 * channels, channels), f32),
+            struct((3 * channels, channels), f32),
+            struct(shape, bf16),
+        ),
+        (grads.reshape(count * rows, channels), part, act_halo, w_temporal),
+        flops=2 * positions * 2 * channels * channels,
     )
     return (
         encoded[None],

time: 57.3 us -> 58.3 us (1.017)
  blocking collectives: 40.1 us -> 29 us
  waiting for transfers between devices: 2.27 us -> 9.55 us
  starting transfers between devices: 6.47 us -> 11.2 us
    all_to_all x4 -> x3, blocking collectives: 40.1 us -> 29 us  [exchange(): lax.all_to_all(value, axes, 0, 0, axis_index_groups=groups, tiled=True)]
    ppermute x1, waiting for transfers between devices: 0.01 us -> 7.54 us  [on_device(): act_halo = lax.ppermute(act, 'seq', ahead_pairs)]
    all_to_all x0 -> x1, starting transfers between devices: none -> 3.55 us  [exchange(): lax.all_to_all(value, axes, 0, 0, axis_index_groups=groups, tiled=True)]
    ppermute x1, starting transfers between devices: 2.53 us -> 3.71 us  [on_device(): act_halo = lax.ppermute(act, 'seq', ahead_pairs)]
    pallas_call x6 -> x7, Pallas kernels: 7.49 us -> 7.38 us  [call(): pl.pallas_call(kernel, out_shape=out_shape, in_specs=specs or [WHOLE] * l...]
  transfers between devices with their start and end apart: 3 -> 4, of which waited for: 1 -> 2; matrix products, arithmetic and copies ran while one was open for 0% -> 0% of each run, Pallas kernels for 5% -> 5%
where the time goes in v7:
time: 58.3 us; the launch traced here: 57.9 us
  blocking collectives  29 us (50%)
  starting transfers between devices  11.2 us (19%)
  waiting for transfers between devices  9.55 us (16%)
  Pallas kernels  7.38 us (13%)
  between operations  0.71 us (1%)
    all_to_all x3, blocking collectives, exchange(): lax.all_to_all(value, axes, 0, 0, axis_index_groups=groups, tiled=True)  29 us
    ppermute x1, waiting for transfers between devices, on_device(): act_halo = lax.ppermute(act, 'seq', ahead_pairs)  7.54 us
    pallas_call x7, Pallas kernels, call(): pl.pallas_call(kernel, out_shape=out_shape, in_specs=specs or [WHOLE] * l...  7.38 us
    ppermute x1, starting transfers between devices, on_device(): act_halo = lax.ppermute(act, 'seq', ahead_pairs)  3.71 us
    all_to_all x1, starting transfers between devices, exchange(): lax.all_to_all(value, axes, 0, 0, axis_index_groups=groups, tiled=True)  3.55 us
    ppermute x1, starting transfers between devices, on_device(): lax.ppermute(mine, 'seq', [(s, (s + half) % seq_size) for s in range(seq_...  2.65 us
    ppermute x1, waiting for transfers between devices, on_device(): lax.ppermute(mine, 'seq', [(s, (s + half) % seq_size) for s in range(seq_...  2.01 us
    ppermute x1, starting transfers between devices, on_device(): cot_halo = lax.ppermute(cot, 'seq', back_pairs)  1.29 us
  transfers between devices with their start and end apart: 4, of which 2 were waited for; matrix products, arithmetic and copies ran while one was open for 0% of the time, Pallas kernels for 5%

profile of v7, /device:TPU:0, one launch (start us, length us, event | category | flops | bytes accessed | tf_op | source)
XLA Modules:
  0.0 57.9 jit_solution(2393080184429706503)
XLA Ops:
  0.6 1.3 %collective-permute-start = (bf16[2,16,32,128]{3,2,1,0:T(8,128)(2,1)}, bf16[2,16,32,128]{3,2,1,0:T(8,128)(2,1)S(1)}, u32[]{:S(2)}, u32[]{:S(2)}) collective-permute-start(bf16[2,16,32,128]{3,2,1,0:T(8,128)(2,1)} %bitcast.12), channel_id=1, source_target_pairs={{1,0},{2,1},{3,2},{5,4},{6,5},{7,6},{9,8},{10,9},{11,10},{13,12},{... | collective-permute-start | bytes 786440 | tf_op jit(solution)/shard_map/ppermute | solution.py:408
  1.9 0.0 copy-start
  1.9 0.0 copy-start.1
  2.0 2.8 %shard_map.101 = (f32[2,16,32,128]{3,2,1,0:T(8,128)S(1)}, f32[4,8,128]{2,1,0:T(8,128)S(1)}, bf16[2,17,32,384]{3,2,1,0:T(8,128)(2,1)S(1)}, bf16[2,16,32,384]{3,2,1,0:T(8,128)(2,1)S(1)}, f32[8,128]{1,0:T(8,128)S(1)}) custom-call(bf16[2,32,64,128]{3,2,1,0:T(8,128)(2,1)} %bitcast.14, bf16[3,384,128]{2,1,0:T(8,128)(2,1)} %bitcast.15, f32[1,128]{1,0:T(1,128)} %bitcast.16, ...), custom_call_target="tpu_custom_call" | custom-call | flops 301989888 | bytes 3511296 | tf_op jit(solution)/shard_map/pallas_call | solution.py:43
  4.7 10.9 %all_to_all.20.stats = f32[4,8,128]{2,1,0:T(8,128)S(1)} all-to-all(f32[4,8,128]{2,1,0:T(8,128)S(1)} %get-tuple-element.29), channel_id=1, replica_groups={{0,1,2,3},{4,5,6,7},{8,9,10,11},{12,13,14,15},{16,17,18,19},{20,21,22,2..., dimensions={0} | all-to-all | bytes 32768 | tf_op jit(solution)/shard_map/all_to_all | solution.py:403
  15.6 0.0 collective-permute-done.halo
  15.6 0.0 copy-done
  15.6 0.0 copy-done.1
  15.6 1.4 %shard_map.102 = (bf16[2,16,32,128]{3,2,1,0:T(8,128)(2,1)S(1)}, f32[2,16,32,128]{3,2,1,0:T(8,128)S(1)}, f32[2,16,32,128]{3,2,1,0:T(8,128)S(1)}, bf16[384,128]{1,0:T(8,128)(2,1)S(1)}, f32[4,8,128]{2,1,0:T(8,128)S(1)}) custom-call(f32[2,16,32,128]{3,2,1,0:T(8,128)S(1)} %get-tuple-element.28.spatial, f32[4,8,128]{2,1,0:T(8,128)S(1)} %all_to_all.20.stats, ...), custom_call_target="tpu_custom_call" | custom-call | flops 100663296 | bytes 2592768 | tf_op jit(solution)/shard_map/pallas_call | solution.py:43
  17.0 7.1 %all_to_all.21.sums = f32[4,8,128]{2,1,0:T(8,128)S(1)} all-to-all(f32[4,8,128]{2,1,0:T(8,128)S(1)} %get-tuple-element.33), channel_id=1, replica_groups={{0,1,2,3},{4,5,6,7},{8,9,10,11},{12,13,14,15},{16,17,18,19},{20,21,22,2..., dimensions={0} | all-to-all | bytes 32768 | tf_op jit(solution)/shard_map/all_to_all | solution.py:403
  24.1 1.0 %shard_map.103 = bf16[16,104,128]{2,1,0:T(8,128)(2,1)S(1)} custom-call(bf16[2,17,32,384]{3,2,1,0:T(8,128)(2,1)S(1)} %get-tuple-element.26.odd, bf16[2,16,32,384]{3,2,1,0:T(8,128)(2,1)S(1)} %get-tuple-element.27.even, f32[2,16,32,128]{3,2,1,0:T(8,128)S(1)} %get-tuple-element.31.normed, f32[2,16,32,128]{3,2,1,0:T(8,128)S(1)} %get-tuple-element.32.pre, ...), custom_call_target="tpu_custom_call" | custom-call | flops 301989888 | bytes 3211264 | tf_op jit(solution)/shard_map/pallas_call | solution.py:43
  25.1 11.0 %all_to_all.22.arrived = bf16[16,104,128]{2,1,0:T(8,128)(2,1)S(1)} all-to-all(bf16[16,104,128]{2,1,0:T(8,128)(2,1)S(1)} %shard_map.103), channel_id=1, replica_groups={{0,1,2,3,8,9,10,11,16,17,18,19,24,25,26,27},{4,5,6,7,12,13,14,15,20,21,..., dimensions={0} | all-to-all | bytes 851968 | tf_op jit(solution)/shard_map/all_to_all | solution.py:403
  36.1 0.1 shard_map.104.mine
  36.2 2.7 %collective-permute-start.1 = (bf16[104,128]{1,0:T(8,128)(2,1)S(1)}, bf16[104,128]{1,0:T(8,128)(2,1)S(1)}, u32[]{:S(2)}, u32[]{:S(2)}) collective-permute-start(bf16[104,128]{1,0:T(8,128)(2,1)S(1)} %shard_map.104.mine), channel_id=1, source_target_pairs={{0,4},{1,5},{2,6},{3,7},{4,0},{5,1},{6,2},{7,3},{8,12},{9,13},{10,... | collective-permute-start | bytes 79880 | tf_op jit(solution)/shard_map/ppermute | solution.py:466
  38.8 0.2 shard_map.105.part
  39.1 2.0 %collective-permute-done.1.other = bf16[104,128]{1,0:T(8,128)(2,1)S(1)} collective-permute-done((bf16[104,128]{1,0:T(8,128)(2,1)S(1)}, bf16[104,128]{1,0:T(8,128)(2,1)S(1)}, u32[]{:S(2)}, u32[]{:S(2)}) %collective-permute-start.1) | collective-permute-done | bytes 26656 | tf_op jit(solution)/shard_map/ppermute | solution.py:466
  41.1 0.8 %shard_map.106 = (bf16[16,96,128]{2,1,0:T(8,128)(2,1)}, f32[1,128]{1,0:T(1,128)}, f32[1,128]{1,0:T(1,128)}) custom-call(bf16[104,128]{1,0:T(8,128)(2,1)S(1)} %shard_map.104.mine, bf16[104,128]{1,0:T(8,128)(2,1)S(1)} %collective-permute-done.1.other), custom_call_target="tpu_custom_call" | custom-call | bytes 447488 | tf_op jit(solution)/shard_map/pallas_call | solution.py:43
  41.9 3.6 %all-to-all-start.3 = ((bf16[16,96,128]{2,1,0:T(8,128)(2,1)}), bf16[16,96,128]{2,1,0:T(8,128)(2,1)S(1)}, u32[]{:S(2)}, u32[]{:S(2)}) async-start(bf16[16,96,128]{2,1,0:T(8,128)(2,1)} %get-tuple-element.39), calls=%async_computation.3 | async-start | bytes 786432 | tf_op jit(solution)/shard_map/all_to_all | solution.py:403
  45.4 3.7 %collective-permute-start.2 = (bf16[2,16,32,128]{3,2,1,0:T(8,128)(2,1)S(1)}, bf16[2,16,32,128]{3,2,1,0:T(8,128)(2,1)S(1)}, u32[]{:S(2)}, u32[]{:S(2)}) collective-permute-start(bf16[2,16,32,128]{3,2,1,0:T(8,128)(2,1)S(1)} %get-tuple-element.41.act), channel_id=1, source_target_pairs={{0,1},{1,2},{2,3},{4,5},{5,6},{6,7},{8,9},{9,10},{10,11},{12,13},{... | collective-permute-start | bytes 786440 | tf_op jit(solution)/shard_map/ppermute | solution.py:477
  49.2 7.5 %collective-permute-done.2.halo = bf16[2,16,32,128]{3,2,1,0:T(8,128)(2,1)S(1)} collective-permute-done((bf16[2,16,32,128]{3,2,1,0:T(8,128)(2,1)S(1)}, bf16[2,16,32,128]{3,2,1,0:T(8,128)(2,1)S(1)}, u32[]{:S(2)}, u32[]{:S(2)}) %collective-permute-start.2) | collective-permute-done | bytes 262176 | tf_op jit(solution)/shard_map/ppermute | solution.py:477
  56.7 0.0 all-to-all-done.3
  56.7 1.1 %shard_map.107 = (f32[1152,128]{1,0:T(8,128)}, f32[384,128]{1,0:T(8,128)}, bf16[2,16,32,128]{3,2,1,0:T(8,128)(2,1)}) custom-call(bf16[1536,128]{1,0:T(8,128)(2,1)S(1)} %bitcast.11, f32[2,16,32,128]{3,2,1,0:T(8,128)S(1)} %shard_map.105.part, bf16[2,16,32,128]{3,2,1,0:T(8,128)(2,1)S(1)} %collective-permute-done.2.halo, bf16[3,128,128]{2,1,0:T(8,128)(2,1)S(1)} %copy-done), custom_call_target="tpu_custom_call" | custom-call | flops 67108864 | bytes 2326528 | tf_op jit(solution)/shard_map/pallas_call | solution.py:43
Async XLA Ops:
  0.6 15.0 %collective-permute-start = (bf16[2,16,32,128]{3,2,1,0:T(8,128)(2,1)}, bf16[2,16,32,128]{3,2,1,0:T(8,128)(2,1)S(1)}, u32[]{:S(2)}, u32[]{:S(2)}) collective-permute-start(bf16[2,16,32,128]{3,2,1,0:T(8,128)(2,1)} %bitcast.12), channel_id=1, source_target_pairs={{1,0},{2,1},{3,2},{5,4},{6,5},{7,6},{9,8},{10,9},{11,10},{13,12},{... | collective-permute-start | bytes 786440 | tf_op jit(solution)/shard_map/ppermute | solution.py:408
  1.9 13.7 %copy-start = (bf16[3,128,128]{2,1,0:T(8,128)(2,1)S(1)}, bf16[3,128,128]{2,1,0:T(8,128)(2,1)}, u32[]{:S(2)}) copy-start(bf16[3,128,128]{2,1,0:T(8,128)(2,1)} %weights.5) | copy-start | bytes 294916
  1.9 13.7 %copy-start.1 = (bf16[1,2,16,32,128]{4,3,2,1,0:T(8,128)(2,1)S(1)}, bf16[1,2,16,32,128]{4,3,2,1,0:T(8,128)(2,1)}, u32[]{:S(2)}) copy-start(bf16[1,2,16,32,128]{4,3,2,1,0:T(8,128)(2,1)} %param.11) | copy-start | bytes 786436
  36.2 4.9 %collective-permute-start.1 = (bf16[104,128]{1,0:T(8,128)(2,1)S(1)}, bf16[104,128]{1,0:T(8,128)(2,1)S(1)}, u32[]{:S(2)}, u32[]{:S(2)}) collective-permute-start(bf16[104,128]{1,0:T(8,128)(2,1)S(1)} %shard_map.104.mine), channel_id=1, source_target_pairs={{0,4},{1,5},{2,6},{3,7},{4,0},{5,1},{6,2},{7,3},{8,12},{9,13},{10,... | collective-permute-start | bytes 79880 | tf_op jit(solution)/shard_map/ppermute | solution.py:466
  41.9 14.8 %all-to-all-start.3 = ((bf16[16,96,128]{2,1,0:T(8,128)(2,1)}), bf16[16,96,128]{2,1,0:T(8,128)(2,1)S(1)}, u32[]{:S(2)}, u32[]{:S(2)}) async-start(bf16[16,96,128]{2,1,0:T(8,128)(2,1)} %get-tuple-element.39), calls=%async_computation.3 | async-start | bytes 786432 | tf_op jit(solution)/shard_map/all_to_all | solution.py:403
  45.4 11.3 %collective-permute-start.2 = (bf16[2,16,32,128]{3,2,1,0:T(8,128)(2,1)S(1)}, bf16[2,16,32,128]{3,2,1,0:T(8,128)(2,1)S(1)}, u32[]{:S(2)}, u32[]{:S(2)}) collective-permute-start(bf16[2,16,32,128]{3,2,1,0:T(8,128)(2,1)S(1)} %get-tuple-element.41.act), channel_id=1, source_target_pairs={{0,1},{1,2},{2,3},{4,5},{5,6},{6,7},{8,9},{9,10},{10,11},{12,13},{... | collective-permute-start | bytes 786440 | tf_op jit(solution)/shard_map/ppermute | solution.py:477

commit v8 on v6

--- a/solution.py
+++ b/solution.py
@@ -14,6 +14,7 @@
 EXTRA = 8
 SPARE_BYTES = 4 * 1024 * 1024
 
+SCALAR = pl.BlockSpec(memory_space=pltpu.SMEM)
 WHOLE = pl.BlockSpec(memory_space=pltpu.VMEM)
 FAR = pl.BlockSpec(memory_space=pltpu.HBM)
 
@@ -183,12 +184,16 @@
 
 
 def act_kernel(
-    loss_scale, spatial, stats, cot, halo, weights, params, act, normed, pre, temporal, sums
+    loss_scale, keep, spatial, stats, cot, arrived, weights, params, act, normed, pre, temporal,
+    sums, halo,
 ):
     frames, out_rows, out_cols, channels = spatial.shape
     positions = frames * out_rows * out_cols
     mean, inv_std = clip_norm(stats, positions, channels // GROUPS)
     gain, shift = params[0:1], params[1:2]
+    for frame in range(2):
+        value = arrived[frame]
+        halo[frame] = jnp.where(keep[0] != 0, value, jnp.zeros_like(value))
     flat = (STEP_ROWS * out_cols, channels)
     shaped = (STEP_ROWS, out_cols, channels)
     sums_shift = jnp.zeros((8, channels), jnp.float32)
@@ -283,7 +288,7 @@
 
 
 def grad_kernel(
-    odd, even, normed, pre, sums, temporal, act, act_halo, weights, grads, encoded
+    odd, even, normed, pre, sums, temporal, grads
 ):
     frames, out_rows, out_cols, channels = normed.shape
     lanes = channels // GROUPS
@@ -320,7 +325,6 @@
     extra = split_rows([share[1:2], share[0:1]], EXTRA)
     for chunk in range(grads.shape[0]):
         grads[chunk, pl.ds(rows, EXTRA)] = extra
-    encode(act, act_halo, weights, encoded)
 
 
 def total_of(arrived, first, count):
@@ -354,7 +358,7 @@
     grad_temporal[...] = arrived[pl.ds(rows, grad_temporal.shape[0])].astype(jnp.float32)
 
 
-def encode(act, halo, weights, encoded):
+def encode_kernel(keep, act, halo, weights, encoded):
     frames, out_rows, out_cols, channels = act.shape
     flat = (STEP_ROWS * out_cols, channels)
     for frame in range(frames):
@@ -363,9 +367,11 @@
             rows = pl.ds(step * STEP_ROWS, STEP_ROWS)
             total = None
             for tap in range(3):
-                source = (
-                    act[frame - tap, rows] if frame >= tap else halo[frames + frame - tap, rows]
-                )
+                if frame >= tap:
+                    source = act[frame - tap, rows]
+                else:
+                    source = halo[frames + frame - tap, rows]
+                    source = jnp.where(keep[0] != 0, source, jnp.zeros_like(source))
                 term = dot(source.reshape(flat), weights[tap])
                 total = term if total is None else total + term
             encoded[frame, rows] = total.astype(jnp.bfloat16).reshape(
@@ -390,8 +396,13 @@
     f32, bf16 = jnp.float32, jnp.bfloat16
     struct = jax.ShapeDtypeStruct
 
-    back_pairs = [(s, s - 1) for s in range(seq_size) if s % per_clip]
-    ahead_pairs = [(s - 1, s) for s in range(seq_size) if s % per_clip]
+    ahead_pairs = [
+        (s, s // per_clip * per_clip + (s + 1) % per_clip) for s in range(seq_size)
+    ]
+    back_pairs = [(target, source) for source, target in ahead_pairs]
+    member = lax.axis_index("seq") % per_clip
+    not_first = (member != 0).astype(jnp.int32)[None]
+    not_last = (member != per_clip - 1).astype(jnp.int32)[None]
     clips = [list(range(first, first + per_clip)) for first in range(0, seq_size, per_clip)]
 
     def exchange(value, axes, groups=None):
@@ -437,7 +448,9 @@
             struct((3 * channels, channels), bf16),
             struct((per_clip, 8, channels), f32),
         ),
-        (spatial, stats, cot, cot_halo, w_temporal, params),
+        (not_last, spatial, stats, cot, cot_halo, w_temporal, params),
+        specs=[SCALAR] + [WHOLE] * 6,
+        scratch=[pltpu.VMEM((2,) + shape[1:], bf16)],
         flops=2 * positions * 3 * channels * channels,
     )
     act_halo = lax.ppermute(act, "seq", ahead_pairs)
@@ -450,11 +463,12 @@
     ]
     count = dp_size * half
     rows = -(-12 * channels // (16 * count)) * 16
-    grads, encoded = call(
+    sums, act_halo = lax.optimization_barrier((sums, act_halo))
+    grads = call(
         grad_kernel,
-        (struct((count, rows + EXTRA, channels), bf16), struct(shape, bf16)),
-        (odd, even, normed, pre, sums, temporal, act, act_halo, w_temporal),
-        flops=2 * positions * 12 * channels * channels,
+        struct((count, rows + EXTRA, channels), bf16),
+        (odd, even, normed, pre, sums, temporal),
+        flops=2 * positions * 9 * channels * channels,
     )
     grads = exchange(grads, ("dp", "seq"), near)
     mine = call(half_kernel, struct((rows + EXTRA, channels), bf16), (grads,))
@@ -462,6 +476,15 @@
         other = lax.ppermute(mine, "seq", [(s, (s + half) % seq_size) for s in range(seq_size)])
     else:
         other = jnp.zeros_like(mine)
+    act, act_halo, _ = lax.optimization_barrier((act, act_halo, mine))
+    encoded = call(
+        encode_kernel,
+        struct(shape, bf16),
+        (not_first, act, act_halo, w_temporal),
+        specs=[SCALAR] + [WHOLE] * 3,
+        flops=2 * positions * 3 * channels * channels,
+    )
+    other, encoded = lax.optimization_barrier((other, encoded))
     grads, grad_gain, grad_shift = call(
         sum_kernel,
         (

time: 57.3 us -> 55.8 us (0.974)
  blocking collectives: 40.1 us -> 30.1 us
  starting transfers between devices: 6.47 us -> 10.6 us
  waiting for transfers between devices: 2.27 us -> 5.89 us
  Pallas kernels: 7.49 us -> 8.25 us
    all_to_all x4 -> x3, blocking collectives: 40.1 us -> 30.1 us  [exchange(): lax.all_to_all(value, axes, 0, 0, axis_index_groups=groups, tiled=True)]
    all_to_all x0 -> x1, waiting for transfers between devices: none -> 4.67 us  [exchange(): lax.all_to_all(value, axes, 0, 0, axis_index_groups=groups, tiled=True)]
    all_to_all x0 -> x1, starting transfers between devices: none -> 3.27 us  [exchange(): lax.all_to_all(value, axes, 0, 0, axis_index_groups=groups, tiled=True)]
    ppermute x1, starting transfers between devices: 1.29 us -> 4 us  [on_device(): cot_halo = lax.ppermute(cot, 'seq', back_pairs)]
    ppermute x1, starting transfers between devices: 2.53 us -> 0.66 us  [on_device(): act_halo = lax.ppermute(act, 'seq', ahead_pairs)]
    ppermute x1, waiting for transfers between devices: 2.26 us -> 1.22 us  [on_device(): lax.ppermute(mine, 'seq', [(s, (s + half) % seq_size) for s in range(seq_...]
    pallas_call x6 -> x7, Pallas kernels: 7.49 us -> 8.25 us  [call(): pl.pallas_call(kernel, out_shape=out_shape, in_specs=specs or [WHOLE] * l...]
  transfers between devices with their start and end apart: 3 -> 4, of which waited for: 1 -> 2; matrix products, arithmetic and copies ran while one was open for 0% -> 0% of each run, Pallas kernels for 5% -> 8%
where the time goes in v8:
time: 55.8 us; the launch traced here: 55.5 us
  blocking collectives  30.1 us (54%)
  starting transfers between devices  10.6 us (19%)
  Pallas kernels  8.25 us (15%)
  waiting for transfers between devices  5.89 us (11%)
  between operations  0.69 us (1%)
    all_to_all x3, blocking collectives, exchange(): lax.all_to_all(value, axes, 0, 0, axis_index_groups=groups, tiled=True)  30.1 us
    pallas_call x7, Pallas kernels, call(): pl.pallas_call(kernel, out_shape=out_shape, in_specs=specs or [WHOLE] * l...  8.25 us
    all_to_all x1, waiting for transfers between devices, exchange(): lax.all_to_all(value, axes, 0, 0, axis_index_groups=groups, tiled=True)  4.67 us
    ppermute x1, starting transfers between devices, on_device(): cot_halo = lax.ppermute(cot, 'seq', back_pairs)  4 us
    all_to_all x1, starting transfers between devices, exchange(): lax.all_to_all(value, axes, 0, 0, axis_index_groups=groups, tiled=True)  3.27 us
    ppermute x1, starting transfers between devices, on_device(): lax.ppermute(mine, 'seq', [(s, (s + half) % seq_size) for s in range(seq_...  2.63 us
    ppermute x1, waiting for transfers between devices, on_device(): lax.ppermute(mine, 'seq', [(s, (s + half) % seq_size) for s in range(seq_...  1.22 us
  transfers between devices with their start and end apart: 4, of which 2 were waited for; matrix products, arithmetic and copies ran while one was open for 0% of the time, Pallas kernels for 8%

profile of v8, /device:TPU:0, one launch (start us, length us, event | category | flops | bytes accessed | tf_op | source)
XLA Modules:
  0.0 55.5 jit_solution(1022284760009822214)
XLA Ops:
  0.6 4.0 %collective-permute-start = (bf16[2,16,32,128]{3,2,1,0:T(8,128)(2,1)}, bf16[2,16,32,128]{3,2,1,0:T(8,128)(2,1)S(1)}, u32[]{:S(2)}, u32[]{:S(2)}) collective-permute-start(bf16[2,16,32,128]{3,2,1,0:T(8,128)(2,1)} %bitcast.14), channel_id=1, source_target_pairs={{1,0},{2,1},{3,2},{0,3},{5,4},{6,5},{7,6},{4,7},{9,8},{10,9},{11,1... | collective-permute-start | bytes 786440 | tf_op jit(solution)/shard_map/ppermute | solution.py:414
  4.6 0.0 copy-start
  4.6 0.0 copy-start.1
  4.6 3.3 %shard_map.101 = (f32[2,16,32,128]{3,2,1,0:T(8,128)S(1)}, f32[4,8,128]{2,1,0:T(8,128)}, bf16[2,17,32,384]{3,2,1,0:T(8,128)(2,1)S(1)}, bf16[2,16,32,384]{3,2,1,0:T(8,128)(2,1)S(1)}, f32[8,128]{1,0:T(8,128)S(1)}) custom-call(bf16[2,32,64,128]{3,2,1,0:T(8,128)(2,1)} %bitcast.16, bf16[3,384,128]{2,1,0:T(8,128)(2,1)} %bitcast.17, f32[1,128]{1,0:T(1,128)} %bitcast.19, ...), custom_call_target="tpu_custom_call" | custom-call | flops 301989888 | bytes 3511296 | tf_op jit(solution)/shard_map/pallas_call | solution.py:44
  8.0 3.3 %all-to-all-start = ((f32[4,8,128]{2,1,0:T(8,128)}), f32[4,8,128]{2,1,0:T(8,128)S(1)}, u32[]{:S(2)}, u32[]{:S(2)}) async-start(f32[4,8,128]{2,1,0:T(8,128)} %get-tuple-element.29), calls=%async_computation | async-start | bytes 32768 | tf_op jit(solution)/shard_map/all_to_all | solution.py:409
  11.3 4.7 %all-to-all-done.stats = f32[4,8,128]{2,1,0:T(8,128)S(1)} async-done(((f32[4,8,128]{2,1,0:T(8,128)}), f32[4,8,128]{2,1,0:T(8,128)S(1)}, u32[]{:S(2)}, u32[]{:S(2)}) %all-to-all-start) | async-done | bytes 16416 | tf_op jit(solution)/shard_map/all_to_all | solution.py:409
  15.9 0.0 collective-permute-done.arrived
  16.0 0.0 copy-done
  16.0 0.0 copy-done.1
  16.0 1.4 %shard_map.102 = (bf16[2,16,32,128]{3,2,1,0:T(8,128)(2,1)S(1)}, f32[2,16,32,128]{3,2,1,0:T(8,128)S(1)}, f32[2,16,32,128]{3,2,1,0:T(8,128)S(1)}, bf16[384,128]{1,0:T(8,128)(2,1)S(1)}, f32[4,8,128]{2,1,0:T(8,128)S(1)}) custom-call(s32[1]{0:T(128)} %bitcast.4.keep, f32[2,16,32,128]{3,2,1,0:T(8,128)S(1)} %get-tuple-element.28.spatial, ...), custom_call_target="tpu_custom_call" | custom-call | flops 100663296 | bytes 2592772 | tf_op jit(solution)/shard_map/pallas_call | solution.py:44
  17.3 0.7 %collective-permute-start.1 = (bf16[2,16,32,128]{3,2,1,0:T(8,128)(2,1)S(1)}, bf16[2,16,32,128]{3,2,1,0:T(8,128)(2,1)S(1)}, u32[]{:S(2)}, u32[]{:S(2)}) collective-permute-start(bf16[2,16,32,128]{3,2,1,0:T(8,128)(2,1)S(1)} %get-tuple-element.38.act), channel_id=1, source_target_pairs={{0,1},{1,2},{2,3},{3,0},{4,5},{5,6},{6,7},{7,4},{8,9},{9,10},{10,1... | collective-permute-start | bytes 786440 | tf_op jit(solution)/shard_map/ppermute | solution.py:456
  18.0 8.1 %all_to_all.20.sums = f32[4,8,128]{2,1,0:T(8,128)S(1)} all-to-all(f32[4,8,128]{2,1,0:T(8,128)S(1)} %get-tuple-element.33), channel_id=1, replica_groups={{0,1,2,3},{4,5,6,7},{8,9,10,11},{12,13,14,15},{16,17,18,19},{20,21,22,2..., dimensions={0} | all-to-all | bytes 32768 | tf_op jit(solution)/shard_map/all_to_all | solution.py:409
  26.1 0.0 collective-permute-done.1.halo
  26.1 1.0 %shard_map.103 = bf16[16,104,128]{2,1,0:T(8,128)(2,1)S(1)} custom-call(bf16[2,17,32,384]{3,2,1,0:T(8,128)(2,1)S(1)} %get-tuple-element.26.odd, bf16[2,16,32,384]{3,2,1,0:T(8,128)(2,1)S(1)} %get-tuple-element.27.even, f32[2,16,32,128]{3,2,1,0:T(8,128)S(1)} %get-tuple-element.31.normed, f32[2,16,32,128]{3,2,1,0:T(8,128)S(1)} %get-tuple-element.32.pre, ...), custom_call_target="tpu_custom_call" | custom-call | flops 301989888 | bytes 3211264 | tf_op jit(solution)/shard_map/pallas_call | solution.py:44
  27.1 11.1 %all_to_all.21.arrived = bf16[16,104,128]{2,1,0:T(8,128)(2,1)S(1)} all-to-all(bf16[16,104,128]{2,1,0:T(8,128)(2,1)S(1)} %shard_map.103), channel_id=1, replica_groups={{0,1,2,3,8,9,10,11,16,17,18,19,24,25,26,27},{4,5,6,7,12,13,14,15,20,21,..., dimensions={0} | all-to-all | bytes 851968 | tf_op jit(solution)/shard_map/all_to_all | solution.py:409
  38.1 0.1 shard_map.104.mine
  38.2 2.6 %collective-permute-start.2 = (bf16[104,128]{1,0:T(8,128)(2,1)S(1)}, bf16[104,128]{1,0:T(8,128)(2,1)S(1)}, u32[]{:S(2)}, u32[]{:S(2)}) collective-permute-start(bf16[104,128]{1,0:T(8,128)(2,1)S(1)} %shard_map.104.mine), channel_id=1, source_target_pairs={{0,4},{1,5},{2,6},{3,7},{4,0},{5,1},{6,2},{7,3},{8,12},{9,13},{10,... | collective-permute-start | bytes 79880 | tf_op jit(solution)/shard_map/ppermute | solution.py:476
  40.8 1.1 %shard_map.105 = bf16[2,16,32,128]{3,2,1,0:T(8,128)(2,1)} custom-call(s32[1]{0:T(128)} %bitcast.6.keep, bf16[2,16,32,128]{3,2,1,0:T(8,128)(2,1)S(1)} %get-tuple-element.38.act, bf16[2,16,32,128]{3,2,1,0:T(8,128)(2,1)S(1)} %collective-permute-done.1.halo, bf16[3,128,128]{2,1,0:T(8,128)(2,1)S(1)} %copy-done), custom_call_target="tpu_custom_call" | custom-call | flops 100663296 | bytes 884740 | tf_op jit(solution)/shard_map/pallas_call | solution.py:44
  41.9 1.2 %collective-permute-done.2.other = bf16[104,128]{1,0:T(8,128)(2,1)S(1)} collective-permute-done((bf16[104,128]{1,0:T(8,128)(2,1)S(1)}, bf16[104,128]{1,0:T(8,128)(2,1)S(1)}, u32[]{:S(2)}, u32[]{:S(2)}) %collective-permute-start.2) | collective-permute-done | bytes 26656 | tf_op jit(solution)/shard_map/ppermute | solution.py:476
  43.1 0.5 shard_map.106
  43.6 10.9 %all_to_all.22 = bf16[16,96,128]{2,1,0:T(8,128)(2,1)S(1)} all-to-all(bf16[16,96,128]{2,1,0:T(8,128)(2,1)S(1)} %get-tuple-element.42), channel_id=1, replica_groups={{0,1,2,3,8,9,10,11,16,17,18,19,24,25,26,27},{4,5,6,7,12,13,14,15,20,21,..., dimensions={0} | all-to-all | bytes 786432 | tf_op jit(solution)/shard_map/all_to_all | solution.py:409
  54.5 0.9 %shard_map.107 = (f32[1152,128]{1,0:T(8,128)}, f32[384,128]{1,0:T(8,128)}) custom-call(bf16[1536,128]{1,0:T(8,128)(2,1)S(1)} %bitcast.13), custom_call_target="tpu_custom_call" | custom-call | bytes 1179648 | tf_op jit(solution)/shard_map/pallas_call | solution.py:44
Async XLA Ops:
  0.6 15.3 %collective-permute-start = (bf16[2,16,32,128]{3,2,1,0:T(8,128)(2,1)}, bf16[2,16,32,128]{3,2,1,0:T(8,128)(2,1)S(1)}, u32[]{:S(2)}, u32[]{:S(2)}) collective-permute-start(bf16[2,16,32,128]{3,2,1,0:T(8,128)(2,1)} %bitcast.14), channel_id=1, source_target_pairs={{1,0},{2,1},{3,2},{0,3},{5,4},{6,5},{7,6},{4,7},{9,8},{10,9},{11,1... | collective-permute-start | bytes 786440 | tf_op jit(solution)/shard_map/ppermute | solution.py:414
  4.6 11.3 %copy-start = (bf16[3,128,128]{2,1,0:T(8,128)(2,1)S(1)}, bf16[3,128,128]{2,1,0:T(8,128)(2,1)}, u32[]{:S(2)}) copy-start(bf16[3,128,128]{2,1,0:T(8,128)(2,1)} %weights.3) | copy-start | bytes 294916
  4.6 11.3 %copy-start.1 = (bf16[1,2,16,32,128]{4,3,2,1,0:T(8,128)(2,1)S(1)}, bf16[1,2,16,32,128]{4,3,2,1,0:T(8,128)(2,1)}, u32[]{:S(2)}) copy-start(bf16[1,2,16,32,128]{4,3,2,1,0:T(8,128)(2,1)} %param.11) | copy-start | bytes 786436
  8.0 8.0 %all-to-all-start = ((f32[4,8,128]{2,1,0:T(8,128)}), f32[4,8,128]{2,1,0:T(8,128)S(1)}, u32[]{:S(2)}, u32[]{:S(2)}) async-start(f32[4,8,128]{2,1,0:T(8,128)} %get-tuple-element.29), calls=%async_computation | async-start | bytes 32768 | tf_op jit(solution)/shard_map/all_to_all | solution.py:409
  17.3 8.8 %collective-permute-start.1 = (bf16[2,16,32,128]{3,2,1,0:T(8,128)(2,1)S(1)}, bf16[2,16,32,128]{3,2,1,0:T(8,128)(2,1)S(1)}, u32[]{:S(2)}, u32[]{:S(2)}) collective-permute-start(bf16[2,16,32,128]{3,2,1,0:T(8,128)(2,1)S(1)} %get-tuple-element.38.act), channel_id=1, source_target_pairs={{0,1},{1,2},{2,3},{3,0},{4,5},{5,6},{6,7},{7,4},{8,9},{9,10},{10,1... | collective-permute-start | bytes 786440 | tf_op jit(solution)/shard_map/ppermute | solution.py:456
  38.2 4.9 %collective-permute-start.2 = (bf16[104,128]{1,0:T(8,128)(2,1)S(1)}, bf16[104,128]{1,0:T(8,128)(2,1)S(1)}, u32[]{:S(2)}, u32[]{:S(2)}) collective-permute-start(bf16[104,128]{1,0:T(8,128)(2,1)S(1)} %shard_map.104.mine), channel_id=1, source_target_pairs={{0,4},{1,5},{2,6},{3,7},{4,0},{5,1},{6,2},{7,3},{8,12},{9,13},{10,... | collective-permute-start | bytes 79880 | tf_op jit(solution)/shard_map/ppermute | solution.py:476

commit v9 on v8

--- a/solution.py
+++ b/solution.py
@@ -14,7 +14,6 @@
 EXTRA = 8
 SPARE_BYTES = 4 * 1024 * 1024
 
-SCALAR = pl.BlockSpec(memory_space=pltpu.SMEM)
 WHOLE = pl.BlockSpec(memory_space=pltpu.VMEM)
 FAR = pl.BlockSpec(memory_space=pltpu.HBM)
 
@@ -95,74 +94,81 @@
         copy.start()
     for copy in small[1:]:
         copy.start()
-    for slot in range(2 * STEP_ROWS):
+    for slot in range(wide.shape[0]):
         wide[slot, 0:8] = jnp.zeros((8, channels), jnp.float32)
-
     for frame in range(frames):
         odd[frame, 0] = jnp.zeros((out_cols, 3 * channels), jnp.bfloat16)
+    flat = (STEP_ROWS * out_cols, 3 * channels)
+    steps = half // 2 // STEP_ROWS
+
+    def place(piece, step):
+        return piece * half // height, piece * half % height // 2 + step * STEP_ROWS
+
+    def separate(piece, step):
+        frame, first = place(piece, step)
+        base = piece % 2 * 2 * STEP_ROWS
+        for line in range(2 * STEP_ROWS):
+            wide[base + line, 8 : 8 + width] = video[frame, 2 * first + line].astype(jnp.float32)
+        for line in range(2 * STEP_ROWS):
+            for tap in range(3):
+                value = wide[base + line, pl.ds(7 + tap, out_cols, stride=2), :]
+                lanes = slice(tap * channels, (tap + 1) * channels)
+                if line % 2:
+                    odd[frame, first + line // 2 + 1, :, lanes] = value.astype(jnp.bfloat16)
+                else:
+                    even[frame, first + line // 2, :, lanes] = value.astype(jnp.bfloat16)
+
+    def multiply(piece, step):
+        frame, first = place(piece, step)
+        total = dot(odd[frame, pl.ds(first, STEP_ROWS)].reshape(flat), weights[0])
+        total += dot(even[frame, pl.ds(first, STEP_ROWS)].reshape(flat), weights[1])
+        total += dot(odd[frame, pl.ds(first + 1, STEP_ROWS)].reshape(flat), weights[2])
+        spatial[frame, pl.ds(first, STEP_ROWS)] = total.reshape(STEP_ROWS, out_cols, channels)
+        return total
+
+    def fold(values):
+        return values.reshape(-1, 8, channels).sum(axis=0)
+
+    def over_steps(piece, term, start):
+        if steps <= 8:
+            for step in range(steps):
+                start = jax.tree.map(jnp.add, start, term(piece, step))
+            return start
+        return lax.fori_loop(
+            0, steps, lambda step, sums: jax.tree.map(jnp.add, sums, term(piece, step)), start
+        )
+
+    zero = jnp.zeros((8, channels), jnp.float32)
+
+    def first_sum(piece, step):
+        return fold(multiply(piece, step))
+
+    def first_moments(piece, step):
+        frame, first = place(piece, step)
+        off = spatial[frame, pl.ds(first, STEP_ROWS)].reshape(-1, channels) - near
+        return fold(off), fold(off * off)
+
+    def moments(piece, step):
+        off = multiply(piece, step) - near
+        return fold(off), fold(off * off)
 
     for piece in range(pieces):
-        frame = piece * half // height
-        base = piece * half % height // 2 // STEP_ROWS
         copies[piece].wait()
-
-        def separate(step, frame=frame, base=base):
-            step = base + step
-            for row in range(STEP_ROWS):
-                for parity in range(2):
-                    slot = 2 * row + parity
-                    wide[slot, 8 : 8 + width] = video[
-                        frame, 2 * (step * STEP_ROWS + row) + parity
-                    ].astype(jnp.float32)
-            for row in range(STEP_ROWS):
-                for parity in range(2):
-                    slot = 2 * row + parity
-                    for tap in range(3):
-                        value = wide[slot, pl.ds(7 + tap, out_cols, stride=2), :].astype(
-                            jnp.bfloat16
-                        )
-                        lanes = slice(tap * channels, (tap + 1) * channels)
-                        if parity:
-                            odd[frame, step * STEP_ROWS + row + 1, :, lanes] = value
-                        else:
-                            even[frame, step * STEP_ROWS + row, :, lanes] = value
-
-        each(half // 2 // STEP_ROWS, separate)
+        each(steps, functools.partial(separate, piece))
         if piece == 0:
             small[0].wait()
-
-        def multiply(step, frame=frame, base=base):
-            step = base + step
-            flat = (STEP_ROWS * out_cols, 3 * channels)
-            first = step * STEP_ROWS
-            total = dot(odd[frame, pl.ds(first, STEP_ROWS)].reshape(flat), weights[0])
-            total += dot(even[frame, pl.ds(first, STEP_ROWS)].reshape(flat), weights[1])
-            total += dot(odd[frame, pl.ds(first + 1, STEP_ROWS)].reshape(flat), weights[2])
-            spatial[frame, pl.ds(first, STEP_ROWS)] = total.reshape(STEP_ROWS, out_cols, channels)
-
-        each(half // 2 // STEP_ROWS, multiply)
-
-    steps = positions // (STEP_ROWS * out_cols)
-    per_frame = out_rows // STEP_ROWS
-
-    def block(step):
-        return spatial[step // per_frame, pl.ds((step % per_frame) * STEP_ROWS, STEP_ROWS)]
-
-    def fold(values):
-        return values.reshape(-1, 8, channels).sum(axis=0)
-
-    def fold_all(term):
-        if steps <= 8:
-            total = term(0)
-            for step in range(1, steps):
-                total += term(step)
-            return total
-        return lax.fori_loop(
-            0, steps, lambda step, total: total + term(step), jnp.zeros((8, channels), jnp.float32)
-        )
-
-    mean = fold_all(lambda step: fold(block(step))).sum(axis=0, keepdims=True) / positions
-    square = fold_all(lambda step: fold((block(step) - mean) ** 2)).sum(axis=0, keepdims=True)
+        elif piece == 1:
+            near = over_steps(0, first_sum, zero).sum(axis=0, keepdims=True) * (
+                pieces / positions
+            )
+        else:
+            if piece == 2:
+                sums = over_steps(0, first_moments, (zero, zero))
+            sums = over_steps(piece - 1, moments, sums)
+    sums = over_steps(pieces - 1, moments, sums)
+    off = sums[0].sum(axis=0, keepdims=True) / positions
+    mean = near + off
+    square = sums[1].sum(axis=0, keepdims=True) - positions * off * off
     row = lax.broadcasted_iota(jnp.int32, (8, channels), 0)
     packed = jnp.where(row == 0, mean, jnp.where(row == 1, square, 0.0))
     for slot in range(stats.shape[0]):
@@ -184,16 +190,19 @@
 
 
 def act_kernel(
-    loss_scale, keep, spatial, stats, cot, arrived, weights, params, act, normed, pre, temporal,
-    sums, halo,
+    loss_scale, spatial, stats, cot, arrived, weights, params, act, normed, pre, temporal, sums,
+    halo,
 ):
     frames, out_rows, out_cols, channels = spatial.shape
     positions = frames * out_rows * out_cols
     mean, inv_std = clip_norm(stats, positions, channels // GROUPS)
     gain, shift = params[0:1], params[1:2]
+    per_clip = sums.shape[0]
+    not_last = lax.rem(lax.axis_index("seq"), per_clip) != per_clip - 1
     for frame in range(2):
         value = arrived[frame]
-        halo[frame] = jnp.where(keep[0] != 0, value, jnp.zeros_like(value))
+        halo[frame] = jnp.where(not_last, value, jnp.zeros_like(value))
+    turned_weights = jnp.concatenate([weights[tap] for tap in range(3)], axis=1)
     flat = (STEP_ROWS * out_cols, channels)
     shaped = (STEP_ROWS, out_cols, channels)
     sums_shift = jnp.zeros((8, channels), jnp.float32)
@@ -215,9 +224,8 @@
             before = norm * gain + shift
             sig = jax.nn.sigmoid(before)
             act[frame, rows] = (before * sig).astype(jnp.bfloat16).reshape(shaped)
-            back = dot_transposed(cot_block(0, rows), weights[0])
-            back += dot_transposed(cot_block(1, rows), weights[1])
-            back += dot_transposed(cot_block(2, rows), weights[2])
+            cots = jnp.concatenate([cot_block(later, rows) for later in range(3)], axis=1)
+            back = dot_transposed(cots, turned_weights)
             back = back.astype(jnp.bfloat16).astype(jnp.float32)
             back_pre = back * loss_scale * sig * (1.0 + before * (1.0 - sig))
             normed[frame, rows] = norm.reshape(shaped)
@@ -243,17 +251,21 @@
         sums[slot] = packed
 
     all_rows = (out_rows * out_cols, channels)
-    parts = [None, None, None]
+    total = None
     for frame in range(frames):
-        turned = act[frame].reshape(all_rows).T
-        for later in range(3):
-            value = cot[frame + later] if frame + later < frames else halo[frame + later - frames]
-            term = dot(turned, value.reshape(all_rows))
-            parts[later] = term if parts[later] is None else parts[later] + term
+        cots = jnp.concatenate(
+            [
+                (cot[frame + later] if frame + later < frames else halo[frame + later - frames])
+                .reshape(all_rows)
+                for later in range(3)
+            ],
+            axis=1,
+        )
+        term = dot(act[frame].reshape(all_rows).T, cots)
+        total = term if total is None else total + term
     for later in range(3):
-        temporal[pl.ds(later * channels, channels)] = (parts[later] * loss_scale).astype(
-            jnp.bfloat16
-        )
+        block = total[:, later * channels : (later + 1) * channels] * loss_scale
+        temporal[pl.ds(later * channels, channels)] = block.astype(jnp.bfloat16)
 
 
 def split_rows(values, rows):
@@ -358,8 +370,9 @@
     grad_temporal[...] = arrived[pl.ds(rows, grad_temporal.shape[0])].astype(jnp.float32)
 
 
-def encode_kernel(keep, act, halo, weights, encoded):
+def encode_kernel(per_clip, act, halo, weights, encoded):
     frames, out_rows, out_cols, channels = act.shape
+    not_first = lax.rem(lax.axis_index("seq"), per_clip) != 0
     flat = (STEP_ROWS * out_cols, channels)
     for frame in range(frames):
 
@@ -371,7 +384,7 @@
                     source = act[frame - tap, rows]
                 else:
                     source = halo[frames + frame - tap, rows]
-                    source = jnp.where(keep[0] != 0, source, jnp.zeros_like(source))
+                    source = jnp.where(not_first, source, jnp.zeros_like(source))
                 term = dot(source.reshape(flat), weights[tap])
                 total = term if total is None else total + term
             encoded[frame, rows] = total.astype(jnp.bfloat16).reshape(
@@ -400,9 +413,6 @@
         (s, s // per_clip * per_clip + (s + 1) % per_clip) for s in range(seq_size)
     ]
     back_pairs = [(target, source) for source, target in ahead_pairs]
-    member = lax.axis_index("seq") % per_clip
-    not_first = (member != 0).astype(jnp.int32)[None]
-    not_last = (member != per_clip - 1).astype(jnp.int32)[None]
     clips = [list(range(first, first + per_clip)) for first in range(0, seq_size, per_clip)]
 
     def exchange(value, axes, groups=None):
@@ -431,7 +441,7 @@
         ),
         specs=[FAR] * 4,
         scratch=[
-            pltpu.VMEM((2 * STEP_ROWS, 8 + width, channels), f32),
+            pltpu.VMEM((4 * STEP_ROWS, 8 + width, channels), f32),
             pltpu.VMEM(video.shape, bf16),
             pltpu.VMEM((3, 3 * channels, channels), bf16),
             pltpu.SemaphoreType.DMA((pieces + 3,)),
@@ -448,8 +458,7 @@
             struct((3 * channels, channels), bf16),
             struct((per_clip, 8, channels), f32),
         ),
-        (not_last, spatial, stats, cot, cot_halo, w_temporal, params),
-        specs=[SCALAR] + [WHOLE] * 6,
+        (spatial, stats, cot, cot_halo, w_temporal, params),
         scratch=[pltpu.VMEM((2,) + shape[1:], bf16)],
         flops=2 * positions * 3 * channels * channels,
     )
@@ -478,10 +487,9 @@
         other = jnp.zeros_like(mine)
     act, act_halo, _ = lax.optimization_barrier((act, act_halo, mine))
     encoded = call(
-        encode_kernel,
+        functools.partial(encode_kernel, per_clip),
         struct(shape, bf16),
-        (not_first, act, act_halo, w_temporal),
-        specs=[SCALAR] + [WHOLE] * 3,
+        (act, act_halo, w_temporal),
         flops=2 * positions * 3 * channels * channels,
     )
     other, encoded = lax.optimization_barrier((other, encoded))

time: 55.8 us -> 54.1 us (0.970)
  blocking collectives: 30.1 us -> 37.1 us
  waiting for transfers between devices: 5.89 us -> 1.2 us
  starting transfers between devices: 10.6 us -> 7.32 us
  Pallas kernels: 8.25 us -> 7.48 us
    all_to_all x3 -> x4, blocking collectives: 30.1 us -> 37.1 us  [exchange(): lax.all_to_all(value, axes, 0, 0, axis_index_groups=groups, tiled=True)]
    all_to_all x1 -> x0, waiting for transfers between devices: 4.67 us -> none  [exchange(): lax.all_to_all(value, axes, 0, 0, axis_index_groups=groups, tiled=True)]
    all_to_all x1 -> x0, starting transfers between devices: 3.27 us -> none  [exchange(): lax.all_to_all(value, axes, 0, 0, axis_index_groups=groups, tiled=True)]
    pallas_call x7, Pallas kernels: 8.25 us -> 7.48 us  [call(): pl.pallas_call(kernel, out_shape=out_shape, in_specs=specs or [WHOLE] * l...]
  transfers between devices with their start and end apart: 4 -> 3, of which waited for: 2 -> 1; matrix products, arithmetic and copies ran while one was open for 0% -> 0% of each run, Pallas kernels for 8% -> 7%
where the time goes in v9:
time: 54.1 us; the launch traced here: 53.8 us
  blocking collectives  37.1 us (69%)
  Pallas kernels  7.48 us (14%)
  starting transfers between devices  7.32 us (14%)
  waiting for transfers between devices  1.2 us (2%)
  between operations  0.67 us (1%)
    all_to_all x4, blocking collectives, exchange(): lax.all_to_all(value, axes, 0, 0, axis_index_groups=groups, tiled=True)  37.1 us
    pallas_call x7, Pallas kernels, call(): pl.pallas_call(kernel, out_shape=out_shape, in_specs=specs or [WHOLE] * l...  7.48 us
    ppermute x1, starting transfers between devices, on_device(): cot_halo = lax.ppermute(cot, 'seq', back_pairs)  4 us
    ppermute x1, starting transfers between devices, on_device(): lax.ppermute(mine, 'seq', [(s, (s + half) % seq_size) for s in range(seq_...  2.65 us
    ppermute x1, waiting for transfers between devices, on_device(): lax.ppermute(mine, 'seq', [(s, (s + half) % seq_size) for s in range(seq_...  1.2 us
  transfers between devices with their start and end apart: 3, of which 1 were waited for; matrix products, arithmetic and copies ran while one was open for 0% of the time, Pallas kernels for 7%

profile of v9, /device:TPU:0, one launch (start us, length us, event | category | flops | bytes accessed | tf_op | source)
XLA Modules:
  0.0 53.8 jit_solution(18305063512199625500)
XLA Ops:
  0.6 4.0 %collective-permute-start = (bf16[2,16,32,128]{3,2,1,0:T(8,128)(2,1)}, bf16[2,16,32,128]{3,2,1,0:T(8,128)(2,1)S(1)}, u32[]{:S(2)}, u32[]{:S(2)}) collective-permute-start(bf16[2,16,32,128]{3,2,1,0:T(8,128)(2,1)} %bitcast.12), channel_id=1, source_target_pairs={{1,0},{2,1},{3,2},{0,3},{5,4},{6,5},{7,6},{4,7},{9,8},{10,9},{11,1... | collective-permute-start | bytes 786440 | tf_op jit(solution)/shard_map/ppermute | solution.py:424
  4.6 0.0 copy-start
  4.6 0.0 copy-start.1
  4.6 2.6 %shard_map.101 = (f32[2,16,32,128]{3,2,1,0:T(8,128)S(1)}, f32[4,8,128]{2,1,0:T(8,128)S(1)}, bf16[2,17,32,384]{3,2,1,0:T(8,128)(2,1)S(1)}, bf16[2,16,32,384]{3,2,1,0:T(8,128)(2,1)S(1)}, f32[8,128]{1,0:T(8,128)S(1)}) custom-call(bf16[2,32,64,128]{3,2,1,0:T(8,128)(2,1)} %bitcast.14, bf16[3,384,128]{2,1,0:T(8,128)(2,1)} %bitcast.15, f32[1,128]{1,0:T(1,128)} %bitcast.17, ...), custom_call_target="tpu_custom_call" | custom-call | flops 301989888 | bytes 3511296 | tf_op jit(solution)/shard_map/pallas_call | solution.py:43
  7.3 7.1 %all_to_all.20.stats = f32[4,8,128]{2,1,0:T(8,128)S(1)} all-to-all(f32[4,8,128]{2,1,0:T(8,128)S(1)} %get-tuple-element.29), channel_id=1, replica_groups={{0,1,2,3},{4,5,6,7},{8,9,10,11},{12,13,14,15},{16,17,18,19},{20,21,22,2..., dimensions={0} | all-to-all | bytes 32768 | tf_op jit(solution)/shard_map/all_to_all | solution.py:419
  14.3 0.0 collective-permute-done.arrived
  14.3 0.0 copy-done
  14.3 0.0 copy-done.1
  14.3 1.3 %shard_map.102 = (bf16[2,16,32,128]{3,2,1,0:T(8,128)(2,1)S(1)}, f32[2,16,32,128]{3,2,1,0:T(8,128)S(1)}, f32[2,16,32,128]{3,2,1,0:T(8,128)S(1)}, bf16[384,128]{1,0:T(8,128)(2,1)S(1)}, f32[4,8,128]{2,1,0:T(8,128)S(1)}) custom-call(f32[2,16,32,128]{3,2,1,0:T(8,128)S(1)} %get-tuple-element.28.spatial, f32[4,8,128]{2,1,0:T(8,128)S(1)} %all_to_all.20.stats, ...), custom_call_target="tpu_custom_call" | custom-call | flops 100663296 | bytes 2592768 | tf_op jit(solution)/shard_map/pallas_call | solution.py:43
  15.7 0.7 %collective-permute-start.1 = (bf16[2,16,32,128]{3,2,1,0:T(8,128)(2,1)S(1)}, bf16[2,16,32,128]{3,2,1,0:T(8,128)(2,1)S(1)}, u32[]{:S(2)}, u32[]{:S(2)}) collective-permute-start(bf16[2,16,32,128]{3,2,1,0:T(8,128)(2,1)S(1)} %get-tuple-element.38.act), channel_id=1, source_target_pairs={{0,1},{1,2},{2,3},{3,0},{4,5},{5,6},{6,7},{7,4},{8,9},{9,10},{10,1... | collective-permute-start | bytes 786440 | tf_op jit(solution)/shard_map/ppermute | solution.py:465
  16.3 8.1 %all_to_all.21.sums = f32[4,8,128]{2,1,0:T(8,128)S(1)} all-to-all(f32[4,8,128]{2,1,0:T(8,128)S(1)} %get-tuple-element.33), channel_id=1, replica_groups={{0,1,2,3},{4,5,6,7},{8,9,10,11},{12,13,14,15},{16,17,18,19},{20,21,22,2..., dimensions={0} | all-to-all | bytes 32768 | tf_op jit(solution)/shard_map/all_to_all | solution.py:419
  24.4 0.0 collective-permute-done.1.halo
  24.4 1.0 %shard_map.103 = bf16[16,104,128]{2,1,0:T(8,128)(2,1)S(1)} custom-call(bf16[2,17,32,384]{3,2,1,0:T(8,128)(2,1)S(1)} %get-tuple-element.26.odd, bf16[2,16,32,384]{3,2,1,0:T(8,128)(2,1)S(1)} %get-tuple-element.27.even, f32[2,16,32,128]{3,2,1,0:T(8,128)S(1)} %get-tuple-element.31.normed, f32[2,16,32,128]{3,2,1,0:T(8,128)S(1)} %get-tuple-element.32.pre, ...), custom_call_target="tpu_custom_call" | custom-call | flops 301989888 | bytes 3211264 | tf_op jit(solution)/shard_map/pallas_call | solution.py:43
  25.4 11.1 %all_to_all.22.arrived = bf16[16,104,128]{2,1,0:T(8,128)(2,1)S(1)} all-to-all(bf16[16,104,128]{2,1,0:T(8,128)(2,1)S(1)} %shard_map.103), channel_id=1, replica_groups={{0,1,2,3,8,9,10,11,16,17,18,19,24,25,26,27},{4,5,6,7,12,13,14,15,20,21,..., dimensions={0} | all-to-all | bytes 851968 | tf_op jit(solution)/shard_map/all_to_all | solution.py:419
  36.5 0.1 shard_map.104.mine
  36.5 2.7 %collective-permute-start.2 = (bf16[104,128]{1,0:T(8,128)(2,1)S(1)}, bf16[104,128]{1,0:T(8,128)(2,1)S(1)}, u32[]{:S(2)}, u32[]{:S(2)}) collective-permute-start(bf16[104,128]{1,0:T(8,128)(2,1)S(1)} %shard_map.104.mine), channel_id=1, source_target_pairs={{0,4},{1,5},{2,6},{3,7},{4,0},{5,1},{6,2},{7,3},{8,12},{9,13},{10,... | collective-permute-start | bytes 79880 | tf_op jit(solution)/shard_map/ppermute | solution.py:485
  39.2 1.1 %shard_map.105 = bf16[2,16,32,128]{3,2,1,0:T(8,128)(2,1)} custom-call(bf16[2,16,32,128]{3,2,1,0:T(8,128)(2,1)S(1)} %get-tuple-element.38.act, bf16[2,16,32,128]{3,2,1,0:T(8,128)(2,1)S(1)} %collective-permute-done.1.halo, bf16[3,128,128]{2,1,0:T(8,128)(2,1)S(1)} %copy-done), custom_call_target="tpu_custom_call" | custom-call | flops 100663296 | bytes 884736 | tf_op jit(solution)/shard_map/pallas_call | solution.py:43
  40.2 1.2 %collective-permute-done.2.other = bf16[104,128]{1,0:T(8,128)(2,1)S(1)} collective-permute-done((bf16[104,128]{1,0:T(8,128)(2,1)S(1)}, bf16[104,128]{1,0:T(8,128)(2,1)S(1)}, u32[]{:S(2)}, u32[]{:S(2)}) %collective-permute-start.2) | collective-permute-done | bytes 26656 | tf_op jit(solution)/shard_map/ppermute | solution.py:485
  41.4 0.5 shard_map.106
  42.0 10.9 %all_to_all.23 = bf16[16,96,128]{2,1,0:T(8,128)(2,1)S(1)} all-to-all(bf16[16,96,128]{2,1,0:T(8,128)(2,1)S(1)} %get-tuple-element.42), channel_id=1, replica_groups={{0,1,2,3,8,9,10,11,16,17,18,19,24,25,26,27},{4,5,6,7,12,13,14,15,20,21,..., dimensions={0} | all-to-all | bytes 786432 | tf_op jit(solution)/shard_map/all_to_all | solution.py:419
  52.9 0.9 %shard_map.107 = (f32[1152,128]{1,0:T(8,128)}, f32[384,128]{1,0:T(8,128)}) custom-call(bf16[1536,128]{1,0:T(8,128)(2,1)S(1)} %bitcast.11), custom_call_target="tpu_custom_call" | custom-call | bytes 1179648 | tf_op jit(solution)/shard_map/pallas_call | solution.py:43
Async XLA Ops:
  0.6 13.7 %collective-permute-start = (bf16[2,16,32,128]{3,2,1,0:T(8,128)(2,1)}, bf16[2,16,32,128]{3,2,1,0:T(8,128)(2,1)S(1)}, u32[]{:S(2)}, u32[]{:S(2)}) collective-permute-start(bf16[2,16,32,128]{3,2,1,0:T(8,128)(2,1)} %bitcast.12), channel_id=1, source_target_pairs={{1,0},{2,1},{3,2},{0,3},{5,4},{6,5},{7,6},{4,7},{9,8},{10,9},{11,1... | collective-permute-start | bytes 786440 | tf_op jit(solution)/shard_map/ppermute | solution.py:424
  4.6 9.7 %copy-start = (bf16[3,128,128]{2,1,0:T(8,128)(2,1)S(1)}, bf16[3,128,128]{2,1,0:T(8,128)(2,1)}, u32[]{:S(2)}) copy-start(bf16[3,128,128]{2,1,0:T(8,128)(2,1)} %weights.3) | copy-start | bytes 294916
  4.6 9.7 %copy-start.1 = (bf16[1,2,16,32,128]{4,3,2,1,0:T(8,128)(2,1)S(1)}, bf16[1,2,16,32,128]{4,3,2,1,0:T(8,128)(2,1)}, u32[]{:S(2)}) copy-start(bf16[1,2,16,32,128]{4,3,2,1,0:T(8,128)(2,1)} %param.11) | copy-start | bytes 786436
  15.7 8.8 %collective-permute-start.1 = (bf16[2,16,32,128]{3,2,1,0:T(8,128)(2,1)S(1)}, bf16[2,16,32,128]{3,2,1,0:T(8,128)(2,1)S(1)}, u32[]{:S(2)}, u32[]{:S(2)}) collective-permute-start(bf16[2,16,32,128]{3,2,1,0:T(8,128)(2,1)S(1)} %get-tuple-element.38.act), channel_id=1, source_target_pairs={{0,1},{1,2},{2,3},{3,0},{4,5},{5,6},{6,7},{7,4},{8,9},{9,10},{10,1... | collective-permute-start | bytes 786440 | tf_op jit(solution)/shard_map/ppermute | solution.py:465
  36.5 4.9 %collective-permute-start.2 = (bf16[104,128]{1,0:T(8,128)(2,1)S(1)}, bf16[104,128]{1,0:T(8,128)(2,1)S(1)}, u32[]{:S(2)}, u32[]{:S(2)}) collective-permute-start(bf16[104,128]{1,0:T(8,128)(2,1)S(1)} %shard_map.104.mine), channel_id=1, source_target_pairs={{0,4},{1,5},{2,6},{3,7},{4,0},{5,1},{6,2},{7,3},{8,12},{9,13},{10,... | collective-permute-start | bytes 79880 | tf_op jit(solution)/shard_map/ppermute | solution.py:485

commit v10 on v9

--- a/solution.py
+++ b/solution.py
@@ -68,31 +68,26 @@
     return values
 
 
+def open_kernel(gate):
+    gate[...] = jnp.zeros(gate.shape, gate.dtype)
+
+
 def conv_kernel(
-    video_far, weights_far, gain_far, shift_far, spatial, stats, odd, even, params, wide, video,
+    pieces, blank, video, weights_far, gain_far, shift_far, spatial, stats, odd, even, params, wide,
     weights, arrived,
 ):
     frames, height, width, channels = video.shape
     out_rows, out_cols = height // 2, width // 2
     positions = frames * out_rows * out_cols
-    pieces = arrived.shape[0] - 3
     half = height * frames // pieces
-    copies = []
-    for piece in range(pieces):
-        rows = pl.ds(piece * half % height, half)
-        at = (piece * half // height, rows)
-        copies.append(pltpu.make_async_copy(video_far.at[at], video.at[at], arrived.at[piece]))
-    small = [
-        pltpu.make_async_copy(source, target, arrived.at[pieces + index])
+    params[...] = blank[...]
+    copies = [
+        pltpu.make_async_copy(source, target, arrived.at[index])
         for index, (source, target) in enumerate(
             ((weights_far, weights), (gain_far, params.at[0:1]), (shift_far, params.at[1:2]))
         )
     ]
-    copies[0].start()
-    small[0].start()
-    for copy in copies[1:]:
-        copy.start()
-    for copy in small[1:]:
+    for copy in copies:
         copy.start()
     for slot in range(wide.shape[0]):
         wide[slot, 0:8] = jnp.zeros((8, channels), jnp.float32)
@@ -153,18 +148,12 @@
         return fold(off), fold(off * off)
 
     for piece in range(pieces):
-        copies[piece].wait()
         each(steps, functools.partial(separate, piece))
-        if piece == 0:
-            small[0].wait()
-        elif piece == 1:
-            near = over_steps(0, first_sum, zero).sum(axis=0, keepdims=True) * (
-                pieces / positions
-            )
-        else:
-            if piece == 2:
-                sums = over_steps(0, first_moments, (zero, zero))
-            sums = over_steps(piece - 1, moments, sums)
+    copies[0].wait()
+    near = over_steps(0, first_sum, zero).sum(axis=0, keepdims=True) * (pieces / positions)
+    sums = over_steps(0, first_moments, (zero, zero))
+    for piece in range(1, pieces - 1):
+        sums = over_steps(piece, moments, sums)
     sums = over_steps(pieces - 1, moments, sums)
     off = sums[0].sum(axis=0, keepdims=True) / positions
     mean = near + off
@@ -173,9 +162,8 @@
     packed = jnp.where(row == 0, mean, jnp.where(row == 1, square, 0.0))
     for slot in range(stats.shape[0]):
         stats[slot] = packed
-    for copy in small[1:]:
+    for copy in copies[1:]:
         copy.wait()
-
 
 def clip_norm(stats, positions, lanes):
     cells = stats.shape[0] * lanes
@@ -418,14 +406,25 @@
     def exchange(value, axes, groups=None):
         return lax.all_to_all(value, axes, 0, 0, axis_index_groups=groups, tiled=True)
 
+    gate = pl.pallas_call(
+        open_kernel,
+        out_shape=struct((8, channels), f32),
+        out_specs=WHOLE,
+        cost_estimate=pl.CostEstimate(
+            flops=2 * positions * 9 * channels * channels,
+            bytes_accessed=2 * video.size,
+            transcendentals=0,
+        ),
+    )()
+    cot_out, gate = lax.optimization_barrier((cot, gate))
+    cot_halo = lax.ppermute(cot_out, "seq", back_pairs)
+
+    pieces = 2 * frames
     def far(value):
         return pltpu.with_memory_space_constraint(value, pltpu.HBM)
 
-    cot_halo = lax.ppermute(cot, "seq", back_pairs)
-
-    pieces = 2 * frames
     spatial, stats, odd, even, params = call(
-        conv_kernel,
+        functools.partial(conv_kernel, pieces),
         (
             struct(shape, f32),
             struct((per_clip, 8, channels), f32),
@@ -434,17 +433,17 @@
             struct((8, channels), f32),
         ),
         (
-            far(video),
+            gate,
+            video,
             far(w_spatial.reshape(3, 3 * channels, channels)),
             far(norm_gain[None]),
             far(norm_shift[None]),
         ),
-        specs=[FAR] * 4,
+        specs=[WHOLE] * 2 + [FAR] * 3,
         scratch=[
             pltpu.VMEM((4 * STEP_ROWS, 8 + width, channels), f32),
-            pltpu.VMEM(video.shape, bf16),
             pltpu.VMEM((3, 3 * channels, channels), bf16),
-            pltpu.SemaphoreType.DMA((pieces + 3,)),
+            pltpu.SemaphoreType.DMA((3,)),
         ],
         flops=2 * positions * 9 * channels * channels,
     )

time: 54.1 us -> 53.9 us (level)
    pallas_call x7, Pallas kernels: 7.48 us -> 6.72 us  [call(): pl.pallas_call(kernel, out_shape=out_shape, in_specs=specs or [WHOLE] * l...]
    pallas_call x0 -> x1, Pallas kernels: none -> 0.6 us  [on_device(): pl.pallas_call(open_kernel, out_shape=struct((8, channels), f32), out_spe...]
  transfers between devices with their start and end apart: 3 -> 3, of which waited for: 1 -> 1; matrix products, arithmetic and copies ran while one was open for 0% -> 0% of each run, Pallas kernels for 7% -> 5%
where the time goes in v10:
time: 53.9 us; the launch traced here: 53.6 us
  blocking collectives  37.1 us (69%)
  Pallas kernels  7.31 us (14%)
  starting transfers between devices  7.26 us (13%)
  waiting for transfers between devices  1.2 us (2%)
  between operations  0.68 us (1%)
    all_to_all x4, blocking collectives, exchange(): lax.all_to_all(value, axes, 0, 0, axis_index_groups=groups, tiled=True)  37.1 us
    pallas_call x7, Pallas kernels, call(): pl.pallas_call(kernel, out_shape=out_shape, in_specs=specs or [WHOLE] * l...  6.72 us
    ppermute x1, starting transfers between devices, on_device(): cot_halo = lax.ppermute(cot_out, 'seq', back_pairs)  3.95 us
    ppermute x1, starting transfers between devices, on_device(): lax.ppermute(mine, 'seq', [(s, (s + half) % seq_size) for s in range(seq_...  2.65 us
    ppermute x1, waiting for transfers between devices, on_device(): lax.ppermute(mine, 'seq', [(s, (s + half) % seq_size) for s in range(seq_...  1.2 us
  transfers between devices with their start and end apart: 3, of which 1 were waited for; matrix products, arithmetic and copies ran while one was open for 0% of the time, Pallas kernels for 5%

profile of v10, /device:TPU:0, one launch (start us, length us, event | category | flops | bytes accessed | tf_op | source)
XLA Modules:
  0.0 53.6 jit_solution(802107648260059026)
XLA Ops:
  0.6 0.0 copy-start
  0.6 0.6 %shard_map.101.blank = f32[8,128]{1,0:T(8,128)} custom-call(), custom_call_target="tpu_custom_call" | custom-call | flops 301989888 | bytes 1048576 | tf_op jit(solution)/shard_map/pallas_call | solution.py:409
  1.2 0.0 copy-start.3
  1.2 4.0 %collective-permute-start = (bf16[2,16,32,128]{3,2,1,0:T(8,128)(2,1)}, bf16[2,16,32,128]{3,2,1,0:T(8,128)(2,1)S(1)}, u32[]{:S(2)}, u32[]{:S(2)}) collective-permute-start(bf16[2,16,32,128]{3,2,1,0:T(8,128)(2,1)} %bitcast.13), channel_id=1, source_target_pairs={{1,0},{2,1},{3,2},{0,3},{5,4},{6,5},{7,6},{4,7},{9,8},{10,9},{11,1... | collective-permute-start | bytes 786440 | tf_op jit(solution)/shard_map/ppermute | solution.py:420
  5.2 0.0 copy-done
  5.2 0.0 copy-done.3
  5.2 0.0 copy-start.1
  5.2 0.0 copy-start.2
  5.2 1.8 %shard_map.102 = (f32[2,16,32,128]{3,2,1,0:T(8,128)S(1)}, f32[4,8,128]{2,1,0:T(8,128)S(1)}, bf16[2,17,32,384]{3,2,1,0:T(8,128)(2,1)S(1)}, bf16[2,16,32,384]{3,2,1,0:T(8,128)(2,1)S(1)}, f32[8,128]{1,0:T(8,128)S(1)}) custom-call(f32[8,128]{1,0:T(8,128)S(1)} %copy-done.3, bf16[2,32,64,128]{3,2,1,0:T(8,128)(2,1)S(1)} %bitcast.12, bf16[3,384,128]{2,1,0:T(8,128)(2,1)} %bitcast.15, ...), custom_call_target="tpu_custom_call" | custom-call | flops 301989888 | bytes 3515392 | tf_op jit(solution)/shard_map/pallas_call | solution.py:43
  7.0 7.1 %all_to_all.20.stats = f32[4,8,128]{2,1,0:T(8,128)S(1)} all-to-all(f32[4,8,128]{2,1,0:T(8,128)S(1)} %get-tuple-element.32), channel_id=1, replica_groups={{0,1,2,3},{4,5,6,7},{8,9,10,11},{12,13,14,15},{16,17,18,19},{20,21,22,2..., dimensions={0} | all-to-all | bytes 32768 | tf_op jit(solution)/shard_map/all_to_all | solution.py:407
  14.1 0.0 collective-permute-done.arrived
  14.1 0.0 copy-done.1
  14.1 0.0 copy-done.2
  14.1 1.3 %shard_map.103 = (bf16[2,16,32,128]{3,2,1,0:T(8,128)(2,1)S(1)}, f32[2,16,32,128]{3,2,1,0:T(8,128)S(1)}, f32[2,16,32,128]{3,2,1,0:T(8,128)S(1)}, bf16[384,128]{1,0:T(8,128)(2,1)S(1)}, f32[4,8,128]{2,1,0:T(8,128)S(1)}) custom-call(f32[2,16,32,128]{3,2,1,0:T(8,128)S(1)} %get-tuple-element.31.spatial, f32[4,8,128]{2,1,0:T(8,128)S(1)} %all_to_all.20.stats, ...), custom_call_target="tpu_custom_call" | custom-call | flops 100663296 | bytes 2592768 | tf_op jit(solution)/shard_map/pallas_call | solution.py:43
  15.5 0.7 %collective-permute-start.1 = (bf16[2,16,32,128]{3,2,1,0:T(8,128)(2,1)S(1)}, bf16[2,16,32,128]{3,2,1,0:T(8,128)(2,1)S(1)}, u32[]{:S(2)}, u32[]{:S(2)}) collective-permute-start(bf16[2,16,32,128]{3,2,1,0:T(8,128)(2,1)S(1)} %get-tuple-element.42.act), channel_id=1, source_target_pairs={{0,1},{1,2},{2,3},{3,0},{4,5},{5,6},{6,7},{7,4},{8,9},{9,10},{10,1... | collective-permute-start | bytes 786440 | tf_op jit(solution)/shard_map/ppermute | solution.py:464
  16.1 8.1 %all_to_all.21.sums = f32[4,8,128]{2,1,0:T(8,128)S(1)} all-to-all(f32[4,8,128]{2,1,0:T(8,128)S(1)} %get-tuple-element.37), channel_id=1, replica_groups={{0,1,2,3},{4,5,6,7},{8,9,10,11},{12,13,14,15},{16,17,18,19},{20,21,22,2..., dimensions={0} | all-to-all | bytes 32768 | tf_op jit(solution)/shard_map/all_to_all | solution.py:407
  24.2 0.0 collective-permute-done.1.halo
  24.2 1.0 %shard_map.104 = bf16[16,104,128]{2,1,0:T(8,128)(2,1)S(1)} custom-call(bf16[2,17,32,384]{3,2,1,0:T(8,128)(2,1)S(1)} %get-tuple-element.29.odd, bf16[2,16,32,384]{3,2,1,0:T(8,128)(2,1)S(1)} %get-tuple-element.30.even, f32[2,16,32,128]{3,2,1,0:T(8,128)S(1)} %get-tuple-element.35.normed, f32[2,16,32,128]{3,2,1,0:T(8,128)S(1)} %get-tuple-element.36.pre, ...), custom_call_target="tpu_custom_call" | custom-call | flops 301989888 | bytes 3211264 | tf_op jit(solution)/shard_map/pallas_call | solution.py:43
  25.2 11.1 %all_to_all.22.arrived = bf16[16,104,128]{2,1,0:T(8,128)(2,1)S(1)} all-to-all(bf16[16,104,128]{2,1,0:T(8,128)(2,1)S(1)} %shard_map.104), channel_id=1, replica_groups={{0,1,2,3,8,9,10,11,16,17,18,19,24,25,26,27},{4,5,6,7,12,13,14,15,20,21,..., dimensions={0} | all-to-all | bytes 851968 | tf_op jit(solution)/shard_map/all_to_all | solution.py:407
  36.2 0.1 shard_map.105.mine
  36.3 2.7 %collective-permute-start.2 = (bf16[104,128]{1,0:T(8,128)(2,1)S(1)}, bf16[104,128]{1,0:T(8,128)(2,1)S(1)}, u32[]{:S(2)}, u32[]{:S(2)}) collective-permute-start(bf16[104,128]{1,0:T(8,128)(2,1)S(1)} %shard_map.105.mine), channel_id=1, source_target_pairs={{0,4},{1,5},{2,6},{3,7},{4,0},{5,1},{6,2},{7,3},{8,12},{9,13},{10,... | collective-permute-start | bytes 79880 | tf_op jit(solution)/shard_map/ppermute | solution.py:484
  39.0 1.1 %shard_map.106 = bf16[2,16,32,128]{3,2,1,0:T(8,128)(2,1)} custom-call(bf16[2,16,32,128]{3,2,1,0:T(8,128)(2,1)S(1)} %get-tuple-element.42.act, bf16[2,16,32,128]{3,2,1,0:T(8,128)(2,1)S(1)} %collective-permute-done.1.halo, bf16[3,128,128]{2,1,0:T(8,128)(2,1)S(1)} %copy-done.1), custom_call_target="tpu_custom_call" | custom-call | flops 100663296 | bytes 884736 | tf_op jit(solution)/shard_map/pallas_call | solution.py:43
  40.0 1.2 %collective-permute-done.2.other = bf16[104,128]{1,0:T(8,128)(2,1)S(1)} collective-permute-done((bf16[104,128]{1,0:T(8,128)(2,1)S(1)}, bf16[104,128]{1,0:T(8,128)(2,1)S(1)}, u32[]{:S(2)}, u32[]{:S(2)}) %collective-permute-start.2) | collective-permute-done | bytes 26656 | tf_op jit(solution)/shard_map/ppermute | solution.py:484
  41.2 0.5 shard_map.107
  41.8 10.9 %all_to_all.23 = bf16[16,96,128]{2,1,0:T(8,128)(2,1)S(1)} all-to-all(bf16[16,96,128]{2,1,0:T(8,128)(2,1)S(1)} %get-tuple-element.46), channel_id=1, replica_groups={{0,1,2,3,8,9,10,11,16,17,18,19,24,25,26,27},{4,5,6,7,12,13,14,15,20,21,..., dimensions={0} | all-to-all | bytes 786432 | tf_op jit(solution)/shard_map/all_to_all | solution.py:407
  52.7 0.9 %shard_map.108 = (f32[1152,128]{1,0:T(8,128)}, f32[384,128]{1,0:T(8,128)}) custom-call(bf16[1536,128]{1,0:T(8,128)(2,1)S(1)} %bitcast.11), custom_call_target="tpu_custom_call" | custom-call | bytes 1179648 | tf_op jit(solution)/shard_map/pallas_call | solution.py:43
Async XLA Ops:
  0.6 4.6 %copy-start = (bf16[1,2,32,64,128]{4,3,2,1,0:T(8,128)(2,1)S(1)}, bf16[1,2,32,64,128]{4,3,2,1,0:T(8,128)(2,1)}, u32[]{:S(2)}) copy-start(bf16[1,2,32,64,128]{4,3,2,1,0:T(8,128)(2,1)} %param.6) | copy-start | bytes 3145732
  1.2 4.0 %copy-start.3 = (f32[8,128]{1,0:T(8,128)S(1)}, f32[8,128]{1,0:T(8,128)}, u32[]{:S(2)}) copy-start(f32[8,128]{1,0:T(8,128)} %shard_map.101.blank) | copy-start | bytes 12292
  1.2 12.9 %collective-permute-start = (bf16[2,16,32,128]{3,2,1,0:T(8,128)(2,1)}, bf16[2,16,32,128]{3,2,1,0:T(8,128)(2,1)S(1)}, u32[]{:S(2)}, u32[]{:S(2)}) collective-permute-start(bf16[2,16,32,128]{3,2,1,0:T(8,128)(2,1)} %bitcast.13), channel_id=1, source_target_pairs={{1,0},{2,1},{3,2},{0,3},{5,4},{6,5},{7,6},{4,7},{9,8},{10,9},{11,1... | collective-permute-start | bytes 786440 | tf_op jit(solution)/shard_map/ppermute | solution.py:420
  5.2 8.9 %copy-start.1 = (bf16[3,128,128]{2,1,0:T(8,128)(2,1)S(1)}, bf16[3,128,128]{2,1,0:T(8,128)(2,1)}, u32[]{:S(2)}) copy-start(bf16[3,128,128]{2,1,0:T(8,128)(2,1)} %weights.3) | copy-start | bytes 294916
  5.2 8.9 %copy-start.2 = (bf16[1,2,16,32,128]{4,3,2,1,0:T(8,128)(2,1)S(1)}, bf16[1,2,16,32,128]{4,3,2,1,0:T(8,128)(2,1)}, u32[]{:S(2)}) copy-start(bf16[1,2,16,32,128]{4,3,2,1,0:T(8,128)(2,1)} %param.11) | copy-start | bytes 786436
  15.5 8.8 %collective-permute-start.1 = (bf16[2,16,32,128]{3,2,1,0:T(8,128)(2,1)S(1)}, bf16[2,16,32,128]{3,2,1,0:T(8,128)(2,1)S(1)}, u32[]{:S(2)}, u32[]{:S(2)}) collective-permute-start(bf16[2,16,32,128]{3,2,1,0:T(8,128)(2,1)S(1)} %get-tuple-element.42.act), channel_id=1, source_target_pairs={{0,1},{1,2},{2,3},{3,0},{4,5},{5,6},{6,7},{7,4},{8,9},{9,10},{10,1... | collective-permute-start | bytes 786440 | tf_op jit(solution)/shard_map/ppermute | solution.py:464
  36.3 4.9 %collective-permute-start.2 = (bf16[104,128]{1,0:T(8,128)(2,1)S(1)}, bf16[104,128]{1,0:T(8,128)(2,1)S(1)}, u32[]{:S(2)}, u32[]{:S(2)}) collective-permute-start(bf16[104,128]{1,0:T(8,128)(2,1)S(1)} %shard_map.105.mine), channel_id=1, source_target_pairs={{0,4},{1,5},{2,6},{3,7},{4,0},{5,1},{6,2},{7,3},{8,12},{9,13},{10,... | collective-permute-start | bytes 79880 | tf_op jit(solution)/shard_map/ppermute | solution.py:484

commit v11 on v10

--- a/solution.py
+++ b/solution.py
@@ -358,23 +358,34 @@
     grad_temporal[...] = arrived[pl.ds(rows, grad_temporal.shape[0])].astype(jnp.float32)
 
 
-def encode_kernel(per_clip, act, halo, weights, encoded):
+def near_encode_kernel(act, weights, part):
     frames, out_rows, out_cols, channels = act.shape
+    flat = (STEP_ROWS * out_cols, channels)
+    for frame in range(frames):
+
+        def one(step, frame=frame):
+            rows = pl.ds(step * STEP_ROWS, STEP_ROWS)
+            total = dot(act[frame, rows].reshape(flat), weights[0])
+            for tap in range(1, min(frame, 2) + 1):
+                total += dot(act[frame - tap, rows].reshape(flat), weights[tap])
+            part[frame, rows] = total.reshape(STEP_ROWS, out_cols, channels)
+
+        each(out_rows // STEP_ROWS, one)
+
+
+def encode_kernel(per_clip, part, halo, weights, encoded):
+    frames, out_rows, out_cols, channels = halo.shape
     not_first = lax.rem(lax.axis_index("seq"), per_clip) != 0
     flat = (STEP_ROWS * out_cols, channels)
     for frame in range(frames):
 
         def one(step, frame=frame):
             rows = pl.ds(step * STEP_ROWS, STEP_ROWS)
-            total = None
-            for tap in range(3):
-                if frame >= tap:
-                    source = act[frame - tap, rows]
-                else:
-                    source = halo[frames + frame - tap, rows]
-                    source = jnp.where(not_first, source, jnp.zeros_like(source))
-                term = dot(source.reshape(flat), weights[tap])
-                total = term if total is None else total + term
+            total = part[frame, rows].reshape(flat)
+            for tap in range(frame + 1, 3):
+                source = halo[frames + frame - tap, rows].reshape(flat)
+                source = jnp.where(not_first, source, jnp.zeros_like(source))
+                total += dot(source, weights[tap])
             encoded[frame, rows] = total.astype(jnp.bfloat16).reshape(
                 STEP_ROWS, out_cols, channels
             )
@@ -408,7 +419,7 @@
 
     gate = pl.pallas_call(
         open_kernel,
-        out_shape=struct((8, channels), f32),
+        out_shape=pltpu.VMEM((8, channels), f32),
         out_specs=WHOLE,
         cost_estimate=pl.CostEstimate(
             flops=2 * positions * 9 * channels * channels,
@@ -461,7 +472,6 @@
         scratch=[pltpu.VMEM((2,) + shape[1:], bf16)],
         flops=2 * positions * 3 * channels * channels,
     )
-    act_halo = lax.ppermute(act, "seq", ahead_pairs)
     sums = exchange(own, "seq", clips)
     halves = 2 if seq_size % 2 == 0 else 1
     half = seq_size // halves
@@ -471,7 +481,6 @@
     ]
     count = dp_size * half
     rows = -(-12 * channels // (16 * count)) * 16
-    sums, act_halo = lax.optimization_barrier((sums, act_halo))
     grads = call(
         grad_kernel,
         struct((count, rows + EXTRA, channels), bf16),
@@ -484,14 +493,22 @@
         other = lax.ppermute(mine, "seq", [(s, (s + half) % seq_size) for s in range(seq_size)])
     else:
         other = jnp.zeros_like(mine)
-    act, act_halo, _ = lax.optimization_barrier((act, act_halo, mine))
+    act, _ = lax.optimization_barrier((act, mine))
+    part = call(
+        near_encode_kernel,
+        struct(shape, f32),
+        (act, w_temporal),
+        flops=2 * positions * 2 * channels * channels,
+    )
+    act, part = lax.optimization_barrier((act, part))
+    act_halo = lax.ppermute(act, "seq", ahead_pairs)
+    other, part = lax.optimization_barrier((other, part))
     encoded = call(
         functools.partial(encode_kernel, per_clip),
         struct(shape, bf16),
-        (act, act_halo, w_temporal),
-        flops=2 * positions * 3 * channels * channels,
-    )
-    other, encoded = lax.optimization_barrier((other, encoded))
+        (part, act_halo, w_temporal),
+        flops=512 * positions * channels * channels,
+    )
     grads, grad_gain, grad_shift = call(
         sum_kernel,
         (

time: 53.9 us -> 58.5 us (1.085)
  blocking collectives: 37.1 us -> 25.2 us
  starting transfers between devices: 7.26 us -> 15.6 us
  waiting for transfers between devices: 1.2 us -> 9.48 us
    all_to_all x4 -> x3, blocking collectives: 37.1 us -> 25.2 us  [exchange(): lax.all_to_all(value, axes, 0, 0, axis_index_groups=groups, tiled=True)]
    all_to_all x0 -> x1, starting transfers between devices: none -> 7.71 us  [exchange(): lax.all_to_all(value, axes, 0, 0, axis_index_groups=groups, tiled=True)]
    all_to_all x0 -> x1, waiting for transfers between devices: none -> 7.06 us  [exchange(): lax.all_to_all(value, axes, 0, 0, axis_index_groups=groups, tiled=True)]
    ppermute x1, waiting for transfers between devices: 1.2 us -> 2.41 us  [on_device(): lax.ppermute(mine, 'seq', [(s, (s + half) % seq_size) for s in range(seq_...]
    ppermute x1, starting transfers between devices: 0.66 us -> 1.33 us  [on_device(): act_halo = lax.ppermute(act, 'seq', ahead_pairs)]
    pallas_call x1, Pallas kernels: 0.6 us -> 0.01 us  [on_device(): pl.pallas_call(open_kernel, out_shape=pltpu.VMEM((8, channels), f32), out...]
    pallas_call x7 -> x8, Pallas kernels: 6.72 us -> 7.1 us  [call(): pl.pallas_call(kernel, out_shape=out_shape, in_specs=specs or [WHOLE] * l...]
  transfers between devices with their start and end apart: 3 -> 4, of which waited for: 1 -> 2; matrix products, arithmetic and copies ran while one was open for 0% -> 0% of each run, Pallas kernels for 5% -> 6%
where the time goes in v11:
time: 58.5 us; the launch traced here: 58.1 us
  blocking collectives  25.2 us (43%)
  starting transfers between devices  15.6 us (27%)
  waiting for transfers between devices  9.48 us (16%)
  Pallas kernels  7.11 us (12%)
  between operations  0.7 us (1%)
    all_to_all x3, blocking collectives, exchange(): lax.all_to_all(value, axes, 0, 0, axis_index_groups=groups, tiled=True)  25.2 us
    all_to_all x1, starting transfers between devices, exchange(): lax.all_to_all(value, axes, 0, 0, axis_index_groups=groups, tiled=True)  7.71 us
    pallas_call x8, Pallas kernels, call(): pl.pallas_call(kernel, out_shape=out_shape, in_specs=specs or [WHOLE] * l...  7.1 us
    all_to_all x1, waiting for transfers between devices, exchange(): lax.all_to_all(value, axes, 0, 0, axis_index_groups=groups, tiled=True)  7.06 us
    ppermute x1, starting transfers between devices, on_device(): cot_halo = lax.ppermute(cot_out, 'seq', back_pairs)  4 us
    ppermute x1, starting transfers between devices, on_device(): lax.ppermute(mine, 'seq', [(s, (s + half) % seq_size) for s in range(seq_...  2.58 us
    ppermute x1, waiting for transfers between devices, on_device(): lax.ppermute(mine, 'seq', [(s, (s + half) % seq_size) for s in range(seq_...  2.41 us
    ppermute x1, starting transfers between devices, on_device(): act_halo = lax.ppermute(act, 'seq', ahead_pairs)  1.33 us
  transfers between devices with their start and end apart: 4, of which 2 were waited for; matrix products, arithmetic and copies ran while one was open for 0% of the time, Pallas kernels for 6%

profile of v11, /device:TPU:0, one launch (start us, length us, event | category | flops | bytes accessed | tf_op | source)
XLA Modules:
  0.0 58.1 jit_solution(5943858645408399829)
XLA Ops:
  0.6 0.0 copy-start
  0.7 4.0 %collective-permute-start = (bf16[2,16,32,128]{3,2,1,0:T(8,128)(2,1)}, bf16[2,16,32,128]{3,2,1,0:T(8,128)(2,1)S(1)}, u32[]{:S(2)}, u32[]{:S(2)}) collective-permute-start(bf16[2,16,32,128]{3,2,1,0:T(8,128)(2,1)} %bitcast.13), channel_id=1, source_target_pairs={{1,0},{2,1},{3,2},{0,3},{5,4},{6,5},{7,6},{4,7},{9,8},{10,9},{11,1... | collective-permute-start | bytes 786440 | tf_op jit(solution)/shard_map/ppermute | solution.py:431
  4.7 0.0 copy-done
  4.7 0.0 copy-start.1
  4.7 0.0 copy-start.2
  4.7 1.8 %shard_map.102 = (f32[2,16,32,128]{3,2,1,0:T(8,128)S(1)}, f32[4,8,128]{2,1,0:T(8,128)S(1)}, bf16[2,17,32,384]{3,2,1,0:T(8,128)(2,1)S(1)}, bf16[2,16,32,384]{3,2,1,0:T(8,128)(2,1)S(1)}, f32[8,128]{1,0:T(8,128)S(1)}) custom-call(f32[8,128]{1,0:T(8,128)S(1)} %shard_map.101.blank, bf16[2,32,64,128]{3,2,1,0:T(8,128)(2,1)S(1)} %bitcast.12, ...), custom_call_target="tpu_custom_call" | custom-call | flops 301989888 | bytes 3515392 | tf_op jit(solution)/shard_map/pallas_call | solution.py:43
  6.5 7.1 %all_to_all.20.stats = f32[4,8,128]{2,1,0:T(8,128)S(1)} all-to-all(f32[4,8,128]{2,1,0:T(8,128)S(1)} %get-tuple-element.31), channel_id=1, replica_groups={{0,1,2,3},{4,5,6,7},{8,9,10,11},{12,13,14,15},{16,17,18,19},{20,21,22,2..., dimensions={0} | all-to-all | bytes 32768 | tf_op jit(solution)/shard_map/all_to_all | solution.py:418
  13.6 0.0 collective-permute-done.arrived
  13.6 0.0 copy-done.1
  13.6 0.0 copy-done.2
  13.6 1.3 %shard_map.103 = (bf16[2,16,32,128]{3,2,1,0:T(8,128)(2,1)S(1)}, f32[2,16,32,128]{3,2,1,0:T(8,128)S(1)}, f32[2,16,32,128]{3,2,1,0:T(8,128)S(1)}, bf16[384,128]{1,0:T(8,128)(2,1)S(1)}, f32[4,8,128]{2,1,0:T(8,128)S(1)}) custom-call(f32[2,16,32,128]{3,2,1,0:T(8,128)S(1)} %get-tuple-element.30.spatial, f32[4,8,128]{2,1,0:T(8,128)S(1)} %all_to_all.20.stats, ...), custom_call_target="tpu_custom_call" | custom-call | flops 100663296 | bytes 2592768 | tf_op jit(solution)/shard_map/pallas_call | solution.py:43
  14.9 7.1 %all_to_all.21.sums = f32[4,8,128]{2,1,0:T(8,128)S(1)} all-to-all(f32[4,8,128]{2,1,0:T(8,128)S(1)} %get-tuple-element.36), channel_id=1, replica_groups={{0,1,2,3},{4,5,6,7},{8,9,10,11},{12,13,14,15},{16,17,18,19},{20,21,22,2..., dimensions={0} | all-to-all | bytes 32768 | tf_op jit(solution)/shard_map/all_to_all | solution.py:418
  22.0 1.0 %shard_map.104 = bf16[16,104,128]{2,1,0:T(8,128)(2,1)S(1)} custom-call(bf16[2,17,32,384]{3,2,1,0:T(8,128)(2,1)S(1)} %get-tuple-element.28.odd, bf16[2,16,32,384]{3,2,1,0:T(8,128)(2,1)S(1)} %get-tuple-element.29.even, f32[2,16,32,128]{3,2,1,0:T(8,128)S(1)} %get-tuple-element.34.normed, f32[2,16,32,128]{3,2,1,0:T(8,128)S(1)} %get-tuple-element.35.pre, ...), custom_call_target="tpu_custom_call" | custom-call | flops 301989888 | bytes 3211264 | tf_op jit(solution)/shard_map/pallas_call | solution.py:43
  23.0 11.1 %all_to_all.22.arrived = bf16[16,104,128]{2,1,0:T(8,128)(2,1)S(1)} all-to-all(bf16[16,104,128]{2,1,0:T(8,128)(2,1)S(1)} %shard_map.104), channel_id=1, replica_groups={{0,1,2,3,8,9,10,11,16,17,18,19,24,25,26,27},{4,5,6,7,12,13,14,15,20,21,..., dimensions={0} | all-to-all | bytes 851968 | tf_op jit(solution)/shard_map/all_to_all | solution.py:418
  34.0 0.1 shard_map.105.mine
  34.1 0.2 shard_map.106.part
  34.3 1.3 %collective-permute-start.2 = (bf16[2,16,32,128]{3,2,1,0:T(8,128)(2,1)S(1)}, bf16[2,16,32,128]{3,2,1,0:T(8,128)(2,1)S(1)}, u32[]{:S(2)}, u32[]{:S(2)}) collective-permute-start(bf16[2,16,32,128]{3,2,1,0:T(8,128)(2,1)S(1)} %get-tuple-element.42.act), channel_id=1, source_target_pairs={{0,1},{1,2},{2,3},{3,0},{4,5},{5,6},{6,7},{7,4},{8,9},{9,10},{10,1... | collective-permute-start | bytes 786440 | tf_op jit(solution)/shard_map/ppermute | solution.py:504
  35.7 2.6 %collective-permute-start.1 = (bf16[104,128]{1,0:T(8,128)(2,1)S(1)}, bf16[104,128]{1,0:T(8,128)(2,1)S(1)}, u32[]{:S(2)}, u32[]{:S(2)}) collective-permute-start(bf16[104,128]{1,0:T(8,128)(2,1)S(1)} %shard_map.105.mine), channel_id=1, source_target_pairs={{0,4},{1,5},{2,6},{3,7},{4,0},{5,1},{6,2},{7,3},{8,12},{9,13},{10,... | collective-permute-start | bytes 79880 | tf_op jit(solution)/shard_map/ppermute | solution.py:493
  38.2 2.4 %collective-permute-done.1.other = bf16[104,128]{1,0:T(8,128)(2,1)S(1)} collective-permute-done((bf16[104,128]{1,0:T(8,128)(2,1)S(1)}, bf16[104,128]{1,0:T(8,128)(2,1)S(1)}, u32[]{:S(2)}, u32[]{:S(2)}) %collective-permute-start.1) | collective-permute-done | bytes 26656 | tf_op jit(solution)/shard_map/ppermute | solution.py:493
  40.7 0.8 %shard_map.108 = (bf16[16,96,128]{2,1,0:T(8,128)(2,1)}, f32[1,128]{1,0:T(1,128)}, f32[1,128]{1,0:T(1,128)}) custom-call(bf16[104,128]{1,0:T(8,128)(2,1)S(1)} %shard_map.105.mine, bf16[104,128]{1,0:T(8,128)(2,1)S(1)} %collective-permute-done.1.other), custom_call_target="tpu_custom_call" | custom-call | bytes 447488 | tf_op jit(solution)/shard_map/pallas_call | solution.py:43
  41.4 7.7 %all-to-all-start.3 = ((bf16[16,96,128]{2,1,0:T(8,128)(2,1)}), bf16[16,96,128]{2,1,0:T(8,128)(2,1)S(1)}, u32[]{:S(2)}, u32[]{:S(2)}) async-start(bf16[16,96,128]{2,1,0:T(8,128)(2,1)} %get-tuple-element.44), calls=%async_computation.3 | async-start | bytes 786432 | tf_op jit(solution)/shard_map/all_to_all | solution.py:418
  49.2 0.0 collective-permute-done.2.halo
  49.2 1.0 %shard_map.107 = bf16[2,16,32,128]{3,2,1,0:T(8,128)(2,1)} custom-call(f32[2,16,32,128]{3,2,1,0:T(8,128)S(1)} %shard_map.106.part, bf16[2,16,32,128]{3,2,1,0:T(8,128)(2,1)S(1)} %collective-permute-done.2.halo, bf16[3,128,128]{2,1,0:T(8,128)(2,1)S(1)} %copy-done.1), custom_call_target="tpu_custom_call" | custom-call | flops 8589934592 | bytes 1146880 | tf_op jit(solution)/shard_map/pallas_call | solution.py:43
  50.1 7.1 %all-to-all-done.3 = bf16[16,96,128]{2,1,0:T(8,128)(2,1)S(1)} async-done(((bf16[16,96,128]{2,1,0:T(8,128)(2,1)}), bf16[16,96,128]{2,1,0:T(8,128)(2,1)S(1)}, u32[]{:S(2)}, u32[]{:S(2)}) %all-to-all-start.3) | async-done | bytes 393248 | tf_op jit(solution)/shard_map/all_to_all | solution.py:418
  57.2 0.9 %shard_map.109 = (f32[1152,128]{1,0:T(8,128)}, f32[384,128]{1,0:T(8,128)}) custom-call(bf16[1536,128]{1,0:T(8,128)(2,1)S(1)} %bitcast.11), custom_call_target="tpu_custom_call" | custom-call | bytes 1179648 | tf_op jit(solution)/shard_map/pallas_call | solution.py:43
  (1 shorter events, 0.0 us)
Async XLA Ops:
  0.6 4.0 %copy-start = (bf16[1,2,32,64,128]{4,3,2,1,0:T(8,128)(2,1)S(1)}, bf16[1,2,32,64,128]{4,3,2,1,0:T(8,128)(2,1)}, u32[]{:S(2)}) copy-start(bf16[1,2,32,64,128]{4,3,2,1,0:T(8,128)(2,1)} %param.6) | copy-start | bytes 3145732
  0.7 12.9 %collective-permute-start = (bf16[2,16,32,128]{3,2,1,0:T(8,128)(2,1)}, bf16[2,16,32,128]{3,2,1,0:T(8,128)(2,1)S(1)}, u32[]{:S(2)}, u32[]{:S(2)}) collective-permute-start(bf16[2,16,32,128]{3,2,1,0:T(8,128)(2,1)} %bitcast.13), channel_id=1, source_target_pairs={{1,0},{2,1},{3,2},{0,3},{5,4},{6,5},{7,6},{4,7},{9,8},{10,9},{11,1... | collective-permute-start | bytes 786440 | tf_op jit(solution)/shard_map/ppermute | solution.py:431
  4.7 8.9 %copy-start.1 = (bf16[3,128,128]{2,1,0:T(8,128)(2,1)S(1)}, bf16[3,128,128]{2,1,0:T(8,128)(2,1)}, u32[]{:S(2)}) copy-start(bf16[3,128,128]{2,1,0:T(8,128)(2,1)} %weights.5) | copy-start | bytes 294916
  4.7 8.9 %copy-start.2 = (bf16[1,2,16,32,128]{4,3,2,1,0:T(8,128)(2,1)S(1)}, bf16[1,2,16,32,128]{4,3,2,1,0:T(8,128)(2,1)}, u32[]{:S(2)}) copy-start(bf16[1,2,16,32,128]{4,3,2,1,0:T(8,128)(2,1)} %param.11) | copy-start | bytes 786436
  34.3 14.8 %collective-permute-start.2 = (bf16[2,16,32,128]{3,2,1,0:T(8,128)(2,1)S(1)}, bf16[2,16,32,128]{3,2,1,0:T(8,128)(2,1)S(1)}, u32[]{:S(2)}, u32[]{:S(2)}) collective-permute-start(bf16[2,16,32,128]{3,2,1,0:T(8,128)(2,1)S(1)} %get-tuple-element.42.act), channel_id=1, source_target_pairs={{0,1},{1,2},{2,3},{3,0},{4,5},{5,6},{6,7},{7,4},{8,9},{9,10},{10,1... | collective-permute-start | bytes 786440 | tf_op jit(solution)/shard_map/ppermute | solution.py:504
  35.7 5.0 %collective-permute-start.1 = (bf16[104,128]{1,0:T(8,128)(2,1)S(1)}, bf16[104,128]{1,0:T(8,128)(2,1)S(1)}, u32[]{:S(2)}, u32[]{:S(2)}) collective-permute-start(bf16[104,128]{1,0:T(8,128)(2,1)S(1)} %shard_map.105.mine), channel_id=1, source_target_pairs={{0,4},{1,5},{2,6},{3,7},{4,0},{5,1},{6,2},{7,3},{8,12},{9,13},{10,... | collective-permute-start | bytes 79880 | tf_op jit(solution)/shard_map/ppermute | solution.py:493
  41.4 15.8 %all-to-all-start.3 = ((bf16[16,96,128]{2,1,0:T(8,128)(2,1)}), bf16[16,96,128]{2,1,0:T(8,128)(2,1)S(1)}, u32[]{:S(2)}, u32[]{:S(2)}) async-start(bf16[16,96,128]{2,1,0:T(8,128)(2,1)} %get-tuple-element.44), calls=%async_computation.3 | async-start | bytes 786432 | tf_op jit(solution)/shard_map/all_to_all | solution.py:418

commit v12 on v10

--- a/solution.py
+++ b/solution.py
@@ -177,14 +177,34 @@
     return mean, lax.rsqrt(square / (cells * positions) + 1e-05)
 
 
-def act_kernel(
-    loss_scale, spatial, stats, cot, arrived, weights, params, act, normed, pre, temporal, sums,
-    halo,
-):
+def act_kernel(loss_scale, spatial, stats, params, act, normed, slope, scales):
     frames, out_rows, out_cols, channels = spatial.shape
     positions = frames * out_rows * out_cols
     mean, inv_std = clip_norm(stats, positions, channels // GROUPS)
     gain, shift = params[0:1], params[1:2]
+    row = lax.broadcasted_iota(jnp.int32, (8, channels), 0)
+    scales[...] = jnp.where(row == 0, inv_std, gain)
+    flat = (STEP_ROWS * out_cols, channels)
+    shaped = (STEP_ROWS, out_cols, channels)
+    for frame in range(frames):
+
+        def one(step, frame=frame):
+            rows = pl.ds(step * STEP_ROWS, STEP_ROWS)
+            norm = (spatial[frame, rows].reshape(flat) - mean) * inv_std
+            before = norm * gain + shift
+            sig = jax.nn.sigmoid(before)
+            act[frame, rows] = (before * sig).astype(jnp.bfloat16).reshape(shaped)
+            normed[frame, rows] = norm.reshape(shaped)
+            slope[frame, rows] = (loss_scale * sig * (1.0 + before * (1.0 - sig))).reshape(shaped)
+
+        each(out_rows // STEP_ROWS, one)
+
+
+def back_kernel(
+    loss_scale, cot, arrived, weights, scales, normed, slope, act, pre, temporal, sums, halo
+):
+    frames, out_rows, out_cols, channels = cot.shape
+    inv_std, gain = scales[0:1], scales[1:2]
     per_clip = sums.shape[0]
     not_last = lax.rem(lax.axis_index("seq"), per_clip) != per_clip - 1
     for frame in range(2):
@@ -201,22 +221,18 @@
 
     for frame in range(frames):
 
-        def cot_block(later, rows):
+        def cot_block(later, rows, shape, frame=frame):
             if frame + later < frames:
-                return cot[frame + later, rows].reshape(flat)
-            return halo[frame + later - frames, rows].reshape(flat)
-
-        def one(step, carry):
+                return cot[frame + later, rows].reshape(shape)
+            return halo[frame + later - frames, rows].reshape(shape)
+
+        def one(step, carry, frame=frame):
             rows = pl.ds(step * STEP_ROWS, STEP_ROWS)
-            norm = (spatial[frame, rows].reshape(flat) - mean) * inv_std
-            before = norm * gain + shift
-            sig = jax.nn.sigmoid(before)
-            act[frame, rows] = (before * sig).astype(jnp.bfloat16).reshape(shaped)
-            cots = jnp.concatenate([cot_block(later, rows) for later in range(3)], axis=1)
+            cots = jnp.concatenate([cot_block(later, rows, flat) for later in range(3)], axis=1)
             back = dot_transposed(cots, turned_weights)
             back = back.astype(jnp.bfloat16).astype(jnp.float32)
-            back_pre = back * loss_scale * sig * (1.0 + before * (1.0 - sig))
-            normed[frame, rows] = norm.reshape(shaped)
+            back_pre = back * slope[frame, rows].reshape(flat)
+            norm = normed[frame, rows].reshape(flat)
             pre[frame, rows] = (back_pre * (gain * inv_std)).reshape(shaped)
             return (carry[0] + fold(back_pre), carry[1] + fold(back_pre * norm))
 
@@ -408,7 +424,7 @@
 
     gate = pl.pallas_call(
         open_kernel,
-        out_shape=struct((8, channels), f32),
+        out_shape=pltpu.VMEM((8, channels), f32),
         out_specs=WHOLE,
         cost_estimate=pl.CostEstimate(
             flops=2 * positions * 9 * channels * channels,
@@ -448,20 +464,28 @@
         flops=2 * positions * 9 * channels * channels,
     )
     stats = exchange(stats, "seq", clips)
-    act, normed, pre, temporal, own = call(
+    act, normed, slope, scales = call(
         functools.partial(act_kernel, loss_scale),
         (
             struct(shape, bf16),
             struct(shape, f32),
             struct(shape, f32),
+            struct((8, channels), f32),
+        ),
+        (spatial, stats, params),
+    )
+    act_halo = lax.ppermute(act, "seq", ahead_pairs)
+    pre, temporal, own = call(
+        functools.partial(back_kernel, loss_scale),
+        (
+            struct(shape, f32),
             struct((3 * channels, channels), bf16),
             struct((per_clip, 8, channels), f32),
         ),
-        (spatial, stats, cot, cot_halo, w_temporal, params),
+        (cot, cot_halo, w_temporal, scales, normed, slope, act),
         scratch=[pltpu.VMEM((2,) + shape[1:], bf16)],
-        flops=2 * positions * 3 * channels * channels,
-    )
-    act_halo = lax.ppermute(act, "seq", ahead_pairs)
+        flops=2 * positions * 6 * channels * channels,
+    )
     sums = exchange(own, "seq", clips)
     halves = 2 if seq_size % 2 == 0 else 1
     half = seq_size // halves

time: 53.9 us -> 53.4 us (level)
  Pallas kernels: 7.31 us -> 6.75 us
    pallas_call x1, Pallas kernels: 0.6 us -> 0.01 us  [on_device(): pl.pallas_call(open_kernel, out_shape=pltpu.VMEM((8, channels), f32), out...]
    pallas_call x7 -> x8, Pallas kernels: 6.72 us -> 6.74 us  [call(): pl.pallas_call(kernel, out_shape=out_shape, in_specs=specs or [WHOLE] * l...]
  transfers between devices with their start and end apart: 3 -> 3, of which waited for: 1 -> 1; matrix products, arithmetic and copies ran while one was open for 0% -> 0% of each run, Pallas kernels for 5% -> 8%
where the time goes in v12:
time: 53.4 us; the launch traced here: 53.1 us
  blocking collectives  37.1 us (69%)
  starting transfers between devices  7.31 us (14%)
  Pallas kernels  6.75 us (13%)
  waiting for transfers between devices  1.2 us (2%)
  between operations  0.69 us (1%)
    all_to_all x4, blocking collectives, exchange(): lax.all_to_all(value, axes, 0, 0, axis_index_groups=groups, tiled=True)  37.1 us
    pallas_call x8, Pallas kernels, call(): pl.pallas_call(kernel, out_shape=out_shape, in_specs=specs or [WHOLE] * l...  6.74 us
    ppermute x1, starting transfers between devices, on_device(): cot_halo = lax.ppermute(cot_out, 'seq', back_pairs)  4 us
    ppermute x1, starting transfers between devices, on_device(): lax.ppermute(mine, 'seq', [(s, (s + half) % seq_size) for s in range(seq_...  2.65 us
    ppermute x1, waiting for transfers between devices, on_device(): lax.ppermute(mine, 'seq', [(s, (s + half) % seq_size) for s in range(seq_...  1.2 us
  transfers between devices with their start and end apart: 3, of which 1 were waited for; matrix products, arithmetic and copies ran while one was open for 0% of the time, Pallas kernels for 8%

profile of v12, /device:TPU:0, one launch (start us, length us, event | category | flops | bytes accessed | tf_op | source)
XLA Modules:
  0.0 53.1 jit_solution(16452873685113087290)
XLA Ops:
  0.6 0.0 copy-start
  0.7 4.0 %collective-permute-start = (bf16[2,16,32,128]{3,2,1,0:T(8,128)(2,1)}, bf16[2,16,32,128]{3,2,1,0:T(8,128)(2,1)S(1)}, u32[]{:S(2)}, u32[]{:S(2)}) collective-permute-start(bf16[2,16,32,128]{3,2,1,0:T(8,128)(2,1)} %bitcast.13), channel_id=1, source_target_pairs={{1,0},{2,1},{3,2},{0,3},{5,4},{6,5},{7,6},{4,7},{9,8},{10,9},{11,1... | collective-permute-start | bytes 786440 | tf_op jit(solution)/shard_map/ppermute | solution.py:436
  4.7 0.0 copy-done
  4.7 1.8 %shard_map.102 = (f32[2,16,32,128]{3,2,1,0:T(8,128)S(1)}, f32[4,8,128]{2,1,0:T(8,128)S(1)}, bf16[2,17,32,384]{3,2,1,0:T(8,128)(2,1)S(1)}, bf16[2,16,32,384]{3,2,1,0:T(8,128)(2,1)S(1)}, f32[8,128]{1,0:T(8,128)S(1)}) custom-call(f32[8,128]{1,0:T(8,128)S(1)} %shard_map.101.blank, bf16[2,32,64,128]{3,2,1,0:T(8,128)(2,1)S(1)} %bitcast.12, ...), custom_call_target="tpu_custom_call" | custom-call | flops 301989888 | bytes 3515392 | tf_op jit(solution)/shard_map/pallas_call | solution.py:43
  6.5 7.1 %all_to_all.20.stats = f32[4,8,128]{2,1,0:T(8,128)S(1)} all-to-all(f32[4,8,128]{2,1,0:T(8,128)S(1)} %get-tuple-element.34), channel_id=1, replica_groups={{0,1,2,3},{4,5,6,7},{8,9,10,11},{12,13,14,15},{16,17,18,19},{20,21,22,2..., dimensions={0} | all-to-all | bytes 32768 | tf_op jit(solution)/shard_map/all_to_all | solution.py:423
  13.5 0.0 copy-start.1
  13.5 0.0 copy-start.2
  13.5 0.9 %shard_map.103 = (bf16[2,16,32,128]{3,2,1,0:T(8,128)(2,1)S(1)}, f32[2,16,32,128]{3,2,1,0:T(8,128)S(1)}, f32[2,16,32,128]{3,2,1,0:T(8,128)S(1)}, f32[8,128]{1,0:T(8,128)S(1)}) custom-call(f32[2,16,32,128]{3,2,1,0:T(8,128)S(1)} %get-tuple-element.33.spatial, f32[4,8,128]{2,1,0:T(8,128)S(1)} %all_to_all.20.stats, f32[8,128]{1,0:T(8,128)S(1)} %get-tuple-element.35.params), custom_call_target="tpu_custom_call" | custom-call | bytes 1859584 | tf_op jit(solution)/shard_map/pallas_call | solution.py:43
  14.4 0.7 %collective-permute-start.1 = (bf16[2,16,32,128]{3,2,1,0:T(8,128)(2,1)S(1)}, bf16[2,16,32,128]{3,2,1,0:T(8,128)(2,1)S(1)}, u32[]{:S(2)}, u32[]{:S(2)}) collective-permute-start(bf16[2,16,32,128]{3,2,1,0:T(8,128)(2,1)S(1)} %get-tuple-element.46.act), channel_id=1, source_target_pairs={{0,1},{1,2},{2,3},{3,0},{4,5},{5,6},{6,7},{7,4},{8,9},{9,10},{10,1... | collective-permute-start | bytes 786440 | tf_op jit(solution)/shard_map/ppermute | solution.py:477
  15.0 0.0 collective-permute-done.arrived
  15.0 0.0 copy-done.1
  15.1 0.0 copy-done.2
  15.1 0.5 %shard_map.104 = (f32[2,16,32,128]{3,2,1,0:T(8,128)S(1)}, bf16[384,128]{1,0:T(8,128)(2,1)S(1)}, f32[4,8,128]{2,1,0:T(8,128)S(1)}) custom-call(bf16[2,16,32,128]{3,2,1,0:T(8,128)(2,1)S(1)} %bitcast.14, bf16[2,16,32,128]{3,2,1,0:T(8,128)(2,1)S(1)} %collective-permute-done.arrived, bf16[3,128,128]{2,1,0:T(8,128)(2,1)S(1)} %copy-done.1, ...), custom_call_target="tpu_custom_call" | custom-call | flops 201326592 | bytes 2576384 | tf_op jit(solution)/shard_map/pallas_call | solution.py:43
  15.6 8.1 %all_to_all.21.sums = f32[4,8,128]{2,1,0:T(8,128)S(1)} all-to-all(f32[4,8,128]{2,1,0:T(8,128)S(1)} %get-tuple-element.42), channel_id=1, replica_groups={{0,1,2,3},{4,5,6,7},{8,9,10,11},{12,13,14,15},{16,17,18,19},{20,21,22,2..., dimensions={0} | all-to-all | bytes 32768 | tf_op jit(solution)/shard_map/all_to_all | solution.py:423
  23.7 0.0 collective-permute-done.1.halo
  23.7 1.0 %shard_map.105 = bf16[16,104,128]{2,1,0:T(8,128)(2,1)S(1)} custom-call(bf16[2,17,32,384]{3,2,1,0:T(8,128)(2,1)S(1)} %get-tuple-element.31.odd, bf16[2,16,32,384]{3,2,1,0:T(8,128)(2,1)S(1)} %get-tuple-element.32.even, f32[2,16,32,128]{3,2,1,0:T(8,128)S(1)} %get-tuple-element.36.normed, f32[2,16,32,128]{3,2,1,0:T(8,128)S(1)} %get-tuple-element.41.pre, ...), custom_call_target="tpu_custom_call" | custom-call | flops 301989888 | bytes 3211264 | tf_op jit(solution)/shard_map/pallas_call | solution.py:43
  24.7 11.1 %all_to_all.22.arrived = bf16[16,104,128]{2,1,0:T(8,128)(2,1)S(1)} all-to-all(bf16[16,104,128]{2,1,0:T(8,128)(2,1)S(1)} %shard_map.105), channel_id=1, replica_groups={{0,1,2,3,8,9,10,11,16,17,18,19,24,25,26,27},{4,5,6,7,12,13,14,15,20,21,..., dimensions={0} | all-to-all | bytes 851968 | tf_op jit(solution)/shard_map/all_to_all | solution.py:423
  35.8 0.1 shard_map.106.mine
  35.8 2.7 %collective-permute-start.2 = (bf16[104,128]{1,0:T(8,128)(2,1)S(1)}, bf16[104,128]{1,0:T(8,128)(2,1)S(1)}, u32[]{:S(2)}, u32[]{:S(2)}) collective-permute-start(bf16[104,128]{1,0:T(8,128)(2,1)S(1)} %shard_map.106.mine), channel_id=1, source_target_pairs={{0,4},{1,5},{2,6},{3,7},{4,0},{5,1},{6,2},{7,3},{8,12},{9,13},{10,... | collective-permute-start | bytes 79880 | tf_op jit(solution)/shard_map/ppermute | solution.py:508
  38.5 1.1 %shard_map.107 = bf16[2,16,32,128]{3,2,1,0:T(8,128)(2,1)} custom-call(bf16[2,16,32,128]{3,2,1,0:T(8,128)(2,1)S(1)} %get-tuple-element.46.act, bf16[2,16,32,128]{3,2,1,0:T(8,128)(2,1)S(1)} %collective-permute-done.1.halo, bf16[3,128,128]{2,1,0:T(8,128)(2,1)S(1)} %copy-done.1), custom_call_target="tpu_custom_call" | custom-call | flops 100663296 | bytes 884736 | tf_op jit(solution)/shard_map/pallas_call | solution.py:43
  39.5 1.2 %collective-permute-done.2.other = bf16[104,128]{1,0:T(8,128)(2,1)S(1)} collective-permute-done((bf16[104,128]{1,0:T(8,128)(2,1)S(1)}, bf16[104,128]{1,0:T(8,128)(2,1)S(1)}, u32[]{:S(2)}, u32[]{:S(2)}) %collective-permute-start.2) | collective-permute-done | bytes 26656 | tf_op jit(solution)/shard_map/ppermute | solution.py:508
  40.7 0.5 shard_map.108
  41.3 10.9 %all_to_all.23 = bf16[16,96,128]{2,1,0:T(8,128)(2,1)S(1)} all-to-all(bf16[16,96,128]{2,1,0:T(8,128)(2,1)S(1)} %get-tuple-element.50), channel_id=1, replica_groups={{0,1,2,3,8,9,10,11,16,17,18,19,24,25,26,27},{4,5,6,7,12,13,14,15,20,21,..., dimensions={0} | all-to-all | bytes 786432 | tf_op jit(solution)/shard_map/all_to_all | solution.py:423
  52.2 0.9 %shard_map.109 = (f32[1152,128]{1,0:T(8,128)}, f32[384,128]{1,0:T(8,128)}) custom-call(bf16[1536,128]{1,0:T(8,128)(2,1)S(1)} %bitcast.11), custom_call_target="tpu_custom_call" | custom-call | bytes 1179648 | tf_op jit(solution)/shard_map/pallas_call | solution.py:43
  (1 shorter events, 0.0 us)
Async XLA Ops:
  0.6 4.0 %copy-start = (bf16[1,2,32,64,128]{4,3,2,1,0:T(8,128)(2,1)S(1)}, bf16[1,2,32,64,128]{4,3,2,1,0:T(8,128)(2,1)}, u32[]{:S(2)}) copy-start(bf16[1,2,32,64,128]{4,3,2,1,0:T(8,128)(2,1)} %param.6) | copy-start | bytes 3145732
  0.7 14.4 %collective-permute-start = (bf16[2,16,32,128]{3,2,1,0:T(8,128)(2,1)}, bf16[2,16,32,128]{3,2,1,0:T(8,128)(2,1)S(1)}, u32[]{:S(2)}, u32[]{:S(2)}) collective-permute-start(bf16[2,16,32,128]{3,2,1,0:T(8,128)(2,1)} %bitcast.13), channel_id=1, source_target_pairs={{1,0},{2,1},{3,2},{0,3},{5,4},{6,5},{7,6},{4,7},{9,8},{10,9},{11,1... | collective-permute-start | bytes 786440 | tf_op jit(solution)/shard_map/ppermute | solution.py:436
  13.5 1.5 %copy-start.1 = (bf16[3,128,128]{2,1,0:T(8,128)(2,1)S(1)}, bf16[3,128,128]{2,1,0:T(8,128)(2,1)}, u32[]{:S(2)}) copy-start(bf16[3,128,128]{2,1,0:T(8,128)(2,1)} %weights.3) | copy-start | bytes 294916
  13.5 1.5 %copy-start.2 = (bf16[1,2,16,32,128]{4,3,2,1,0:T(8,128)(2,1)S(1)}, bf16[1,2,16,32,128]{4,3,2,1,0:T(8,128)(2,1)}, u32[]{:S(2)}) copy-start(bf16[1,2,16,32,128]{4,3,2,1,0:T(8,128)(2,1)} %param.11) | copy-start | bytes 786436
  14.4 9.3 %collective-permute-start.1 = (bf16[2,16,32,128]{3,2,1,0:T(8,128)(2,1)S(1)}, bf16[2,16,32,128]{3,2,1,0:T(8,128)(2,1)S(1)}, u32[]{:S(2)}, u32[]{:S(2)}) collective-permute-start(bf16[2,16,32,128]{3,2,1,0:T(8,128)(2,1)S(1)} %get-tuple-element.46.act), channel_id=1, source_target_pairs={{0,1},{1,2},{2,3},{3,0},{4,5},{5,6},{6,7},{7,4},{8,9},{9,10},{10,1... | collective-permute-start | bytes 786440 | tf_op jit(solution)/shard_map/ppermute | solution.py:477
  35.8 4.9 %collective-permute-start.2 = (bf16[104,128]{1,0:T(8,128)(2,1)S(1)}, bf16[104,128]{1,0:T(8,128)(2,1)S(1)}, u32[]{:S(2)}, u32[]{:S(2)}) collective-permute-start(bf16[104,128]{1,0:T(8,128)(2,1)S(1)} %shard_map.106.mine), channel_id=1, source_target_pairs={{0,4},{1,5},{2,6},{3,7},{4,0},{5,1},{6,2},{7,3},{8,12},{9,13},{10,... | collective-permute-start | bytes 79880 | tf_op jit(solution)/shard_map/ppermute | solution.py:508

commit v13 on v12

--- a/solution.py
+++ b/solution.py
@@ -192,7 +192,7 @@
             rows = pl.ds(step * STEP_ROWS, STEP_ROWS)
             norm = (spatial[frame, rows].reshape(flat) - mean) * inv_std
             before = norm * gain + shift
-            sig = jax.nn.sigmoid(before)
+            sig = 0.5 + 0.5 * jnp.tanh(0.5 * before)
             act[frame, rows] = (before * sig).astype(jnp.bfloat16).reshape(shaped)
             normed[frame, rows] = norm.reshape(shaped)
             slope[frame, rows] = (loss_scale * sig * (1.0 + before * (1.0 - sig))).reshape(shaped)
@@ -329,8 +329,8 @@
             parts[tap] = term if parts[tap] is None else parts[tap] + term
     for tap in range(3):
         for side in range(3):
-            block = parts[tap][:, side * channels : (side + 1) * channels].T
-            store_rows(grads, rows, (3 * tap + side) * channels, block.astype(jnp.bfloat16))
+            block = parts[tap][:, side * channels : (side + 1) * channels].astype(jnp.bfloat16).T
+            store_rows(grads, rows, (3 * tap + side) * channels, block)
     for tap in range(3):
         block = temporal[pl.ds(tap * channels, channels)]
         store_rows(grads, rows, (9 + tap) * channels, block)
@@ -357,18 +357,20 @@
     chunk[pl.ds(count, EXTRA)] = split_rows(sums, EXTRA)
 
 
-def sum_kernel(mine, other, spread, grad_gain, grad_shift):
+def sum_kernel(mine, other, spread, totals):
     count = spread.shape[1]
     wide = [source[...].astype(jnp.float32) for source in (mine, other)]
     total = (wide[0][:count] + wide[1][:count]).astype(jnp.bfloat16)
     for slot in range(spread.shape[0]):
         spread[slot] = total
     sums = [join_rows(source[count:], 2) for source in wide]
-    grad_gain[...] = sums[0][0] + sums[1][0]
-    grad_shift[...] = sums[0][1] + sums[1][1]
-
-
-def final_kernel(arrived, grad_spatial, grad_temporal):
+    row = lax.broadcasted_iota(jnp.int32, totals.shape, 0)
+    totals[...] = jnp.where(row == 0, sums[0][0] + sums[1][0], sums[0][1] + sums[1][1])
+
+
+def final_kernel(arrived, totals, grad_spatial, grad_temporal, grad_gain, grad_shift):
+    grad_gain[...] = totals[0:1]
+    grad_shift[...] = totals[1:2]
     rows = grad_spatial.shape[0]
     grad_spatial[...] = arrived[pl.ds(0, rows)].astype(jnp.float32)
     grad_temporal[...] = arrived[pl.ds(rows, grad_temporal.shape[0])].astype(jnp.float32)
@@ -516,20 +518,21 @@
         flops=2 * positions * 3 * channels * channels,
     )
     other, encoded = lax.optimization_barrier((other, encoded))
-    grads, grad_gain, grad_shift = call(
+    grads, totals = call(
         sum_kernel,
+        (struct((count, rows, channels), bf16), struct((8, channels), f32)),
+        (mine, other),
+    )
+    grads = exchange(grads, ("dp", "seq"), near)
+    grad_spatial, grad_temporal, grad_gain, grad_shift = call(
+        final_kernel,
         (
-            struct((count, rows, channels), bf16),
+            struct((9 * channels, channels), f32),
+            struct((3 * channels, channels), f32),
             struct((1, channels), f32),
             struct((1, channels), f32),
         ),
-        (mine, other),
-    )
-    grads = exchange(grads, ("dp", "seq"), near)
-    grad_spatial, grad_temporal = call(
-        final_kernel,
-        (struct((9 * channels, channels), f32), struct((3 * channels, channels), f32)),
-        (grads.reshape(count * rows, channels),),
+        (grads.reshape(count * rows, channels), totals),
     )
     return (
         encoded[None],

time: 53.4 us -> 52.9 us (level)
  no operation moved by 1% of the time
where the time goes in v13:
time: 52.9 us; the launch traced here: 52.6 us
  blocking collectives  37.1 us (70%)
  starting transfers between devices  7.31 us (14%)
  Pallas kernels  6.27 us (12%)
  waiting for transfers between devices  1.21 us (2%)
  between operations  0.69 us (1%)
    all_to_all x4, blocking collectives, exchange(): lax.all_to_all(value, axes, 0, 0, axis_index_groups=groups, tiled=True)  37.1 us
    pallas_call x8, Pallas kernels, call(): pl.pallas_call(kernel, out_shape=out_shape, in_specs=specs or [WHOLE] * l...  6.27 us
    ppermute x1, starting transfers between devices, on_device(): cot_halo = lax.ppermute(cot_out, 'seq', back_pairs)  4 us
    ppermute x1, starting transfers between devices, on_device(): lax.ppermute(mine, 'seq', [(s, (s + half) % seq_size) for s in range(seq_...  2.65 us
    ppermute x1, waiting for transfers between devices, on_device(): lax.ppermute(mine, 'seq', [(s, (s + half) % seq_size) for s in range(seq_...  1.2 us
  transfers between devices with their start and end apart: 3, of which 1 were waited for; matrix products, arithmetic and copies ran while one was open for 0% of the time, Pallas kernels for 8%

profile of v13, /device:TPU:0, one launch (start us, length us, event | category | flops | bytes accessed | tf_op | source)
XLA Modules:
  0.0 52.6 jit_solution(7702294074419249250)
XLA Ops:
  0.6 0.0 copy-start
  0.7 4.0 %collective-permute-start = (bf16[2,16,32,128]{3,2,1,0:T(8,128)(2,1)}, bf16[2,16,32,128]{3,2,1,0:T(8,128)(2,1)S(1)}, u32[]{:S(2)}, u32[]{:S(2)}) collective-permute-start(bf16[2,16,32,128]{3,2,1,0:T(8,128)(2,1)} %bitcast.13), channel_id=1, source_target_pairs={{1,0},{2,1},{3,2},{0,3},{5,4},{6,5},{7,6},{4,7},{9,8},{10,9},{11,1... | collective-permute-start | bytes 786440 | tf_op jit(solution)/shard_map/ppermute | solution.py:438
  4.7 0.0 copy-done
  4.7 1.8 %shard_map.102 = (f32[2,16,32,128]{3,2,1,0:T(8,128)S(1)}, f32[4,8,128]{2,1,0:T(8,128)S(1)}, bf16[2,17,32,384]{3,2,1,0:T(8,128)(2,1)S(1)}, bf16[2,16,32,384]{3,2,1,0:T(8,128)(2,1)S(1)}, f32[8,128]{1,0:T(8,128)S(1)}) custom-call(f32[8,128]{1,0:T(8,128)S(1)} %shard_map.101.blank, bf16[2,32,64,128]{3,2,1,0:T(8,128)(2,1)S(1)} %bitcast.12, ...), custom_call_target="tpu_custom_call" | custom-call | flops 301989888 | bytes 3515392 | tf_op jit(solution)/shard_map/pallas_call | solution.py:43
  6.5 7.1 %all_to_all.20.stats = f32[4,8,128]{2,1,0:T(8,128)S(1)} all-to-all(f32[4,8,128]{2,1,0:T(8,128)S(1)} %get-tuple-element.35), channel_id=1, replica_groups={{0,1,2,3},{4,5,6,7},{8,9,10,11},{12,13,14,15},{16,17,18,19},{20,21,22,2..., dimensions={0} | all-to-all | bytes 32768 | tf_op jit(solution)/shard_map/all_to_all | solution.py:425
  13.5 0.0 copy-start.1
  13.5 0.0 copy-start.2
  13.5 0.9 %shard_map.103 = (bf16[2,16,32,128]{3,2,1,0:T(8,128)(2,1)S(1)}, f32[2,16,32,128]{3,2,1,0:T(8,128)S(1)}, f32[2,16,32,128]{3,2,1,0:T(8,128)S(1)}, f32[8,128]{1,0:T(8,128)S(1)}) custom-call(f32[2,16,32,128]{3,2,1,0:T(8,128)S(1)} %get-tuple-element.34.spatial, f32[4,8,128]{2,1,0:T(8,128)S(1)} %all_to_all.20.stats, f32[8,128]{1,0:T(8,128)S(1)} %get-tuple-element.36.params), custom_call_target="tpu_custom_call" | custom-call | bytes 1859584 | tf_op jit(solution)/shard_map/pallas_call | solution.py:43
  14.4 0.7 %collective-permute-start.1 = (bf16[2,16,32,128]{3,2,1,0:T(8,128)(2,1)S(1)}, bf16[2,16,32,128]{3,2,1,0:T(8,128)(2,1)S(1)}, u32[]{:S(2)}, u32[]{:S(2)}) collective-permute-start(bf16[2,16,32,128]{3,2,1,0:T(8,128)(2,1)S(1)} %get-tuple-element.47.act), channel_id=1, source_target_pairs={{0,1},{1,2},{2,3},{3,0},{4,5},{5,6},{6,7},{7,4},{8,9},{9,10},{10,1... | collective-permute-start | bytes 786440 | tf_op jit(solution)/shard_map/ppermute | solution.py:479
  15.0 0.0 collective-permute-done.arrived
  15.0 0.0 copy-done.1
  15.1 0.0 copy-done.2
  15.1 0.5 %shard_map.104 = (f32[2,16,32,128]{3,2,1,0:T(8,128)S(1)}, bf16[384,128]{1,0:T(8,128)(2,1)S(1)}, f32[4,8,128]{2,1,0:T(8,128)S(1)}) custom-call(bf16[2,16,32,128]{3,2,1,0:T(8,128)(2,1)S(1)} %bitcast.14, bf16[2,16,32,128]{3,2,1,0:T(8,128)(2,1)S(1)} %collective-permute-done.arrived, bf16[3,128,128]{2,1,0:T(8,128)(2,1)S(1)} %copy-done.1, ...), custom_call_target="tpu_custom_call" | custom-call | flops 201326592 | bytes 2576384 | tf_op jit(solution)/shard_map/pallas_call | solution.py:43
  15.6 8.1 %all_to_all.21.sums = f32[4,8,128]{2,1,0:T(8,128)S(1)} all-to-all(f32[4,8,128]{2,1,0:T(8,128)S(1)} %get-tuple-element.43), channel_id=1, replica_groups={{0,1,2,3},{4,5,6,7},{8,9,10,11},{12,13,14,15},{16,17,18,19},{20,21,22,2..., dimensions={0} | all-to-all | bytes 32768 | tf_op jit(solution)/shard_map/all_to_all | solution.py:425
  23.7 0.0 collective-permute-done.1.halo
  23.7 1.0 %shard_map.105 = bf16[16,104,128]{2,1,0:T(8,128)(2,1)S(1)} custom-call(bf16[2,17,32,384]{3,2,1,0:T(8,128)(2,1)S(1)} %get-tuple-element.32.odd, bf16[2,16,32,384]{3,2,1,0:T(8,128)(2,1)S(1)} %get-tuple-element.33.even, f32[2,16,32,128]{3,2,1,0:T(8,128)S(1)} %get-tuple-element.37.normed, f32[2,16,32,128]{3,2,1,0:T(8,128)S(1)} %get-tuple-element.42.pre, ...), custom_call_target="tpu_custom_call" | custom-call | flops 301989888 | bytes 3211264 | tf_op jit(solution)/shard_map/pallas_call | solution.py:43
  24.7 11.0 %all_to_all.22.arrived = bf16[16,104,128]{2,1,0:T(8,128)(2,1)S(1)} all-to-all(bf16[16,104,128]{2,1,0:T(8,128)(2,1)S(1)} %shard_map.105), channel_id=1, replica_groups={{0,1,2,3,8,9,10,11,16,17,18,19,24,25,26,27},{4,5,6,7,12,13,14,15,20,21,..., dimensions={0} | all-to-all | bytes 851968 | tf_op jit(solution)/shard_map/all_to_all | solution.py:425
  35.7 0.1 shard_map.106.mine
  35.8 2.6 %collective-permute-start.2 = (bf16[104,128]{1,0:T(8,128)(2,1)S(1)}, bf16[104,128]{1,0:T(8,128)(2,1)S(1)}, u32[]{:S(2)}, u32[]{:S(2)}) collective-permute-start(bf16[104,128]{1,0:T(8,128)(2,1)S(1)} %shard_map.106.mine), channel_id=1, source_target_pairs={{0,4},{1,5},{2,6},{3,7},{4,0},{5,1},{6,2},{7,3},{8,12},{9,13},{10,... | collective-permute-start | bytes 79880 | tf_op jit(solution)/shard_map/ppermute | solution.py:510
  38.5 1.1 %shard_map.107 = bf16[2,16,32,128]{3,2,1,0:T(8,128)(2,1)} custom-call(bf16[2,16,32,128]{3,2,1,0:T(8,128)(2,1)S(1)} %get-tuple-element.47.act, bf16[2,16,32,128]{3,2,1,0:T(8,128)(2,1)S(1)} %collective-permute-done.1.halo, bf16[3,128,128]{2,1,0:T(8,128)(2,1)S(1)} %copy-done.1), custom_call_target="tpu_custom_call" | custom-call | flops 100663296 | bytes 884736 | tf_op jit(solution)/shard_map/pallas_call | solution.py:43
  39.5 1.2 %collective-permute-done.2.other = bf16[104,128]{1,0:T(8,128)(2,1)S(1)} collective-permute-done((bf16[104,128]{1,0:T(8,128)(2,1)S(1)}, bf16[104,128]{1,0:T(8,128)(2,1)S(1)}, u32[]{:S(2)}, u32[]{:S(2)}) %collective-permute-start.2) | collective-permute-done | bytes 26656 | tf_op jit(solution)/shard_map/ppermute | solution.py:510
  40.8 10.9 %all_to_all.23 = bf16[16,96,128]{2,1,0:T(8,128)(2,1)S(1)} all-to-all(bf16[16,96,128]{2,1,0:T(8,128)(2,1)S(1)} %get-tuple-element.51), channel_id=1, replica_groups={{0,1,2,3,8,9,10,11,16,17,18,19,24,25,26,27},{4,5,6,7,12,13,14,15,20,21,..., dimensions={0} | all-to-all | bytes 786432 | tf_op jit(solution)/shard_map/all_to_all | solution.py:425
  51.7 0.9 %shard_map.109 = (f32[1152,128]{1,0:T(8,128)}, f32[384,128]{1,0:T(8,128)}, f32[1,128]{1,0:T(1,128)}, f32[1,128]{1,0:T(1,128)}) custom-call(bf16[1536,128]{1,0:T(8,128)(2,1)S(1)} %bitcast.11, f32[8,128]{1,0:T(8,128)S(1)} %get-tuple-element.52.totals), custom_call_target="tpu_custom_call" | custom-call | bytes 1184768 | tf_op jit(solution)/shard_map/pallas_call | solution.py:43
  (2 shorter events, 0.0 us)
Async XLA Ops:
  0.6 4.0 %copy-start = (bf16[1,2,32,64,128]{4,3,2,1,0:T(8,128)(2,1)S(1)}, bf16[1,2,32,64,128]{4,3,2,1,0:T(8,128)(2,1)}, u32[]{:S(2)}) copy-start(bf16[1,2,32,64,128]{4,3,2,1,0:T(8,128)(2,1)} %param.6) | copy-start | bytes 3145732
  0.7 14.4 %collective-permute-start = (bf16[2,16,32,128]{3,2,1,0:T(8,128)(2,1)}, bf16[2,16,32,128]{3,2,1,0:T(8,128)(2,1)S(1)}, u32[]{:S(2)}, u32[]{:S(2)}) collective-permute-start(bf16[2,16,32,128]{3,2,1,0:T(8,128)(2,1)} %bitcast.13), channel_id=1, source_target_pairs={{1,0},{2,1},{3,2},{0,3},{5,4},{6,5},{7,6},{4,7},{9,8},{10,9},{11,1... | collective-permute-start | bytes 786440 | tf_op jit(solution)/shard_map/ppermute | solution.py:438
  13.5 1.5 %copy-start.1 = (bf16[3,128,128]{2,1,0:T(8,128)(2,1)S(1)}, bf16[3,128,128]{2,1,0:T(8,128)(2,1)}, u32[]{:S(2)}) copy-start(bf16[3,128,128]{2,1,0:T(8,128)(2,1)} %weights.3) | copy-start | bytes 294916
  13.5 1.5 %copy-start.2 = (bf16[1,2,16,32,128]{4,3,2,1,0:T(8,128)(2,1)S(1)}, bf16[1,2,16,32,128]{4,3,2,1,0:T(8,128)(2,1)}, u32[]{:S(2)}) copy-start(bf16[1,2,16,32,128]{4,3,2,1,0:T(8,128)(2,1)} %param.11) | copy-start | bytes 786436
  14.4 9.3 %collective-permute-start.1 = (bf16[2,16,32,128]{3,2,1,0:T(8,128)(2,1)S(1)}, bf16[2,16,32,128]{3,2,1,0:T(8,128)(2,1)S(1)}, u32[]{:S(2)}, u32[]{:S(2)}) collective-permute-start(bf16[2,16,32,128]{3,2,1,0:T(8,128)(2,1)S(1)} %get-tuple-element.47.act), channel_id=1, source_target_pairs={{0,1},{1,2},{2,3},{3,0},{4,5},{5,6},{6,7},{7,4},{8,9},{9,10},{10,1... | collective-permute-start | bytes 786440 | tf_op jit(solution)/shard_map/ppermute | solution.py:479
  35.8 4.9 %collective-permute-start.2 = (bf16[104,128]{1,0:T(8,128)(2,1)S(1)}, bf16[104,128]{1,0:T(8,128)(2,1)S(1)}, u32[]{:S(2)}, u32[]{:S(2)}) collective-permute-start(bf16[104,128]{1,0:T(8,128)(2,1)S(1)} %shard_map.106.mine), channel_id=1, source_target_pairs={{0,4},{1,5},{2,6},{3,7},{4,0},{5,1},{6,2},{7,3},{8,12},{9,13},{10,... | collective-permute-start | bytes 79880 | tf_op jit(solution)/shard_map/ppermute | solution.py:510

commit v14 on v13

--- a/solution.py
+++ b/solution.py
@@ -36,7 +36,7 @@
         lax.fori_loop(0, count, lambda step, carry: (body(step), carry)[1], 0)
 
 
-def call(kernel, out_shape, operands, specs=None, scratch=(), flops=0):
+def call(kernel, out_shape, operands, specs=None, scratch=(), flops=0, outs=WHOLE):
     sizes = [value.size * value.dtype.itemsize for value in operands]
     sizes += [value.size * value.dtype.itemsize for value in jax.tree.leaves(out_shape)]
     held = sum(math.prod(item.shape) * 4 for item in scratch if hasattr(item, "shape"))
@@ -44,7 +44,7 @@
         kernel,
         out_shape=out_shape,
         in_specs=specs or [WHOLE] * len(operands),
-        out_specs=jax.tree.map(lambda _: WHOLE, out_shape),
+        out_specs=jax.tree.map(lambda _: outs, out_shape),
         scratch_shapes=list(scratch),
         compiler_params=pltpu.CompilerParams(vmem_limit_bytes=sum(sizes) + held + SPARE_BYTES),
         cost_estimate=pl.CostEstimate(
@@ -55,17 +55,14 @@
 
 def group_spread(values, lanes):
     channels = values.shape[-1]
-    shift = 1
-    while shift < lanes:
-        values = values + pltpu.roll(values, channels - shift, 1)
-        shift *= 2
-    lane = lax.broadcasted_iota(jnp.int32, values.shape, 1)
-    values = jnp.where(lax.rem(lane, lanes) == 0, values, 0.0)
-    shift = 1
-    while shift < lanes:
-        values = values + pltpu.roll(values, shift, 1)
-        shift *= 2
-    return values
+    place = lax.rem(lax.broadcasted_iota(jnp.int32, values.shape, 1), lanes)
+    total = values
+    for shift in range(1, lanes):
+        ahead = pltpu.roll(values, channels - shift, 1)
+        behind = pltpu.roll(values, shift, 1)
+        total += jnp.where(place < lanes - shift, ahead, 0.0)
+        total += jnp.where(place >= shift, behind, 0.0)
+    return total
 
 
 def open_kernel(gate):
@@ -73,7 +70,7 @@
 
 
 def conv_kernel(
-    pieces, blank, video, weights_far, gain_far, shift_far, spatial, stats, odd, even, params, wide,
+    pieces, blank, video, weights_far, gain_far, shift_far, spatial, stats, patches, params, wide,
     weights, arrived,
 ):
     frames, height, width, channels = video.shape
@@ -92,8 +89,10 @@
     for slot in range(wide.shape[0]):
         wide[slot, 0:8] = jnp.zeros((8, channels), jnp.float32)
     for frame in range(frames):
-        odd[frame, 0] = jnp.zeros((out_cols, 3 * channels), jnp.bfloat16)
-    flat = (STEP_ROWS * out_cols, 3 * channels)
+        patches[frame, 0, :, 0 : 3 * channels] = jnp.zeros(
+            (out_cols, 3 * channels), jnp.bfloat16
+        )
+    flat = (STEP_ROWS * out_cols, 9 * channels)
     steps = half // 2 // STEP_ROWS
 
     def place(piece, step):
@@ -105,19 +104,26 @@
         for line in range(2 * STEP_ROWS):
             wide[base + line, 8 : 8 + width] = video[frame, 2 * first + line].astype(jnp.float32)
         for line in range(2 * STEP_ROWS):
+            row = first + line // 2
+
+            def put(row, block, value):
+                patches[frame, row, :, block * channels : (block + 1) * channels] = value
+
             for tap in range(3):
                 value = wide[base + line, pl.ds(7 + tap, out_cols, stride=2), :]
-                lanes = slice(tap * channels, (tap + 1) * channels)
-                if line % 2:
-                    odd[frame, first + line // 2 + 1, :, lanes] = value.astype(jnp.bfloat16)
-                else:
-                    even[frame, first + line // 2, :, lanes] = value.astype(jnp.bfloat16)
+                value = value.astype(jnp.bfloat16)
+                if line % 2 == 0:
+                    put(row, 3 + tap, value)
+                    continue
+                put(row, 6 + tap, value)
+                if not isinstance(row, int):
+                    pl.when(row + 1 < out_rows)(functools.partial(put, row + 1, tap, value))
+                elif row + 1 < out_rows:
+                    put(row + 1, tap, value)
 
     def multiply(piece, step):
         frame, first = place(piece, step)
-        total = dot(odd[frame, pl.ds(first, STEP_ROWS)].reshape(flat), weights[0])
-        total += dot(even[frame, pl.ds(first, STEP_ROWS)].reshape(flat), weights[1])
-        total += dot(odd[frame, pl.ds(first + 1, STEP_ROWS)].reshape(flat), weights[2])
+        total = dot(patches[frame, pl.ds(first, STEP_ROWS)].reshape(flat), weights[...])
         spatial[frame, pl.ds(first, STEP_ROWS)] = total.reshape(STEP_ROWS, out_cols, channels)
         return total
 
@@ -303,9 +309,7 @@
         done += count
 
 
-def grad_kernel(
-    odd, even, normed, pre, sums, temporal, grads
-):
+def grad_kernel(patches, normed, pre, sums, temporal, grads):
     frames, out_rows, out_cols, channels = normed.shape
     lanes = channels // GROUPS
     members = sums.shape[0] * frames * out_rows * out_cols * lanes
@@ -314,23 +318,21 @@
     group = group_spread(clip, lanes) * inv_std / members
     group_shift, group_gain = group[2:3], group[3:4]
     flat = (out_rows * out_cols, channels)
-    flat_wide = (out_rows * out_cols, 3 * channels)
     rows = grads.shape[1] - EXTRA
-    parts = [None, None, None]
+    backs = []
     for frame in range(frames):
         back = (
             pre[frame].reshape(flat) - group_shift - normed[frame].reshape(flat) * group_gain
         )
-        back = back.astype(jnp.bfloat16).T
-        for tap, source in enumerate(
-            (odd.at[frame, pl.ds(0, out_rows)], even.at[frame], odd.at[frame, pl.ds(1, out_rows)])
-        ):
-            term = dot(back, source[...].reshape(flat_wide))
-            parts[tap] = term if parts[tap] is None else parts[tap] + term
-    for tap in range(3):
-        for side in range(3):
-            block = parts[tap][:, side * channels : (side + 1) * channels].astype(jnp.bfloat16).T
-            store_rows(grads, rows, (3 * tap + side) * channels, block)
+        backs.append(back.astype(jnp.bfloat16).T)
+    backs = jnp.concatenate(backs, axis=1)
+    for first in range(0, 9, 2):
+        lanes = slice(first * channels, min(first + 2, 9) * channels)
+        source = patches[:, :, :, lanes].reshape(frames * out_rows * out_cols, -1)
+        part = dot(backs, source)
+        for side in range(part.shape[1] // channels):
+            block = part[:, side * channels : (side + 1) * channels].astype(jnp.bfloat16).T
+            store_rows(grads, rows, (first + side) * channels, block)
     for tap in range(3):
         block = temporal[pl.ds(tap * channels, channels)]
         store_rows(grads, rows, (9 + tap) * channels, block)
@@ -368,12 +370,26 @@
     totals[...] = jnp.where(row == 0, sums[0][0] + sums[1][0], sums[0][1] + sums[1][1])
 
 
-def final_kernel(arrived, totals, grad_spatial, grad_temporal, grad_gain, grad_shift):
-    grad_gain[...] = totals[0:1]
-    grad_shift[...] = totals[1:2]
-    rows = grad_spatial.shape[0]
-    grad_spatial[...] = arrived[pl.ds(0, rows)].astype(jnp.float32)
-    grad_temporal[...] = arrived[pl.ds(rows, grad_temporal.shape[0])].astype(jnp.float32)
+def final_kernel(
+    arrived, totals, grad_spatial, grad_temporal, grad_gain, grad_shift, held, row_sums, done
+):
+    channels = arrived.shape[1]
+    row_sums[...] = totals[...]
+    copies = [
+        pltpu.make_async_copy(row_sums.at[0:1], grad_gain, done.at[0]),
+        pltpu.make_async_copy(row_sums.at[1:2], grad_shift, done.at[1]),
+    ]
+    for copy in copies:
+        copy.start()
+    piece = 3 * channels
+    for index in range(4):
+        rows = pl.ds(index * piece, piece)
+        held[rows] = arrived[rows].astype(jnp.float32)
+        target = grad_temporal if index == 3 else grad_spatial.at[rows]
+        copies.append(pltpu.make_async_copy(held.at[rows], target, done.at[2 + index]))
+        copies[-1].start()
+    for copy in copies:
+        copy.wait()
 
 
 def encode_kernel(per_clip, act, halo, weights, encoded):
@@ -441,26 +457,25 @@
     def far(value):
         return pltpu.with_memory_space_constraint(value, pltpu.HBM)
 
-    spatial, stats, odd, even, params = call(
+    spatial, stats, patches, params = call(
         functools.partial(conv_kernel, pieces),
         (
             struct(shape, f32),
             struct((per_clip, 8, channels), f32),
-            struct((frames, out_rows + 1, out_cols, 3 * channels), bf16),
-            struct((frames, out_rows, out_cols, 3 * channels), bf16),
+            struct((frames, out_rows, out_cols, 9 * channels), bf16),
             struct((8, channels), f32),
         ),
         (
             gate,
             video,
-            far(w_spatial.reshape(3, 3 * channels, channels)),
+            far(w_spatial.reshape(9 * channels, channels)),
             far(norm_gain[None]),
             far(norm_shift[None]),
         ),
         specs=[WHOLE] * 2 + [FAR] * 3,
         scratch=[
             pltpu.VMEM((4 * STEP_ROWS, 8 + width, channels), f32),
-            pltpu.VMEM((3, 3 * channels, channels), bf16),
+            pltpu.VMEM((9 * channels, channels), bf16),
             pltpu.SemaphoreType.DMA((3,)),
         ],
         flops=2 * positions * 9 * channels * channels,
@@ -501,7 +516,7 @@
     grads = call(
         grad_kernel,
         struct((count, rows + EXTRA, channels), bf16),
-        (odd, even, normed, pre, sums, temporal),
+        (patches, normed, pre, sums, temporal),
         flops=2 * positions * 9 * channels * channels,
     )
     grads = exchange(grads, ("dp", "seq"), near)
@@ -533,6 +548,12 @@
             struct((1, channels), f32),
         ),
         (grads.reshape(count * rows, channels), totals),
+        outs=FAR,
+        scratch=[
+            pltpu.VMEM((12 * channels, channels), f32),
+            pltpu.VMEM((8, channels), f32),
+            pltpu.SemaphoreType.DMA((6,)),
+        ],
     )
     return (
         encoded[None],

time: 52.9 us -> 53.5 us (1.011)
  local copies, waits for them, and re-layouts: 0.01 us -> 1.23 us
  Pallas kernels: 6.27 us -> 5.56 us
    unnamed x6, local copies, waits for them, and re-layouts: 0.01 us -> 1.23 us
    pallas_call x8, Pallas kernels: 6.27 us -> 5.56 us  [call(): pl.pallas_call(kernel, out_shape=out_shape, in_specs=specs or [WHOLE] * l...]
  transfers between devices with their start and end apart: 3 -> 3, of which waited for: 1 -> 1; matrix products, arithmetic and copies ran while one was open for 0% -> 0% of each run, Pallas kernels for 8% -> 7%
where the time goes in v14:
time: 53.5 us; the launch traced here: 53.2 us
  blocking collectives  37.1 us (69%)
  starting transfers between devices  7.31 us (14%)
  Pallas kernels  5.56 us (10%)
  local copies, waits for them, and re-layouts  1.23 us (2%)
  waiting for transfers between devices  1.21 us (2%)
  between operations  0.7 us (1%)
    all_to_all x4, blocking collectives, exchange(): lax.all_to_all(value, axes, 0, 0, axis_index_groups=groups, tiled=True)  37.1 us
    pallas_call x8, Pallas kernels, call(): pl.pallas_call(kernel, out_shape=out_shape, in_specs=specs or [WHOLE] * l...  5.56 us
    ppermute x1, starting transfers between devices, on_device(): cot_halo = lax.ppermute(cot_out, 'seq', back_pairs)  4 us
    ppermute x1, starting transfers between devices, on_device(): lax.ppermute(mine, 'seq', [(s, (s + half) % seq_size) for s in range(seq_...  2.65 us
    unnamed x6, local copies, waits for them, and re-layouts  1.23 us
    ppermute x1, waiting for transfers between devices, on_device(): lax.ppermute(mine, 'seq', [(s, (s + half) % seq_size) for s in range(seq_...  1.2 us
  transfers between devices with their start and end apart: 3, of which 1 were waited for; matrix products, arithmetic and copies ran while one was open for 0% of the time, Pallas kernels for 7%

profile of v14, /device:TPU:0, one launch (start us, length us, event | category | flops | bytes accessed | tf_op | source)
XLA Modules:
  0.0 53.2 jit_solution(4701267485777239718)
XLA Ops:
  0.6 0.0 copy-start.2
  0.6 0.0 copy-start.1
  0.7 4.0 %collective-permute-start = (bf16[2,16,32,128]{3,2,1,0:T(8,128)(2,1)}, bf16[2,16,32,128]{3,2,1,0:T(8,128)(2,1)S(1)}, u32[]{:S(2)}, u32[]{:S(2)}) collective-permute-start(bf16[2,16,32,128]{3,2,1,0:T(8,128)(2,1)} %bitcast.13), channel_id=1, source_target_pairs={{1,0},{2,1},{3,2},{0,3},{5,4},{6,5},{7,6},{4,7},{9,8},{10,9},{11,1... | collective-permute-start | bytes 786440 | tf_op jit(solution)/shard_map/ppermute | solution.py:454
  4.7 0.0 copy-start
  4.7 1.2 %copy-done = bf16[1,2,32,64,128]{4,3,2,1,0:T(8,128)(2,1)S(1)} copy-done((bf16[1,2,32,64,128]{4,3,2,1,0:T(8,128)(2,1)S(1)}, bf16[1,2,32,64,128]{4,3,2,1,0:T(8,128)(2,1)}, u32[]{:S(2)}) %copy-start) | copy-done | bytes 1048600
  5.9 1.8 %shard_map.102 = (f32[2,16,32,128]{3,2,1,0:T(8,128)S(1)}, f32[4,8,128]{2,1,0:T(8,128)S(1)}, bf16[2,16,32,1152]{3,2,1,0:T(8,128)(2,1)S(1)}, f32[8,128]{1,0:T(8,128)S(1)}) custom-call(f32[8,128]{1,0:T(8,128)S(1)} %shard_map.101.blank, bf16[2,32,64,128]{3,2,1,0:T(8,128)(2,1)S(1)} %bitcast.12, bf16[1152,128]{1,0:T(8,128)(2,1)} %bitcast.15, f32[1,128]{1,0:T(1,128)} %bitcast.17, ...), custom_call_target="tpu_custom_call" | custom-call | flops 301989888 | bytes 4252672 | tf_op jit(solution)/shard_map/pallas_call | solution.py:43
  7.7 7.1 %all_to_all.20.stats = f32[4,8,128]{2,1,0:T(8,128)S(1)} all-to-all(f32[4,8,128]{2,1,0:T(8,128)S(1)} %get-tuple-element.33), channel_id=1, replica_groups={{0,1,2,3},{4,5,6,7},{8,9,10,11},{12,13,14,15},{16,17,18,19},{20,21,22,2..., dimensions={0} | all-to-all | bytes 32768 | tf_op jit(solution)/shard_map/all_to_all | solution.py:441
  14.7 0.4 shard_map.103
  15.2 0.7 %collective-permute-start.1 = (bf16[2,16,32,128]{3,2,1,0:T(8,128)(2,1)S(1)}, bf16[2,16,32,128]{3,2,1,0:T(8,128)(2,1)S(1)}, u32[]{:S(2)}, u32[]{:S(2)}) collective-permute-start(bf16[2,16,32,128]{3,2,1,0:T(8,128)(2,1)S(1)} %get-tuple-element.45.act), channel_id=1, source_target_pairs={{0,1},{1,2},{2,3},{3,0},{4,5},{5,6},{6,7},{7,4},{8,9},{9,10},{10,1... | collective-permute-start | bytes 786440 | tf_op jit(solution)/shard_map/ppermute | solution.py:494
  15.9 0.0 collective-permute-done.arrived
  15.9 0.0 copy-done.2
  15.9 0.0 copy-done.1
  15.9 0.5 %shard_map.104 = (f32[2,16,32,128]{3,2,1,0:T(8,128)S(1)}, bf16[384,128]{1,0:T(8,128)(2,1)S(1)}, f32[4,8,128]{2,1,0:T(8,128)S(1)}) custom-call(bf16[2,16,32,128]{3,2,1,0:T(8,128)(2,1)S(1)} %bitcast.14, bf16[2,16,32,128]{3,2,1,0:T(8,128)(2,1)S(1)} %collective-permute-done.arrived, bf16[3,128,128]{2,1,0:T(8,128)(2,1)S(1)} %copy-done.1, ...), custom_call_target="tpu_custom_call" | custom-call | flops 201326592 | bytes 2576384 | tf_op jit(solution)/shard_map/pallas_call | solution.py:43
  16.4 8.1 %all_to_all.21.sums = f32[4,8,128]{2,1,0:T(8,128)S(1)} all-to-all(f32[4,8,128]{2,1,0:T(8,128)S(1)} %get-tuple-element.41), channel_id=1, replica_groups={{0,1,2,3},{4,5,6,7},{8,9,10,11},{12,13,14,15},{16,17,18,19},{20,21,22,2..., dimensions={0} | all-to-all | bytes 32768 | tf_op jit(solution)/shard_map/all_to_all | solution.py:441
  24.5 0.0 collective-permute-done.1.halo
  24.5 0.7 %shard_map.105 = bf16[16,104,128]{2,1,0:T(8,128)(2,1)S(1)} custom-call(bf16[2,16,32,1152]{3,2,1,0:T(8,128)(2,1)S(1)} %get-tuple-element.31.patches, f32[2,16,32,128]{3,2,1,0:T(8,128)S(1)} %get-tuple-element.35.normed, f32[2,16,32,128]{3,2,1,0:T(8,128)S(1)} %get-tuple-element.40.pre, f32[4,8,128]{2,1,0:T(8,128)S(1)} %all_to_all.21.sums, ...), custom_call_target="tpu_custom_call" | custom-call | flops 301989888 | bytes 3948544 | tf_op jit(solution)/shard_map/pallas_call | solution.py:43
  25.2 11.1 %all_to_all.22.arrived = bf16[16,104,128]{2,1,0:T(8,128)(2,1)S(1)} all-to-all(bf16[16,104,128]{2,1,0:T(8,128)(2,1)S(1)} %shard_map.105), channel_id=1, replica_groups={{0,1,2,3,8,9,10,11,16,17,18,19,24,25,26,27},{4,5,6,7,12,13,14,15,20,21,..., dimensions={0} | all-to-all | bytes 851968 | tf_op jit(solution)/shard_map/all_to_all | solution.py:441
  36.3 0.1 shard_map.106.mine
  36.4 2.6 %collective-permute-start.2 = (bf16[104,128]{1,0:T(8,128)(2,1)S(1)}, bf16[104,128]{1,0:T(8,128)(2,1)S(1)}, u32[]{:S(2)}, u32[]{:S(2)}) collective-permute-start(bf16[104,128]{1,0:T(8,128)(2,1)S(1)} %shard_map.106.mine), channel_id=1, source_target_pairs={{0,4},{1,5},{2,6},{3,7},{4,0},{5,1},{6,2},{7,3},{8,12},{9,13},{10,... | collective-permute-start | bytes 79880 | tf_op jit(solution)/shard_map/ppermute | solution.py:525
  39.0 1.1 %shard_map.107 = bf16[2,16,32,128]{3,2,1,0:T(8,128)(2,1)} custom-call(bf16[2,16,32,128]{3,2,1,0:T(8,128)(2,1)S(1)} %get-tuple-element.45.act, bf16[2,16,32,128]{3,2,1,0:T(8,128)(2,1)S(1)} %collective-permute-done.1.halo, bf16[3,128,128]{2,1,0:T(8,128)(2,1)S(1)} %copy-done.1), custom_call_target="tpu_custom_call" | custom-call | flops 100663296 | bytes 884736 | tf_op jit(solution)/shard_map/pallas_call | solution.py:43
  40.1 1.2 %collective-permute-done.2.other = bf16[104,128]{1,0:T(8,128)(2,1)S(1)} collective-permute-done((bf16[104,128]{1,0:T(8,128)(2,1)S(1)}, bf16[104,128]{1,0:T(8,128)(2,1)S(1)}, u32[]{:S(2)}, u32[]{:S(2)}) %collective-permute-start.2) | collective-permute-done | bytes 26656 | tf_op jit(solution)/shard_map/ppermute | solution.py:525
  41.3 10.9 %all_to_all.23 = bf16[16,96,128]{2,1,0:T(8,128)(2,1)S(1)} all-to-all(bf16[16,96,128]{2,1,0:T(8,128)(2,1)S(1)} %get-tuple-element.49), channel_id=1, replica_groups={{0,1,2,3,8,9,10,11,16,17,18,19,24,25,26,27},{4,5,6,7,12,13,14,15,20,21,..., dimensions={0} | all-to-all | bytes 786432 | tf_op jit(solution)/shard_map/all_to_all | solution.py:441
  52.2 0.9 %shard_map.109 = (f32[1152,128]{1,0:T(8,128)}, f32[384,128]{1,0:T(8,128)}, f32[1,128]{1,0:T(1,128)}, f32[1,128]{1,0:T(1,128)}) custom-call(bf16[1536,128]{1,0:T(8,128)(2,1)S(1)} %bitcast.11, f32[8,128]{1,0:T(8,128)S(1)} %get-tuple-element.50.totals), custom_call_target="tpu_custom_call" | custom-call | bytes 1184768 | tf_op jit(solution)/shard_map/pallas_call | solution.py:43
  (2 shorter events, 0.0 us)
Async XLA Ops:
  0.6 15.2 %copy-start.2 = (bf16[1,2,16,32,128]{4,3,2,1,0:T(8,128)(2,1)S(1)}, bf16[1,2,16,32,128]{4,3,2,1,0:T(8,128)(2,1)}, u32[]{:S(2)}) copy-start(bf16[1,2,16,32,128]{4,3,2,1,0:T(8,128)(2,1)} %param.11) | copy-start | bytes 786436
  0.6 15.2 %copy-start.1 = (bf16[3,128,128]{2,1,0:T(8,128)(2,1)S(1)}, bf16[3,128,128]{2,1,0:T(8,128)(2,1)}, u32[]{:S(2)}) copy-start(bf16[3,128,128]{2,1,0:T(8,128)(2,1)} %weights.3) | copy-start | bytes 294916
  0.7 15.2 %collective-permute-start = (bf16[2,16,32,128]{3,2,1,0:T(8,128)(2,1)}, bf16[2,16,32,128]{3,2,1,0:T(8,128)(2,1)S(1)}, u32[]{:S(2)}, u32[]{:S(2)}) collective-permute-start(bf16[2,16,32,128]{3,2,1,0:T(8,128)(2,1)} %bitcast.13), channel_id=1, source_target_pairs={{1,0},{2,1},{3,2},{0,3},{5,4},{6,5},{7,6},{4,7},{9,8},{10,9},{11,1... | collective-permute-start | bytes 786440 | tf_op jit(solution)/shard_map/ppermute | solution.py:454
  4.7 1.2 %copy-start = (bf16[1,2,32,64,128]{4,3,2,1,0:T(8,128)(2,1)S(1)}, bf16[1,2,32,64,128]{4,3,2,1,0:T(8,128)(2,1)}, u32[]{:S(2)}) copy-start(bf16[1,2,32,64,128]{4,3,2,1,0:T(8,128)(2,1)} %param.6) | copy-start | bytes 3145732
  15.2 9.3 %collective-permute-start.1 = (bf16[2,16,32,128]{3,2,1,0:T(8,128)(2,1)S(1)}, bf16[2,16,32,128]{3,2,1,0:T(8,128)(2,1)S(1)}, u32[]{:S(2)}, u32[]{:S(2)}) collective-permute-start(bf16[2,16,32,128]{3,2,1,0:T(8,128)(2,1)S(1)} %get-tuple-element.45.act), channel_id=1, source_target_pairs={{0,1},{1,2},{2,3},{3,0},{4,5},{5,6},{6,7},{7,4},{8,9},{9,10},{10,1... | collective-permute-start | bytes 786440 | tf_op jit(solution)/shard_map/ppermute | solution.py:494
  36.4 4.9 %collective-permute-start.2 = (bf16[104,128]{1,0:T(8,128)(2,1)S(1)}, bf16[104,128]{1,0:T(8,128)(2,1)S(1)}, u32[]{:S(2)}, u32[]{:S(2)}) collective-permute-start(bf16[104,128]{1,0:T(8,128)(2,1)S(1)} %shard_map.106.mine), channel_id=1, source_target_pairs={{0,4},{1,5},{2,6},{3,7},{4,0},{5,1},{6,2},{7,3},{8,12},{9,13},{10,... | collective-permute-start | bytes 79880 | tf_op jit(solution)/shard_map/ppermute | solution.py:525

commit v15 on v13

--- a/solution.py
+++ b/solution.py
@@ -55,17 +55,14 @@
 
 def group_spread(values, lanes):
     channels = values.shape[-1]
-    shift = 1
-    while shift < lanes:
-        values = values + pltpu.roll(values, channels - shift, 1)
-        shift *= 2
-    lane = lax.broadcasted_iota(jnp.int32, values.shape, 1)
-    values = jnp.where(lax.rem(lane, lanes) == 0, values, 0.0)
-    shift = 1
-    while shift < lanes:
-        values = values + pltpu.roll(values, shift, 1)
-        shift *= 2
-    return values
+    place = lax.rem(lax.broadcasted_iota(jnp.int32, values.shape, 1), lanes)
+    total = values
+    for shift in range(1, lanes):
+        ahead = pltpu.roll(values, channels - shift, 1)
+        behind = pltpu.roll(values, shift, 1)
+        total += jnp.where(place < lanes - shift, ahead, 0.0)
+        total += jnp.where(place >= shift, behind, 0.0)
+    return total
 
 
 def open_kernel(gate):
@@ -314,22 +311,18 @@
     group = group_spread(clip, lanes) * inv_std / members
     group_shift, group_gain = group[2:3], group[3:4]
     flat = (out_rows * out_cols, channels)
-    flat_wide = (out_rows * out_cols, 3 * channels)
     rows = grads.shape[1] - EXTRA
-    parts = [None, None, None]
+    backs = []
     for frame in range(frames):
         back = (
             pre[frame].reshape(flat) - group_shift - normed[frame].reshape(flat) * group_gain
         )
-        back = back.astype(jnp.bfloat16).T
-        for tap, source in enumerate(
-            (odd.at[frame, pl.ds(0, out_rows)], even.at[frame], odd.at[frame, pl.ds(1, out_rows)])
-        ):
-            term = dot(back, source[...].reshape(flat_wide))
-            parts[tap] = term if parts[tap] is None else parts[tap] + term
-    for tap in range(3):
+        backs.append(back.astype(jnp.bfloat16).T)
+    backs = jnp.concatenate(backs, axis=1)
+    for tap, source in enumerate((odd[:, 0:out_rows], even[...], odd[:, 1 : out_rows + 1])):
+        part = dot(backs, source.reshape(frames * out_rows * out_cols, 3 * channels))
         for side in range(3):
-            block = parts[tap][:, side * channels : (side + 1) * channels].astype(jnp.bfloat16).T
+            block = part[:, side * channels : (side + 1) * channels].astype(jnp.bfloat16).T
             store_rows(grads, rows, (3 * tap + side) * channels, block)
     for tap in range(3):
         block = temporal[pl.ds(tap * channels, channels)]

time: 52.9 us -> 52.3 us (0.989)
  Pallas kernels: 6.27 us -> 5.66 us
    pallas_call x8, Pallas kernels: 6.27 us -> 5.66 us  [call(): pl.pallas_call(kernel, out_shape=out_shape, in_specs=specs or [WHOLE] * l...]
  transfers between devices with their start and end apart: 3 -> 3, of which waited for: 1 -> 1; matrix products, arithmetic and copies ran while one was open for 0% -> 0% of each run, Pallas kernels for 8% -> 7%
where the time goes in v15:
time: 52.3 us; the launch traced here: 52 us
  blocking collectives  37.1 us (71%)
  starting transfers between devices  7.31 us (14%)
  Pallas kernels  5.66 us (11%)
  waiting for transfers between devices  1.21 us (2%)
  between operations  0.69 us (1%)
    all_to_all x4, blocking collectives, exchange(): lax.all_to_all(value, axes, 0, 0, axis_index_groups=groups, tiled=True)  37.1 us
    pallas_call x8, Pallas kernels, call(): pl.pallas_call(kernel, out_shape=out_shape, in_specs=specs or [WHOLE] * l...  5.66 us
    ppermute x1, starting transfers between devices, on_device(): cot_halo = lax.ppermute(cot_out, 'seq', back_pairs)  4 us
    ppermute x1, starting transfers between devices, on_device(): lax.ppermute(mine, 'seq', [(s, (s + half) % seq_size) for s in range(seq_...  2.65 us
    ppermute x1, waiting for transfers between devices, on_device(): lax.ppermute(mine, 'seq', [(s, (s + half) % seq_size) for s in range(seq_...  1.2 us
  transfers between devices with their start and end apart: 3, of which 1 were waited for; matrix products, arithmetic and copies ran while one was open for 0% of the time, Pallas kernels for 7%

profile of v15, /device:TPU:0, one launch (start us, length us, event | category | flops | bytes accessed | tf_op | source)
XLA Modules:
  0.0 52.0 jit_solution(18356504415080875380)
XLA Ops:
  0.6 0.0 copy-start
  0.7 4.0 %collective-permute-start = (bf16[2,16,32,128]{3,2,1,0:T(8,128)(2,1)}, bf16[2,16,32,128]{3,2,1,0:T(8,128)(2,1)S(1)}, u32[]{:S(2)}, u32[]{:S(2)}) collective-permute-start(bf16[2,16,32,128]{3,2,1,0:T(8,128)(2,1)} %bitcast.13), channel_id=1, source_target_pairs={{1,0},{2,1},{3,2},{0,3},{5,4},{6,5},{7,6},{4,7},{9,8},{10,9},{11,1... | collective-permute-start | bytes 786440 | tf_op jit(solution)/shard_map/ppermute | solution.py:431
  4.7 0.0 copy-done
  4.7 1.8 %shard_map.102 = (f32[2,16,32,128]{3,2,1,0:T(8,128)S(1)}, f32[4,8,128]{2,1,0:T(8,128)S(1)}, bf16[2,17,32,384]{3,2,1,0:T(8,128)(2,1)S(1)}, bf16[2,16,32,384]{3,2,1,0:T(8,128)(2,1)S(1)}, f32[8,128]{1,0:T(8,128)S(1)}) custom-call(f32[8,128]{1,0:T(8,128)S(1)} %shard_map.101.blank, bf16[2,32,64,128]{3,2,1,0:T(8,128)(2,1)S(1)} %bitcast.12, ...), custom_call_target="tpu_custom_call" | custom-call | flops 301989888 | bytes 3515392 | tf_op jit(solution)/shard_map/pallas_call | solution.py:43
  6.5 7.1 %all_to_all.20.stats = f32[4,8,128]{2,1,0:T(8,128)S(1)} all-to-all(f32[4,8,128]{2,1,0:T(8,128)S(1)} %get-tuple-element.35), channel_id=1, replica_groups={{0,1,2,3},{4,5,6,7},{8,9,10,11},{12,13,14,15},{16,17,18,19},{20,21,22,2..., dimensions={0} | all-to-all | bytes 32768 | tf_op jit(solution)/shard_map/all_to_all | solution.py:418
  13.5 0.0 copy-start.1
  13.5 0.0 copy-start.2
  13.5 0.4 shard_map.103
  14.0 0.7 %collective-permute-start.1 = (bf16[2,16,32,128]{3,2,1,0:T(8,128)(2,1)S(1)}, bf16[2,16,32,128]{3,2,1,0:T(8,128)(2,1)S(1)}, u32[]{:S(2)}, u32[]{:S(2)}) collective-permute-start(bf16[2,16,32,128]{3,2,1,0:T(8,128)(2,1)S(1)} %get-tuple-element.47.act), channel_id=1, source_target_pairs={{0,1},{1,2},{2,3},{3,0},{4,5},{5,6},{6,7},{7,4},{8,9},{9,10},{10,1... | collective-permute-start | bytes 786440 | tf_op jit(solution)/shard_map/ppermute | solution.py:472
  14.6 0.0 collective-permute-done.arrived
  14.6 0.0 copy-done.1
  14.6 0.0 copy-done.2
  14.6 0.5 %shard_map.104 = (f32[2,16,32,128]{3,2,1,0:T(8,128)S(1)}, bf16[384,128]{1,0:T(8,128)(2,1)S(1)}, f32[4,8,128]{2,1,0:T(8,128)S(1)}) custom-call(bf16[2,16,32,128]{3,2,1,0:T(8,128)(2,1)S(1)} %bitcast.14, bf16[2,16,32,128]{3,2,1,0:T(8,128)(2,1)S(1)} %collective-permute-done.arrived, bf16[3,128,128]{2,1,0:T(8,128)(2,1)S(1)} %copy-done.1, ...), custom_call_target="tpu_custom_call" | custom-call | flops 201326592 | bytes 2576384 | tf_op jit(solution)/shard_map/pallas_call | solution.py:43
  15.2 8.1 %all_to_all.21.sums = f32[4,8,128]{2,1,0:T(8,128)S(1)} all-to-all(f32[4,8,128]{2,1,0:T(8,128)S(1)} %get-tuple-element.43), channel_id=1, replica_groups={{0,1,2,3},{4,5,6,7},{8,9,10,11},{12,13,14,15},{16,17,18,19},{20,21,22,2..., dimensions={0} | all-to-all | bytes 32768 | tf_op jit(solution)/shard_map/all_to_all | solution.py:418
  23.3 0.0 collective-permute-done.1.halo
  23.3 0.8 %shard_map.105 = bf16[16,104,128]{2,1,0:T(8,128)(2,1)S(1)} custom-call(bf16[2,17,32,384]{3,2,1,0:T(8,128)(2,1)S(1)} %get-tuple-element.32.odd, bf16[2,16,32,384]{3,2,1,0:T(8,128)(2,1)S(1)} %get-tuple-element.33.even, f32[2,16,32,128]{3,2,1,0:T(8,128)S(1)} %get-tuple-element.37.normed, f32[2,16,32,128]{3,2,1,0:T(8,128)S(1)} %get-tuple-element.42.pre, ...), custom_call_target="tpu_custom_call" | custom-call | flops 301989888 | bytes 3211264 | tf_op jit(solution)/shard_map/pallas_call | solution.py:43
  24.1 11.0 %all_to_all.22.arrived = bf16[16,104,128]{2,1,0:T(8,128)(2,1)S(1)} all-to-all(bf16[16,104,128]{2,1,0:T(8,128)(2,1)S(1)} %shard_map.105), channel_id=1, replica_groups={{0,1,2,3,8,9,10,11,16,17,18,19,24,25,26,27},{4,5,6,7,12,13,14,15,20,21,..., dimensions={0} | all-to-all | bytes 851968 | tf_op jit(solution)/shard_map/all_to_all | solution.py:418
  35.1 0.1 shard_map.106.mine
  35.2 2.6 %collective-permute-start.2 = (bf16[104,128]{1,0:T(8,128)(2,1)S(1)}, bf16[104,128]{1,0:T(8,128)(2,1)S(1)}, u32[]{:S(2)}, u32[]{:S(2)}) collective-permute-start(bf16[104,128]{1,0:T(8,128)(2,1)S(1)} %shard_map.106.mine), channel_id=1, source_target_pairs={{0,4},{1,5},{2,6},{3,7},{4,0},{5,1},{6,2},{7,3},{8,12},{9,13},{10,... | collective-permute-start | bytes 79880 | tf_op jit(solution)/shard_map/ppermute | solution.py:503
  37.9 1.1 %shard_map.107 = bf16[2,16,32,128]{3,2,1,0:T(8,128)(2,1)} custom-call(bf16[2,16,32,128]{3,2,1,0:T(8,128)(2,1)S(1)} %get-tuple-element.47.act, bf16[2,16,32,128]{3,2,1,0:T(8,128)(2,1)S(1)} %collective-permute-done.1.halo, bf16[3,128,128]{2,1,0:T(8,128)(2,1)S(1)} %copy-done.1), custom_call_target="tpu_custom_call" | custom-call | flops 100663296 | bytes 884736 | tf_op jit(solution)/shard_map/pallas_call | solution.py:43
  38.9 1.2 %collective-permute-done.2.other = bf16[104,128]{1,0:T(8,128)(2,1)S(1)} collective-permute-done((bf16[104,128]{1,0:T(8,128)(2,1)S(1)}, bf16[104,128]{1,0:T(8,128)(2,1)S(1)}, u32[]{:S(2)}, u32[]{:S(2)}) %collective-permute-start.2) | collective-permute-done | bytes 26656 | tf_op jit(solution)/shard_map/ppermute | solution.py:503
  40.2 10.9 %all_to_all.23 = bf16[16,96,128]{2,1,0:T(8,128)(2,1)S(1)} all-to-all(bf16[16,96,128]{2,1,0:T(8,128)(2,1)S(1)} %get-tuple-element.51), channel_id=1, replica_groups={{0,1,2,3,8,9,10,11,16,17,18,19,24,25,26,27},{4,5,6,7,12,13,14,15,20,21,..., dimensions={0} | all-to-all | bytes 786432 | tf_op jit(solution)/shard_map/all_to_all | solution.py:418
  51.1 0.9 %shard_map.109 = (f32[1152,128]{1,0:T(8,128)}, f32[384,128]{1,0:T(8,128)}, f32[1,128]{1,0:T(1,128)}, f32[1,128]{1,0:T(1,128)}) custom-call(bf16[1536,128]{1,0:T(8,128)(2,1)S(1)} %bitcast.11, f32[8,128]{1,0:T(8,128)S(1)} %get-tuple-element.52.totals), custom_call_target="tpu_custom_call" | custom-call | bytes 1184768 | tf_op jit(solution)/shard_map/pallas_call | solution.py:43
  (2 shorter events, 0.0 us)
Async XLA Ops:
  0.6 4.0 %copy-start = (bf16[1,2,32,64,128]{4,3,2,1,0:T(8,128)(2,1)S(1)}, bf16[1,2,32,64,128]{4,3,2,1,0:T(8,128)(2,1)}, u32[]{:S(2)}) copy-start(bf16[1,2,32,64,128]{4,3,2,1,0:T(8,128)(2,1)} %param.6) | copy-start | bytes 3145732
  0.7 14.0 %collective-permute-start = (bf16[2,16,32,128]{3,2,1,0:T(8,128)(2,1)}, bf16[2,16,32,128]{3,2,1,0:T(8,128)(2,1)S(1)}, u32[]{:S(2)}, u32[]{:S(2)}) collective-permute-start(bf16[2,16,32,128]{3,2,1,0:T(8,128)(2,1)} %bitcast.13), channel_id=1, source_target_pairs={{1,0},{2,1},{3,2},{0,3},{5,4},{6,5},{7,6},{4,7},{9,8},{10,9},{11,1... | collective-permute-start | bytes 786440 | tf_op jit(solution)/shard_map/ppermute | solution.py:431
  13.5 1.1 %copy-start.1 = (bf16[3,128,128]{2,1,0:T(8,128)(2,1)S(1)}, bf16[3,128,128]{2,1,0:T(8,128)(2,1)}, u32[]{:S(2)}) copy-start(bf16[3,128,128]{2,1,0:T(8,128)(2,1)} %weights.3) | copy-start | bytes 294916
  13.5 1.1 %copy-start.2 = (bf16[1,2,16,32,128]{4,3,2,1,0:T(8,128)(2,1)S(1)}, bf16[1,2,16,32,128]{4,3,2,1,0:T(8,128)(2,1)}, u32[]{:S(2)}) copy-start(bf16[1,2,16,32,128]{4,3,2,1,0:T(8,128)(2,1)} %param.11) | copy-start | bytes 786436
  14.0 9.3 %collective-permute-start.1 = (bf16[2,16,32,128]{3,2,1,0:T(8,128)(2,1)S(1)}, bf16[2,16,32,128]{3,2,1,0:T(8,128)(2,1)S(1)}, u32[]{:S(2)}, u32[]{:S(2)}) collective-permute-start(bf16[2,16,32,128]{3,2,1,0:T(8,128)(2,1)S(1)} %get-tuple-element.47.act), channel_id=1, source_target_pairs={{0,1},{1,2},{2,3},{3,0},{4,5},{5,6},{6,7},{7,4},{8,9},{9,10},{10,1... | collective-permute-start | bytes 786440 | tf_op jit(solution)/shard_map/ppermute | solution.py:472
  35.2 4.9 %collective-permute-start.2 = (bf16[104,128]{1,0:T(8,128)(2,1)S(1)}, bf16[104,128]{1,0:T(8,128)(2,1)S(1)}, u32[]{:S(2)}, u32[]{:S(2)}) collective-permute-start(bf16[104,128]{1,0:T(8,128)(2,1)S(1)} %shard_map.106.mine), channel_id=1, source_target_pairs={{0,4},{1,5},{2,6},{3,7},{4,0},{5,1},{6,2},{7,3},{8,12},{9,13},{10,... | collective-permute-start | bytes 79880 | tf_op jit(solution)/shard_map/ppermute | solution.py:503

commit v16 on v15

--- a/solution.py
+++ b/solution.py
@@ -112,9 +112,13 @@
 
     def multiply(piece, step):
         frame, first = place(piece, step)
-        total = dot(odd[frame, pl.ds(first, STEP_ROWS)].reshape(flat), weights[0])
-        total += dot(even[frame, pl.ds(first, STEP_ROWS)].reshape(flat), weights[1])
-        total += dot(odd[frame, pl.ds(first + 1, STEP_ROWS)].reshape(flat), weights[2])
+        sources = (
+            odd[frame, pl.ds(first, STEP_ROWS)],
+            even[frame, pl.ds(first, STEP_ROWS)],
+            odd[frame, pl.ds(first + 1, STEP_ROWS)],
+        )
+        side_by_side = jnp.concatenate([source.reshape(flat) for source in sources], axis=1)
+        total = dot(side_by_side, weights[...])
         spatial[frame, pl.ds(first, STEP_ROWS)] = total.reshape(STEP_ROWS, out_cols, channels)
         return total
 
@@ -319,11 +323,23 @@
         )
         backs.append(back.astype(jnp.bfloat16).T)
     backs = jnp.concatenate(backs, axis=1)
-    for tap, source in enumerate((odd[:, 0:out_rows], even[...], odd[:, 1 : out_rows + 1])):
-        part = dot(backs, source.reshape(frames * out_rows * out_cols, 3 * channels))
-        for side in range(3):
-            block = part[:, side * channels : (side + 1) * channels].astype(jnp.bfloat16).T
-            store_rows(grads, rows, (3 * tap + side) * channels, block)
+    def turned(columns, blocks):
+        part = dot(backs, columns)
+        for side, block in enumerate(blocks):
+            value = part[:, side * channels : (side + 1) * channels].astype(jnp.bfloat16).T
+            store_rows(grads, rows, block * channels, value)
+
+    def columns_of(tap, lanes):
+        source = even[:, :, :, lanes] if tap == 1 else None
+        if source is None:
+            source = odd[:, tap // 2 : tap // 2 + out_rows, :, lanes]
+        return source.reshape(frames * out_rows * out_cols, -1)
+
+    for tap in range(3):
+        turned(columns_of(tap, slice(0, 2 * channels)), (3 * tap, 3 * tap + 1))
+    last = slice(2 * channels, 3 * channels)
+    turned(jnp.concatenate([columns_of(0, last), columns_of(1, last)], axis=1), (2, 5))
+    turned(columns_of(2, last), (8,))
     for tap in range(3):
         block = temporal[pl.ds(tap * channels, channels)]
         store_rows(grads, rows, (9 + tap) * channels, block)
@@ -446,14 +462,14 @@
         (
             gate,
             video,
-            far(w_spatial.reshape(3, 3 * channels, channels)),
+            far(w_spatial.reshape(9 * channels, channels)),
             far(norm_gain[None]),
             far(norm_shift[None]),
         ),
         specs=[WHOLE] * 2 + [FAR] * 3,
         scratch=[
             pltpu.VMEM((4 * STEP_ROWS, 8 + width, channels), f32),
-            pltpu.VMEM((3, 3 * channels, channels), bf16),
+            pltpu.VMEM((9 * channels, channels), bf16),
             pltpu.SemaphoreType.DMA((3,)),
         ],
         flops=2 * positions * 9 * channels * channels,

time: 52.3 us -> 52.2 us (level)
  no operation moved by 1% of the time
where the time goes in v16:
time: 52.2 us; the launch traced here: 51.9 us
  blocking collectives  37.1 us (71%)
  starting transfers between devices  7.32 us (14%)
  Pallas kernels  5.57 us (11%)
  waiting for transfers between devices  1.2 us (2%)
  between operations  0.69 us (1%)
    all_to_all x4, blocking collectives, exchange(): lax.all_to_all(value, axes, 0, 0, axis_index_groups=groups, tiled=True)  37.1 us
    pallas_call x8, Pallas kernels, call(): pl.pallas_call(kernel, out_shape=out_shape, in_specs=specs or [WHOLE] * l...  5.57 us
    ppermute x1, starting transfers between devices, on_device(): cot_halo = lax.ppermute(cot_out, 'seq', back_pairs)  4 us
    ppermute x1, starting transfers between devices, on_device(): lax.ppermute(mine, 'seq', [(s, (s + half) % seq_size) for s in range(seq_...  2.65 us
    ppermute x1, waiting for transfers between devices, on_device(): lax.ppermute(mine, 'seq', [(s, (s + half) % seq_size) for s in range(seq_...  1.2 us
  transfers between devices with their start and end apart: 3, of which 1 were waited for; matrix products, arithmetic and copies ran while one was open for 0% of the time, Pallas kernels for 7%

profile of v16, /device:TPU:0, one launch (start us, length us, event | category | flops | bytes accessed | tf_op | source)
XLA Modules:
  0.0 51.9 jit_solution(7989928848344211962)
XLA Ops:
  0.6 0.0 copy-start
  0.7 4.0 %collective-permute-start = (bf16[2,16,32,128]{3,2,1,0:T(8,128)(2,1)}, bf16[2,16,32,128]{3,2,1,0:T(8,128)(2,1)S(1)}, u32[]{:S(2)}, u32[]{:S(2)}) collective-permute-start(bf16[2,16,32,128]{3,2,1,0:T(8,128)(2,1)} %bitcast.13), channel_id=1, source_target_pairs={{1,0},{2,1},{3,2},{0,3},{5,4},{6,5},{7,6},{4,7},{9,8},{10,9},{11,1... | collective-permute-start | bytes 786440 | tf_op jit(solution)/shard_map/ppermute | solution.py:447
  4.7 0.0 copy-done
  4.7 1.8 %shard_map.102 = (f32[2,16,32,128]{3,2,1,0:T(8,128)S(1)}, f32[4,8,128]{2,1,0:T(8,128)S(1)}, bf16[2,17,32,384]{3,2,1,0:T(8,128)(2,1)S(1)}, bf16[2,16,32,384]{3,2,1,0:T(8,128)(2,1)S(1)}, f32[8,128]{1,0:T(8,128)S(1)}) custom-call(f32[8,128]{1,0:T(8,128)S(1)} %shard_map.101.blank, bf16[2,32,64,128]{3,2,1,0:T(8,128)(2,1)S(1)} %bitcast.12, ...), custom_call_target="tpu_custom_call" | custom-call | flops 301989888 | bytes 3515392 | tf_op jit(solution)/shard_map/pallas_call | solution.py:43
  6.5 7.1 %all_to_all.20.stats = f32[4,8,128]{2,1,0:T(8,128)S(1)} all-to-all(f32[4,8,128]{2,1,0:T(8,128)S(1)} %get-tuple-element.35), channel_id=1, replica_groups={{0,1,2,3},{4,5,6,7},{8,9,10,11},{12,13,14,15},{16,17,18,19},{20,21,22,2..., dimensions={0} | all-to-all | bytes 32768 | tf_op jit(solution)/shard_map/all_to_all | solution.py:434
  13.5 0.0 copy-start.1
  13.5 0.0 copy-start.2
  13.5 0.4 shard_map.103
  14.0 0.7 %collective-permute-start.1 = (bf16[2,16,32,128]{3,2,1,0:T(8,128)(2,1)S(1)}, bf16[2,16,32,128]{3,2,1,0:T(8,128)(2,1)S(1)}, u32[]{:S(2)}, u32[]{:S(2)}) collective-permute-start(bf16[2,16,32,128]{3,2,1,0:T(8,128)(2,1)S(1)} %get-tuple-element.47.act), channel_id=1, source_target_pairs={{0,1},{1,2},{2,3},{3,0},{4,5},{5,6},{6,7},{7,4},{8,9},{9,10},{10,1... | collective-permute-start | bytes 786440 | tf_op jit(solution)/shard_map/ppermute | solution.py:488
  14.6 0.0 collective-permute-done.arrived
  14.6 0.0 copy-done.1
  14.6 0.0 copy-done.2
  14.6 0.5 %shard_map.104 = (f32[2,16,32,128]{3,2,1,0:T(8,128)S(1)}, bf16[384,128]{1,0:T(8,128)(2,1)S(1)}, f32[4,8,128]{2,1,0:T(8,128)S(1)}) custom-call(bf16[2,16,32,128]{3,2,1,0:T(8,128)(2,1)S(1)} %bitcast.14, bf16[2,16,32,128]{3,2,1,0:T(8,128)(2,1)S(1)} %collective-permute-done.arrived, bf16[3,128,128]{2,1,0:T(8,128)(2,1)S(1)} %copy-done.1, ...), custom_call_target="tpu_custom_call" | custom-call | flops 201326592 | bytes 2576384 | tf_op jit(solution)/shard_map/pallas_call | solution.py:43
  15.2 8.1 %all_to_all.21.sums = f32[4,8,128]{2,1,0:T(8,128)S(1)} all-to-all(f32[4,8,128]{2,1,0:T(8,128)S(1)} %get-tuple-element.43), channel_id=1, replica_groups={{0,1,2,3},{4,5,6,7},{8,9,10,11},{12,13,14,15},{16,17,18,19},{20,21,22,2..., dimensions={0} | all-to-all | bytes 32768 | tf_op jit(solution)/shard_map/all_to_all | solution.py:434
  23.3 0.0 collective-permute-done.1.halo
  23.3 0.7 %shard_map.105 = bf16[16,104,128]{2,1,0:T(8,128)(2,1)S(1)} custom-call(bf16[2,17,32,384]{3,2,1,0:T(8,128)(2,1)S(1)} %get-tuple-element.32.odd, bf16[2,16,32,384]{3,2,1,0:T(8,128)(2,1)S(1)} %get-tuple-element.33.even, f32[2,16,32,128]{3,2,1,0:T(8,128)S(1)} %get-tuple-element.37.normed, f32[2,16,32,128]{3,2,1,0:T(8,128)S(1)} %get-tuple-element.42.pre, ...), custom_call_target="tpu_custom_call" | custom-call | flops 301989888 | bytes 3211264 | tf_op jit(solution)/shard_map/pallas_call | solution.py:43
  24.0 11.0 %all_to_all.22.arrived = bf16[16,104,128]{2,1,0:T(8,128)(2,1)S(1)} all-to-all(bf16[16,104,128]{2,1,0:T(8,128)(2,1)S(1)} %shard_map.105), channel_id=1, replica_groups={{0,1,2,3,8,9,10,11,16,17,18,19,24,25,26,27},{4,5,6,7,12,13,14,15,20,21,..., dimensions={0} | all-to-all | bytes 851968 | tf_op jit(solution)/shard_map/all_to_all | solution.py:434
  35.1 0.1 shard_map.106.mine
  35.1 2.7 %collective-permute-start.2 = (bf16[104,128]{1,0:T(8,128)(2,1)S(1)}, bf16[104,128]{1,0:T(8,128)(2,1)S(1)}, u32[]{:S(2)}, u32[]{:S(2)}) collective-permute-start(bf16[104,128]{1,0:T(8,128)(2,1)S(1)} %shard_map.106.mine), channel_id=1, source_target_pairs={{0,4},{1,5},{2,6},{3,7},{4,0},{5,1},{6,2},{7,3},{8,12},{9,13},{10,... | collective-permute-start | bytes 79880 | tf_op jit(solution)/shard_map/ppermute | solution.py:519
  37.8 1.1 %shard_map.107 = bf16[2,16,32,128]{3,2,1,0:T(8,128)(2,1)} custom-call(bf16[2,16,32,128]{3,2,1,0:T(8,128)(2,1)S(1)} %get-tuple-element.47.act, bf16[2,16,32,128]{3,2,1,0:T(8,128)(2,1)S(1)} %collective-permute-done.1.halo, bf16[3,128,128]{2,1,0:T(8,128)(2,1)S(1)} %copy-done.1), custom_call_target="tpu_custom_call" | custom-call | flops 100663296 | bytes 884736 | tf_op jit(solution)/shard_map/pallas_call | solution.py:43
  38.9 1.2 %collective-permute-done.2.other = bf16[104,128]{1,0:T(8,128)(2,1)S(1)} collective-permute-done((bf16[104,128]{1,0:T(8,128)(2,1)S(1)}, bf16[104,128]{1,0:T(8,128)(2,1)S(1)}, u32[]{:S(2)}, u32[]{:S(2)}) %collective-permute-start.2) | collective-permute-done | bytes 26656 | tf_op jit(solution)/shard_map/ppermute | solution.py:519
  40.1 10.9 %all_to_all.23 = bf16[16,96,128]{2,1,0:T(8,128)(2,1)S(1)} all-to-all(bf16[16,96,128]{2,1,0:T(8,128)(2,1)S(1)} %get-tuple-element.51), channel_id=1, replica_groups={{0,1,2,3,8,9,10,11,16,17,18,19,24,25,26,27},{4,5,6,7,12,13,14,15,20,21,..., dimensions={0} | all-to-all | bytes 786432 | tf_op jit(solution)/shard_map/all_to_all | solution.py:434
  51.0 0.9 %shard_map.109 = (f32[1152,128]{1,0:T(8,128)}, f32[384,128]{1,0:T(8,128)}, f32[1,128]{1,0:T(1,128)}, f32[1,128]{1,0:T(1,128)}) custom-call(bf16[1536,128]{1,0:T(8,128)(2,1)S(1)} %bitcast.11, f32[8,128]{1,0:T(8,128)S(1)} %get-tuple-element.52.totals), custom_call_target="tpu_custom_call" | custom-call | bytes 1184768 | tf_op jit(solution)/shard_map/pallas_call | solution.py:43
  (2 shorter events, 0.0 us)
Async XLA Ops:
  0.6 4.0 %copy-start = (bf16[1,2,32,64,128]{4,3,2,1,0:T(8,128)(2,1)S(1)}, bf16[1,2,32,64,128]{4,3,2,1,0:T(8,128)(2,1)}, u32[]{:S(2)}) copy-start(bf16[1,2,32,64,128]{4,3,2,1,0:T(8,128)(2,1)} %param.6) | copy-start | bytes 3145732
  0.7 14.0 %collective-permute-start = (bf16[2,16,32,128]{3,2,1,0:T(8,128)(2,1)}, bf16[2,16,32,128]{3,2,1,0:T(8,128)(2,1)S(1)}, u32[]{:S(2)}, u32[]{:S(2)}) collective-permute-start(bf16[2,16,32,128]{3,2,1,0:T(8,128)(2,1)} %bitcast.13), channel_id=1, source_target_pairs={{1,0},{2,1},{3,2},{0,3},{5,4},{6,5},{7,6},{4,7},{9,8},{10,9},{11,1... | collective-permute-start | bytes 786440 | tf_op jit(solution)/shard_map/ppermute | solution.py:447
  13.5 1.1 %copy-start.1 = (bf16[3,128,128]{2,1,0:T(8,128)(2,1)S(1)}, bf16[3,128,128]{2,1,0:T(8,128)(2,1)}, u32[]{:S(2)}) copy-start(bf16[3,128,128]{2,1,0:T(8,128)(2,1)} %weights.3) | copy-start | bytes 294916
  13.5 1.1 %copy-start.2 = (bf16[1,2,16,32,128]{4,3,2,1,0:T(8,128)(2,1)S(1)}, bf16[1,2,16,32,128]{4,3,2,1,0:T(8,128)(2,1)}, u32[]{:S(2)}) copy-start(bf16[1,2,16,32,128]{4,3,2,1,0:T(8,128)(2,1)} %param.11) | copy-start | bytes 786436
  14.0 9.3 %collective-permute-start.1 = (bf16[2,16,32,128]{3,2,1,0:T(8,128)(2,1)S(1)}, bf16[2,16,32,128]{3,2,1,0:T(8,128)(2,1)S(1)}, u32[]{:S(2)}, u32[]{:S(2)}) collective-permute-start(bf16[2,16,32,128]{3,2,1,0:T(8,128)(2,1)S(1)} %get-tuple-element.47.act), channel_id=1, source_target_pairs={{0,1},{1,2},{2,3},{3,0},{4,5},{5,6},{6,7},{7,4},{8,9},{9,10},{10,1... | collective-permute-start | bytes 786440 | tf_op jit(solution)/shard_map/ppermute | solution.py:488
  35.1 4.9 %collective-permute-start.2 = (bf16[104,128]{1,0:T(8,128)(2,1)S(1)}, bf16[104,128]{1,0:T(8,128)(2,1)S(1)}, u32[]{:S(2)}, u32[]{:S(2)}) collective-permute-start(bf16[104,128]{1,0:T(8,128)(2,1)S(1)} %shard_map.106.mine), channel_id=1, source_target_pairs={{0,4},{1,5},{2,6},{3,7},{4,0},{5,1},{6,2},{7,3},{8,12},{9,13},{10,... | collective-permute-start | bytes 79880 | tf_op jit(solution)/shard_map/ppermute | solution.py:519

commit v17 on v16

--- a/solution.py
+++ b/solution.py
@@ -12,6 +12,7 @@
 FRAMES = 8
 STEP_ROWS = 8
 EXTRA = 8
+WEIGHT_PARTS = 6
 SPARE_BYTES = 4 * 1024 * 1024
 
 WHOLE = pl.BlockSpec(memory_space=pltpu.VMEM)
@@ -78,11 +79,15 @@
     positions = frames * out_rows * out_cols
     half = height * frames // pieces
     params[...] = blank[...]
+    part = weights.shape[0] // WEIGHT_PARTS
+    pairs = [
+        (weights_far.at[pl.ds(index * part, part)], weights.at[pl.ds(index * part, part)])
+        for index in range(WEIGHT_PARTS)
+    ]
+    pairs += [(gain_far, params.at[0:1]), (shift_far, params.at[1:2])]
     copies = [
         pltpu.make_async_copy(source, target, arrived.at[index])
-        for index, (source, target) in enumerate(
-            ((weights_far, weights), (gain_far, params.at[0:1]), (shift_far, params.at[1:2]))
-        )
+        for index, (source, target) in enumerate(pairs)
     ]
     for copy in copies:
         copy.start()
@@ -150,7 +155,8 @@
 
     for piece in range(pieces):
         each(steps, functools.partial(separate, piece))
-    copies[0].wait()
+    for copy in copies[:WEIGHT_PARTS]:
+        copy.wait()
     near = over_steps(0, first_sum, zero).sum(axis=0, keepdims=True) * (pieces / positions)
     sums = over_steps(0, first_moments, (zero, zero))
     for piece in range(1, pieces - 1):
@@ -163,7 +169,7 @@
     packed = jnp.where(row == 0, mean, jnp.where(row == 1, square, 0.0))
     for slot in range(stats.shape[0]):
         stats[slot] = packed
-    for copy in copies[1:]:
+    for copy in copies[WEIGHT_PARTS:]:
         copy.wait()
 
 def clip_norm(stats, positions, lanes):
@@ -470,7 +476,7 @@
         scratch=[
             pltpu.VMEM((4 * STEP_ROWS, 8 + width, channels), f32),
             pltpu.VMEM((9 * channels, channels), bf16),
-            pltpu.SemaphoreType.DMA((3,)),
+            pltpu.SemaphoreType.DMA((WEIGHT_PARTS + 2,)),
         ],
         flops=2 * positions * 9 * channels * channels,
     )

time: 52.2 us -> 52.2 us (level)
  no operation moved by 1% of the time
where the time goes in v17:
time: 52.2 us; the launch traced here: 51.9 us
  blocking collectives  37.1 us (71%)
  starting transfers between devices  7.31 us (14%)
  Pallas kernels  5.57 us (11%)
  waiting for transfers between devices  1.21 us (2%)
  between operations  0.69 us (1%)
    all_to_all x4, blocking collectives, exchange(): lax.all_to_all(value, axes, 0, 0, axis_index_groups=groups, tiled=True)  37.1 us
    pallas_call x8, Pallas kernels, call(): pl.pallas_call(kernel, out_shape=out_shape, in_specs=specs or [WHOLE] * l...  5.57 us
    ppermute x1, starting transfers between devices, on_device(): cot_halo = lax.ppermute(cot_out, 'seq', back_pairs)  4 us
    ppermute x1, starting transfers between devices, on_device(): lax.ppermute(mine, 'seq', [(s, (s + half) % seq_size) for s in range(seq_...  2.65 us
    ppermute x1, waiting for transfers between devices, on_device(): lax.ppermute(mine, 'seq', [(s, (s + half) % seq_size) for s in range(seq_...  1.2 us
  transfers between devices with their start and end apart: 3, of which 1 were waited for; matrix products, arithmetic and copies ran while one was open for 0% of the time, Pallas kernels for 7%

profile of v17, /device:TPU:0, one launch (start us, length us, event | category | flops | bytes accessed | tf_op | source)
XLA Modules:
  0.0 51.9 jit_solution(9175507765460302864)
XLA Ops:
  0.6 0.0 copy-start
  0.7 4.0 %collective-permute-start = (bf16[2,16,32,128]{3,2,1,0:T(8,128)(2,1)}, bf16[2,16,32,128]{3,2,1,0:T(8,128)(2,1)S(1)}, u32[]{:S(2)}, u32[]{:S(2)}) collective-permute-start(bf16[2,16,32,128]{3,2,1,0:T(8,128)(2,1)} %bitcast.13), channel_id=1, source_target_pairs={{1,0},{2,1},{3,2},{0,3},{5,4},{6,5},{7,6},{4,7},{9,8},{10,9},{11,1... | collective-permute-start | bytes 786440 | tf_op jit(solution)/shard_map/ppermute | solution.py:453
  4.7 0.0 copy-done
  4.7 1.8 %shard_map.102 = (f32[2,16,32,128]{3,2,1,0:T(8,128)S(1)}, f32[4,8,128]{2,1,0:T(8,128)S(1)}, bf16[2,17,32,384]{3,2,1,0:T(8,128)(2,1)S(1)}, bf16[2,16,32,384]{3,2,1,0:T(8,128)(2,1)S(1)}, f32[8,128]{1,0:T(8,128)S(1)}) custom-call(f32[8,128]{1,0:T(8,128)S(1)} %shard_map.101.blank, bf16[2,32,64,128]{3,2,1,0:T(8,128)(2,1)S(1)} %bitcast.12, ...), custom_call_target="tpu_custom_call" | custom-call | flops 301989888 | bytes 3515392 | tf_op jit(solution)/shard_map/pallas_call | solution.py:44
  6.5 7.1 %all_to_all.20.stats = f32[4,8,128]{2,1,0:T(8,128)S(1)} all-to-all(f32[4,8,128]{2,1,0:T(8,128)S(1)} %get-tuple-element.35), channel_id=1, replica_groups={{0,1,2,3},{4,5,6,7},{8,9,10,11},{12,13,14,15},{16,17,18,19},{20,21,22,2..., dimensions={0} | all-to-all | bytes 32768 | tf_op jit(solution)/shard_map/all_to_all | solution.py:440
  13.5 0.0 copy-start.1
  13.5 0.0 copy-start.2
  13.5 0.4 shard_map.103
  14.0 0.7 %collective-permute-start.1 = (bf16[2,16,32,128]{3,2,1,0:T(8,128)(2,1)S(1)}, bf16[2,16,32,128]{3,2,1,0:T(8,128)(2,1)S(1)}, u32[]{:S(2)}, u32[]{:S(2)}) collective-permute-start(bf16[2,16,32,128]{3,2,1,0:T(8,128)(2,1)S(1)} %get-tuple-element.47.act), channel_id=1, source_target_pairs={{0,1},{1,2},{2,3},{3,0},{4,5},{5,6},{6,7},{7,4},{8,9},{9,10},{10,1... | collective-permute-start | bytes 786440 | tf_op jit(solution)/shard_map/ppermute | solution.py:494
  14.6 0.0 collective-permute-done.arrived
  14.6 0.0 copy-done.1
  14.6 0.0 copy-done.2
  14.6 0.5 %shard_map.104 = (f32[2,16,32,128]{3,2,1,0:T(8,128)S(1)}, bf16[384,128]{1,0:T(8,128)(2,1)S(1)}, f32[4,8,128]{2,1,0:T(8,128)S(1)}) custom-call(bf16[2,16,32,128]{3,2,1,0:T(8,128)(2,1)S(1)} %bitcast.14, bf16[2,16,32,128]{3,2,1,0:T(8,128)(2,1)S(1)} %collective-permute-done.arrived, bf16[3,128,128]{2,1,0:T(8,128)(2,1)S(1)} %copy-done.1, ...), custom_call_target="tpu_custom_call" | custom-call | flops 201326592 | bytes 2576384 | tf_op jit(solution)/shard_map/pallas_call | solution.py:44
  15.2 8.1 %all_to_all.21.sums = f32[4,8,128]{2,1,0:T(8,128)S(1)} all-to-all(f32[4,8,128]{2,1,0:T(8,128)S(1)} %get-tuple-element.43), channel_id=1, replica_groups={{0,1,2,3},{4,5,6,7},{8,9,10,11},{12,13,14,15},{16,17,18,19},{20,21,22,2..., dimensions={0} | all-to-all | bytes 32768 | tf_op jit(solution)/shard_map/all_to_all | solution.py:440
  23.3 0.0 collective-permute-done.1.halo
  23.3 0.7 %shard_map.105 = bf16[16,104,128]{2,1,0:T(8,128)(2,1)S(1)} custom-call(bf16[2,17,32,384]{3,2,1,0:T(8,128)(2,1)S(1)} %get-tuple-element.32.odd, bf16[2,16,32,384]{3,2,1,0:T(8,128)(2,1)S(1)} %get-tuple-element.33.even, f32[2,16,32,128]{3,2,1,0:T(8,128)S(1)} %get-tuple-element.37.normed, f32[2,16,32,128]{3,2,1,0:T(8,128)S(1)} %get-tuple-element.42.pre, ...), custom_call_target="tpu_custom_call" | custom-call | flops 301989888 | bytes 3211264 | tf_op jit(solution)/shard_map/pallas_call | solution.py:44
  24.0 11.0 %all_to_all.22.arrived = bf16[16,104,128]{2,1,0:T(8,128)(2,1)S(1)} all-to-all(bf16[16,104,128]{2,1,0:T(8,128)(2,1)S(1)} %shard_map.105), channel_id=1, replica_groups={{0,1,2,3,8,9,10,11,16,17,18,19,24,25,26,27},{4,5,6,7,12,13,14,15,20,21,..., dimensions={0} | all-to-all | bytes 851968 | tf_op jit(solution)/shard_map/all_to_all | solution.py:440
  35.1 0.1 shard_map.106.mine
  35.1 2.7 %collective-permute-start.2 = (bf16[104,128]{1,0:T(8,128)(2,1)S(1)}, bf16[104,128]{1,0:T(8,128)(2,1)S(1)}, u32[]{:S(2)}, u32[]{:S(2)}) collective-permute-start(bf16[104,128]{1,0:T(8,128)(2,1)S(1)} %shard_map.106.mine), channel_id=1, source_target_pairs={{0,4},{1,5},{2,6},{3,7},{4,0},{5,1},{6,2},{7,3},{8,12},{9,13},{10,... | collective-permute-start | bytes 79880 | tf_op jit(solution)/shard_map/ppermute | solution.py:525
  37.8 1.1 %shard_map.107 = bf16[2,16,32,128]{3,2,1,0:T(8,128)(2,1)} custom-call(bf16[2,16,32,128]{3,2,1,0:T(8,128)(2,1)S(1)} %get-tuple-element.47.act, bf16[2,16,32,128]{3,2,1,0:T(8,128)(2,1)S(1)} %collective-permute-done.1.halo, bf16[3,128,128]{2,1,0:T(8,128)(2,1)S(1)} %copy-done.1), custom_call_target="tpu_custom_call" | custom-call | flops 100663296 | bytes 884736 | tf_op jit(solution)/shard_map/pallas_call | solution.py:44
  38.8 1.2 %collective-permute-done.2.other = bf16[104,128]{1,0:T(8,128)(2,1)S(1)} collective-permute-done((bf16[104,128]{1,0:T(8,128)(2,1)S(1)}, bf16[104,128]{1,0:T(8,128)(2,1)S(1)}, u32[]{:S(2)}, u32[]{:S(2)}) %collective-permute-start.2) | collective-permute-done | bytes 26656 | tf_op jit(solution)/shard_map/ppermute | solution.py:525
  40.1 10.9 %all_to_all.23 = bf16[16,96,128]{2,1,0:T(8,128)(2,1)S(1)} all-to-all(bf16[16,96,128]{2,1,0:T(8,128)(2,1)S(1)} %get-tuple-element.51), channel_id=1, replica_groups={{0,1,2,3,8,9,10,11,16,17,18,19,24,25,26,27},{4,5,6,7,12,13,14,15,20,21,..., dimensions={0} | all-to-all | bytes 786432 | tf_op jit(solution)/shard_map/all_to_all | solution.py:440
  51.0 0.9 %shard_map.109 = (f32[1152,128]{1,0:T(8,128)}, f32[384,128]{1,0:T(8,128)}, f32[1,128]{1,0:T(1,128)}, f32[1,128]{1,0:T(1,128)}) custom-call(bf16[1536,128]{1,0:T(8,128)(2,1)S(1)} %bitcast.11, f32[8,128]{1,0:T(8,128)S(1)} %get-tuple-element.52.totals), custom_call_target="tpu_custom_call" | custom-call | bytes 1184768 | tf_op jit(solution)/shard_map/pallas_call | solution.py:44
  (2 shorter events, 0.0 us)
Async XLA Ops:
  0.6 4.0 %copy-start = (bf16[1,2,32,64,128]{4,3,2,1,0:T(8,128)(2,1)S(1)}, bf16[1,2,32,64,128]{4,3,2,1,0:T(8,128)(2,1)}, u32[]{:S(2)}) copy-start(bf16[1,2,32,64,128]{4,3,2,1,0:T(8,128)(2,1)} %param.6) | copy-start | bytes 3145732
  0.7 14.0 %collective-permute-start = (bf16[2,16,32,128]{3,2,1,0:T(8,128)(2,1)}, bf16[2,16,32,128]{3,2,1,0:T(8,128)(2,1)S(1)}, u32[]{:S(2)}, u32[]{:S(2)}) collective-permute-start(bf16[2,16,32,128]{3,2,1,0:T(8,128)(2,1)} %bitcast.13), channel_id=1, source_target_pairs={{1,0},{2,1},{3,2},{0,3},{5,4},{6,5},{7,6},{4,7},{9,8},{10,9},{11,1... | collective-permute-start | bytes 786440 | tf_op jit(solution)/shard_map/ppermute | solution.py:453
  13.5 1.1 %copy-start.1 = (bf16[3,128,128]{2,1,0:T(8,128)(2,1)S(1)}, bf16[3,128,128]{2,1,0:T(8,128)(2,1)}, u32[]{:S(2)}) copy-start(bf16[3,128,128]{2,1,0:T(8,128)(2,1)} %weights.3) | copy-start | bytes 294916
  13.5 1.1 %copy-start.2 = (bf16[1,2,16,32,128]{4,3,2,1,0:T(8,128)(2,1)S(1)}, bf16[1,2,16,32,128]{4,3,2,1,0:T(8,128)(2,1)}, u32[]{:S(2)}) copy-start(bf16[1,2,16,32,128]{4,3,2,1,0:T(8,128)(2,1)} %param.11) | copy-start | bytes 786436
  14.0 9.3 %collective-permute-start.1 = (bf16[2,16,32,128]{3,2,1,0:T(8,128)(2,1)S(1)}, bf16[2,16,32,128]{3,2,1,0:T(8,128)(2,1)S(1)}, u32[]{:S(2)}, u32[]{:S(2)}) collective-permute-start(bf16[2,16,32,128]{3,2,1,0:T(8,128)(2,1)S(1)} %get-tuple-element.47.act), channel_id=1, source_target_pairs={{0,1},{1,2},{2,3},{3,0},{4,5},{5,6},{6,7},{7,4},{8,9},{9,10},{10,1... | collective-permute-start | bytes 786440 | tf_op jit(solution)/shard_map/ppermute | solution.py:494
  35.1 4.9 %collective-permute-start.2 = (bf16[104,128]{1,0:T(8,128)(2,1)S(1)}, bf16[104,128]{1,0:T(8,128)(2,1)S(1)}, u32[]{:S(2)}, u32[]{:S(2)}) collective-permute-start(bf16[104,128]{1,0:T(8,128)(2,1)S(1)} %shard_map.106.mine), channel_id=1, source_target_pairs={{0,4},{1,5},{2,6},{3,7},{4,0},{5,1},{6,2},{7,3},{8,12},{9,13},{10,... | collective-permute-start | bytes 79880 | tf_op jit(solution)/shard_map/ppermute | solution.py:525

commit v18 on v16

--- a/solution.py
+++ b/solution.py
@@ -10,7 +10,7 @@
 
 GROUPS = 32
 FRAMES = 8
-STEP_ROWS = 8
+STEP_ROWS = 16
 EXTRA = 8
 SPARE_BYTES = 4 * 1024 * 1024
 
@@ -446,7 +446,7 @@
     cot_out, gate = lax.optimization_barrier((cot, gate))
     cot_halo = lax.ppermute(cot_out, "seq", back_pairs)
 
-    pieces = 2 * frames
+    pieces = frames
     def far(value):
         return pltpu.with_memory_space_constraint(value, pltpu.HBM)
 

time: 52.2 us -> 52.3 us (level)
  transfers between devices with their start and end apart: 3 -> 3, of which waited for: 1 -> 1; matrix products, arithmetic and copies ran while one was open for 0% -> 0% of each run, Pallas kernels for 7% -> 8%
where the time goes in v18:
time: 52.3 us; the launch traced here: 52 us
  blocking collectives  37.1 us (71%)
  starting transfers between devices  7.32 us (14%)
  Pallas kernels  5.67 us (11%)
  waiting for transfers between devices  1.2 us (2%)
  between operations  0.69 us (1%)
    all_to_all x4, blocking collectives, exchange(): lax.all_to_all(value, axes, 0, 0, axis_index_groups=groups, tiled=True)  37.1 us
    pallas_call x8, Pallas kernels, call(): pl.pallas_call(kernel, out_shape=out_shape, in_specs=specs or [WHOLE] * l...  5.67 us
    ppermute x1, starting transfers between devices, on_device(): cot_halo = lax.ppermute(cot_out, 'seq', back_pairs)  4 us
    ppermute x1, starting transfers between devices, on_device(): lax.ppermute(mine, 'seq', [(s, (s + half) % seq_size) for s in range(seq_...  2.65 us
    ppermute x1, waiting for transfers between devices, on_device(): lax.ppermute(mine, 'seq', [(s, (s + half) % seq_size) for s in range(seq_...  1.2 us
  transfers between devices with their start and end apart: 3, of which 1 were waited for; matrix products, arithmetic and copies ran while one was open for 0% of the time, Pallas kernels for 8%

profile of v18, /device:TPU:0, one launch (start us, length us, event | category | flops | bytes accessed | tf_op | source)
XLA Modules:
  0.0 52.0 jit_solution(1273435792907996277)
XLA Ops:
  0.6 0.0 copy-start
  0.7 4.0 %collective-permute-start = (bf16[2,16,32,128]{3,2,1,0:T(8,128)(2,1)}, bf16[2,16,32,128]{3,2,1,0:T(8,128)(2,1)S(1)}, u32[]{:S(2)}, u32[]{:S(2)}) collective-permute-start(bf16[2,16,32,128]{3,2,1,0:T(8,128)(2,1)} %bitcast.13), channel_id=1, source_target_pairs={{1,0},{2,1},{3,2},{0,3},{5,4},{6,5},{7,6},{4,7},{9,8},{10,9},{11,1... | collective-permute-start | bytes 786440 | tf_op jit(solution)/shard_map/ppermute | solution.py:447
  4.7 0.0 copy-done
  4.7 1.8 %shard_map.102 = (f32[2,16,32,128]{3,2,1,0:T(8,128)S(1)}, f32[4,8,128]{2,1,0:T(8,128)S(1)}, bf16[2,17,32,384]{3,2,1,0:T(8,128)(2,1)S(1)}, bf16[2,16,32,384]{3,2,1,0:T(8,128)(2,1)S(1)}, f32[8,128]{1,0:T(8,128)S(1)}) custom-call(f32[8,128]{1,0:T(8,128)S(1)} %shard_map.101.blank, bf16[2,32,64,128]{3,2,1,0:T(8,128)(2,1)S(1)} %bitcast.12, ...), custom_call_target="tpu_custom_call" | custom-call | flops 301989888 | bytes 3515392 | tf_op jit(solution)/shard_map/pallas_call | solution.py:43
  6.5 7.1 %all_to_all.20.stats = f32[4,8,128]{2,1,0:T(8,128)S(1)} all-to-all(f32[4,8,128]{2,1,0:T(8,128)S(1)} %get-tuple-element.35), channel_id=1, replica_groups={{0,1,2,3},{4,5,6,7},{8,9,10,11},{12,13,14,15},{16,17,18,19},{20,21,22,2..., dimensions={0} | all-to-all | bytes 32768 | tf_op jit(solution)/shard_map/all_to_all | solution.py:434
  13.6 0.0 copy-start.1
  13.6 0.0 copy-start.2
  13.6 0.5 shard_map.103
  14.1 0.7 %collective-permute-start.1 = (bf16[2,16,32,128]{3,2,1,0:T(8,128)(2,1)S(1)}, bf16[2,16,32,128]{3,2,1,0:T(8,128)(2,1)S(1)}, u32[]{:S(2)}, u32[]{:S(2)}) collective-permute-start(bf16[2,16,32,128]{3,2,1,0:T(8,128)(2,1)S(1)} %get-tuple-element.47.act), channel_id=1, source_target_pairs={{0,1},{1,2},{2,3},{3,0},{4,5},{5,6},{6,7},{7,4},{8,9},{9,10},{10,1... | collective-permute-start | bytes 786440 | tf_op jit(solution)/shard_map/ppermute | solution.py:488
  14.7 0.0 collective-permute-done.arrived
  14.7 0.0 copy-done.1
  14.7 0.0 copy-done.2
  14.7 0.6 %shard_map.104 = (f32[2,16,32,128]{3,2,1,0:T(8,128)S(1)}, bf16[384,128]{1,0:T(8,128)(2,1)S(1)}, f32[4,8,128]{2,1,0:T(8,128)S(1)}) custom-call(bf16[2,16,32,128]{3,2,1,0:T(8,128)(2,1)S(1)} %bitcast.14, bf16[2,16,32,128]{3,2,1,0:T(8,128)(2,1)S(1)} %collective-permute-done.arrived, bf16[3,128,128]{2,1,0:T(8,128)(2,1)S(1)} %copy-done.1, ...), custom_call_target="tpu_custom_call" | custom-call | flops 201326592 | bytes 2576384 | tf_op jit(solution)/shard_map/pallas_call | solution.py:43
  15.3 8.1 %all_to_all.21.sums = f32[4,8,128]{2,1,0:T(8,128)S(1)} all-to-all(f32[4,8,128]{2,1,0:T(8,128)S(1)} %get-tuple-element.43), channel_id=1, replica_groups={{0,1,2,3},{4,5,6,7},{8,9,10,11},{12,13,14,15},{16,17,18,19},{20,21,22,2..., dimensions={0} | all-to-all | bytes 32768 | tf_op jit(solution)/shard_map/all_to_all | solution.py:434
  23.4 0.0 collective-permute-done.1.halo
  23.4 0.7 %shard_map.105 = bf16[16,104,128]{2,1,0:T(8,128)(2,1)S(1)} custom-call(bf16[2,17,32,384]{3,2,1,0:T(8,128)(2,1)S(1)} %get-tuple-element.32.odd, bf16[2,16,32,384]{3,2,1,0:T(8,128)(2,1)S(1)} %get-tuple-element.33.even, f32[2,16,32,128]{3,2,1,0:T(8,128)S(1)} %get-tuple-element.37.normed, f32[2,16,32,128]{3,2,1,0:T(8,128)S(1)} %get-tuple-element.42.pre, ...), custom_call_target="tpu_custom_call" | custom-call | flops 301989888 | bytes 3211264 | tf_op jit(solution)/shard_map/pallas_call | solution.py:43
  24.1 11.0 %all_to_all.22.arrived = bf16[16,104,128]{2,1,0:T(8,128)(2,1)S(1)} all-to-all(bf16[16,104,128]{2,1,0:T(8,128)(2,1)S(1)} %shard_map.105), channel_id=1, replica_groups={{0,1,2,3,8,9,10,11,16,17,18,19,24,25,26,27},{4,5,6,7,12,13,14,15,20,21,..., dimensions={0} | all-to-all | bytes 851968 | tf_op jit(solution)/shard_map/all_to_all | solution.py:434
  35.2 0.1 shard_map.106.mine
  35.2 2.7 %collective-permute-start.2 = (bf16[104,128]{1,0:T(8,128)(2,1)S(1)}, bf16[104,128]{1,0:T(8,128)(2,1)S(1)}, u32[]{:S(2)}, u32[]{:S(2)}) collective-permute-start(bf16[104,128]{1,0:T(8,128)(2,1)S(1)} %shard_map.106.mine), channel_id=1, source_target_pairs={{0,4},{1,5},{2,6},{3,7},{4,0},{5,1},{6,2},{7,3},{8,12},{9,13},{10,... | collective-permute-start | bytes 79880 | tf_op jit(solution)/shard_map/ppermute | solution.py:519
  37.9 1.1 %shard_map.107 = bf16[2,16,32,128]{3,2,1,0:T(8,128)(2,1)} custom-call(bf16[2,16,32,128]{3,2,1,0:T(8,128)(2,1)S(1)} %get-tuple-element.47.act, bf16[2,16,32,128]{3,2,1,0:T(8,128)(2,1)S(1)} %collective-permute-done.1.halo, bf16[3,128,128]{2,1,0:T(8,128)(2,1)S(1)} %copy-done.1), custom_call_target="tpu_custom_call" | custom-call | flops 100663296 | bytes 884736 | tf_op jit(solution)/shard_map/pallas_call | solution.py:43
  38.9 1.2 %collective-permute-done.2.other = bf16[104,128]{1,0:T(8,128)(2,1)S(1)} collective-permute-done((bf16[104,128]{1,0:T(8,128)(2,1)S(1)}, bf16[104,128]{1,0:T(8,128)(2,1)S(1)}, u32[]{:S(2)}, u32[]{:S(2)}) %collective-permute-start.2) | collective-permute-done | bytes 26656 | tf_op jit(solution)/shard_map/ppermute | solution.py:519
  40.2 10.9 %all_to_all.23 = bf16[16,96,128]{2,1,0:T(8,128)(2,1)S(1)} all-to-all(bf16[16,96,128]{2,1,0:T(8,128)(2,1)S(1)} %get-tuple-element.51), channel_id=1, replica_groups={{0,1,2,3,8,9,10,11,16,17,18,19,24,25,26,27},{4,5,6,7,12,13,14,15,20,21,..., dimensions={0} | all-to-all | bytes 786432 | tf_op jit(solution)/shard_map/all_to_all | solution.py:434
  51.1 0.9 %shard_map.109 = (f32[1152,128]{1,0:T(8,128)}, f32[384,128]{1,0:T(8,128)}, f32[1,128]{1,0:T(1,128)}, f32[1,128]{1,0:T(1,128)}) custom-call(bf16[1536,128]{1,0:T(8,128)(2,1)S(1)} %bitcast.11, f32[8,128]{1,0:T(8,128)S(1)} %get-tuple-element.52.totals), custom_call_target="tpu_custom_call" | custom-call | bytes 1184768 | tf_op jit(solution)/shard_map/pallas_call | solution.py:43
  (2 shorter events, 0.0 us)
Async XLA Ops:
  0.6 4.0 %copy-start = (bf16[1,2,32,64,128]{4,3,2,1,0:T(8,128)(2,1)S(1)}, bf16[1,2,32,64,128]{4,3,2,1,0:T(8,128)(2,1)}, u32[]{:S(2)}) copy-start(bf16[1,2,32,64,128]{4,3,2,1,0:T(8,128)(2,1)} %param.6) | copy-start | bytes 3145732
  0.7 14.1 %collective-permute-start = (bf16[2,16,32,128]{3,2,1,0:T(8,128)(2,1)}, bf16[2,16,32,128]{3,2,1,0:T(8,128)(2,1)S(1)}, u32[]{:S(2)}, u32[]{:S(2)}) collective-permute-start(bf16[2,16,32,128]{3,2,1,0:T(8,128)(2,1)} %bitcast.13), channel_id=1, source_target_pairs={{1,0},{2,1},{3,2},{0,3},{5,4},{6,5},{7,6},{4,7},{9,8},{10,9},{11,1... | collective-permute-start | bytes 786440 | tf_op jit(solution)/shard_map/ppermute | solution.py:447
  13.6 1.2 %copy-start.1 = (bf16[3,128,128]{2,1,0:T(8,128)(2,1)S(1)}, bf16[3,128,128]{2,1,0:T(8,128)(2,1)}, u32[]{:S(2)}) copy-start(bf16[3,128,128]{2,1,0:T(8,128)(2,1)} %weights.3) | copy-start | bytes 294916
  13.6 1.2 %copy-start.2 = (bf16[1,2,16,32,128]{4,3,2,1,0:T(8,128)(2,1)S(1)}, bf16[1,2,16,32,128]{4,3,2,1,0:T(8,128)(2,1)}, u32[]{:S(2)}) copy-start(bf16[1,2,16,32,128]{4,3,2,1,0:T(8,128)(2,1)} %param.11) | copy-start | bytes 786436
  14.1 9.3 %collective-permute-start.1 = (bf16[2,16,32,128]{3,2,1,0:T(8,128)(2,1)S(1)}, bf16[2,16,32,128]{3,2,1,0:T(8,128)(2,1)S(1)}, u32[]{:S(2)}, u32[]{:S(2)}) collective-permute-start(bf16[2,16,32,128]{3,2,1,0:T(8,128)(2,1)S(1)} %get-tuple-element.47.act), channel_id=1, source_target_pairs={{0,1},{1,2},{2,3},{3,0},{4,5},{5,6},{6,7},{7,4},{8,9},{9,10},{10,1... | collective-permute-start | bytes 786440 | tf_op jit(solution)/shard_map/ppermute | solution.py:488
  35.2 4.9 %collective-permute-start.2 = (bf16[104,128]{1,0:T(8,128)(2,1)S(1)}, bf16[104,128]{1,0:T(8,128)(2,1)S(1)}, u32[]{:S(2)}, u32[]{:S(2)}) collective-permute-start(bf16[104,128]{1,0:T(8,128)(2,1)S(1)} %shard_map.106.mine), channel_id=1, source_target_pairs={{0,4},{1,5},{2,6},{3,7},{4,0},{5,1},{6,2},{7,3},{8,12},{9,13},{10,... | collective-permute-start | bytes 79880 | tf_op jit(solution)/shard_map/ppermute | solution.py:519
